TPU v7x, 256 devices: a whole 4x4x8 slice. The times are simulated.
256 devices in a mesh: lon: 32 (over z, y_lo, core), lat: 8 (over x, y_hi).
Axes of the slice: x: 4, y: 4 (y_hi: 2, y_lo: 2; y = y_hi * 2 + y_lo), z: 8, core: 2. Of those that a mesh axis runs over, the one named last changes fastest.
Arguments:
- adjoint: float32 [4, 4, 4320, 1024], P(None, None, 'lon', 'lat'), may hold values from -6 to 6
- land: int32 [4320, 1024], P('lon', 'lat'), may hold values from 0 to 1, as said below
- diffusivity: float32 [2, 4320, 1024], P(None, 'lon', 'lat'), may hold values from 0.01 to 0.2
- cutoff: int32 [128], replicated, may hold values from 270 to 2160
Outputs:
- adjoint_in: float32 [4, 4, 4320, 1024], P(None, None, 'lon', 'lat')
Inputs may be any that keep to these rules, and one draw needn't show every extreme that they name: In each of the first 64 and the last 64 latitude rows the land cells form one run of consecutive longitudes around the circle, of 270 to 1080 cells; the rest of that row is ocean.
All inputs are finite; a program needn't handle non-finite values.
Results may differ from a plain program's by a relative error of at most 0.0009.
Values may be sent and summed in bfloat16 or wider, within the bound.
No kernel may reach another device: no remote copies, remote signals or barrier semaphores. Data moves between devices by JAX's collectives and lax.ppermute only.
A program may use at most 128 MiB of HBM per device.

v0:
```python
import math

import jax
import jax.numpy as jnp
from jax import lax
from jax.sharding import PartitionSpec as P

PROWS = 64


PRESSURE = 0.3
ALPHA_T = 1.0
BETA_S = 0.8


def with_halo(block, sides, width, periodic):
    for axis, dim in sides:
        count = lax.axis_size(axis)
        forward = [(i, i + 1) for i in range(count - 1)]
        if periodic:
            forward.append((count - 1, 0))
        backward = [(target, source) for source, target in forward]
        low = lax.ppermute(
            lax.slice_in_dim(block, block.shape[dim] - width, None, axis=dim), axis, forward
        )
        high = lax.ppermute(lax.slice_in_dim(block, 0, width, axis=dim), axis, backward)
        block = jnp.concatenate([low, block, high], axis=dim)
    return block


def diffuse(padded, mask_pad, kappa_pad):
    extent = padded.shape[-2] - 2
    height = padded.shape[-1] - 2
    centre = padded[..., 1:-1, 1:-1]
    mask_centre = mask_pad[1:-1, 1:-1]
    kappa_centre = kappa_pad[1:-1, 1:-1]
    accumulated = jnp.zeros_like(centre)
    for offset_a, offset_b in ((0, 1), (2, 1), (1, 0), (1, 2)):
        neighbour = padded[..., offset_a : offset_a + extent, offset_b : offset_b + height]
        face_weight = (
            0.5
            * (kappa_centre + kappa_pad[offset_a : offset_a + extent, offset_b : offset_b + height])
            * mask_centre
            * mask_pad[offset_a : offset_a + extent, offset_b : offset_b + height]
        )
        accumulated = accumulated + face_weight * (neighbour - centre)
    return accumulated


def adjoint_step(extended, levels):
    extent = extended.shape[1] - 2
    height = extended.shape[2] - 2
    fields_pad = extended[: 4 * levels].reshape(4, levels, extent + 2, height + 2)
    mask_pad = extended[4 * levels]
    kappa_mom = extended[4 * levels + 1]
    kappa_trc = extended[4 * levels + 2]
    zonal_pad = fields_pad[0]
    merid_pad = fields_pad[1]
    temper_pad = fields_pad[2]
    saline_pad = fields_pad[3]
    zonal_c = zonal_pad[:, 1:-1, 1:-1]
    merid_c = merid_pad[:, 1:-1, 1:-1]
    mask_centre = mask_pad[1:-1, 1:-1]
    mask_east = mask_pad[2:, 1:-1]
    mask_north = mask_pad[1:-1, 2:]
    zonal_west = zonal_pad[:, :-2, 1:-1]
    merid_south = merid_pad[:, 1:-1, :-2]
    adjoint_rho = PRESSURE * (
        mask_east * zonal_c + mask_north * merid_c
    ) - PRESSURE * mask_centre * (zonal_west + merid_south)
    zonal_out = zonal_c + diffuse(zonal_pad, mask_pad, kappa_mom)
    merid_out = merid_c + diffuse(merid_pad, mask_pad, kappa_mom)
    temper_out = (
        temper_pad[:, 1:-1, 1:-1] + diffuse(temper_pad, mask_pad, kappa_trc) - ALPHA_T * adjoint_rho
    )
    saline_out = (
        saline_pad[:, 1:-1, 1:-1] + diffuse(saline_pad, mask_pad, kappa_trc) + BETA_S * adjoint_rho
    )
    return jnp.stack([zonal_out, merid_out, temper_out, saline_out], 0)


def back_product(coefs, table):
    return lax.dot_general(
        coefs, table, (((1,), (1,)), ((), ())), preferred_element_type=jnp.float32
    )


def highpass(row_block, row_cuts):
    count_lon = row_block.shape[1]
    halfway = count_lon // 2
    per_block = halfway // 4
    positions = jnp.arange(count_lon, dtype=jnp.int32)
    result = jnp.zeros((row_block.shape[0], count_lon), jnp.float32)
    cut_float = row_cuts.astype(jnp.float32)[:, None]
    for block_number in range(4):
        wavenumbers = jnp.arange(per_block, dtype=jnp.int32) + block_number * per_block + 1
        phase_index = positions[:, None] * wavenumbers[None, :] % count_lon
        angles = phase_index.astype(jnp.float32) * (2.0 * math.pi / count_lon)
        cosine = jnp.cos(angles).astype(jnp.bfloat16)
        sine_table = jnp.sin(angles).astype(jnp.bfloat16)
        along_cos = jnp.dot(row_block, cosine, preferred_element_type=jnp.float32)
        along_sin = jnp.dot(row_block, sine_table, preferred_element_type=jnp.float32)
        wave_float = wavenumbers.astype(jnp.float32)[None, :]
        damping = jnp.maximum(0.0, 1.0 - (cut_float / wave_float) ** 2)
        weights = jnp.where(wavenumbers == halfway, 1.0 / count_lon, 2.0 / count_lon).astype(
            jnp.float32
        )[None, :]
        coef_cos = (along_cos * damping * weights).astype(jnp.bfloat16)
        coef_sin = (along_sin * damping * weights).astype(jnp.bfloat16)
        result = result + back_product(coef_cos, cosine)
        result = result + back_product(coef_sin, sine_table)
    return result


def local(adjoint, land, diffusivity, cutoff):
    levels = adjoint.shape[1]
    lon_cols = adjoint.shape[2]
    lat_rows = adjoint.shape[3]
    mask_float = land.astype(jnp.float32)
    masked = adjoint * mask_float
    stacked = jnp.concatenate(
        [masked.reshape(4 * levels, lon_cols, lat_rows), mask_float[None], diffusivity], 0
    )
    beside_all = with_halo(stacked, (("lon", 1),), 1, True)
    beside_all = with_halo(beside_all, (("lat", 2),), 1, False)
    middle = adjoint_step(beside_all, levels)
    polar_rows = PROWS
    total_rows = 2 * levels * polar_rows
    lat_index = lax.axis_index("lat")
    lat_count = lax.axis_size("lat")
    lon_index = lax.axis_index("lon")
    northern = lat_index == lat_count - 1
    southern = lat_index == 0
    first_row = jnp.where(northern, lat_rows - polar_rows, 0).astype(jnp.int32)
    band_block = lax.dynamic_slice_in_dim(middle[:2], first_row, polar_rows, 3)
    flat_cols = (
        jnp.transpose(band_block, (2, 0, 1, 3)).reshape(lon_cols, total_rows).astype(jnp.bfloat16)
    )
    band_cuts = lax.dynamic_slice_in_dim(
        cutoff, northern.astype(jnp.int32) * polar_rows, polar_rows, 0
    )
    row_cuts = jnp.tile(band_cuts, 2 * levels)
    circles = lax.all_to_all(flat_cols, "lon", split_axis=1, concat_axis=0, tiled=True)
    owned = circles.shape[1]
    my_cuts = lax.dynamic_slice_in_dim(row_cuts, lon_index * owned, owned, 0)
    filtered = highpass(circles.T, my_cuts)
    removed = lax.all_to_all(
        filtered.T.astype(jnp.bfloat16), "lon", split_axis=0, concat_axis=1, tiled=True
    ).astype(jnp.float32)
    is_polar = jnp.logical_or(northern, southern)
    removed_block = jnp.transpose(removed.reshape(lon_cols, 2, levels, polar_rows), (1, 2, 0, 3))
    correction = jnp.where(is_polar, removed_block, 0.0)
    updated = band_block - correction
    momentum = lax.dynamic_update_slice_in_dim(middle[:2], updated, first_row, 3)
    return jnp.concatenate([momentum, middle[2:]], 0)


def solution(mesh):
    placed = (P(None, None, "lon", "lat"), P("lon", "lat"), P(None, "lon", "lat"), P())
    return jax.shard_map(
        local, mesh=mesh, in_specs=placed, out_specs=P(None, None, "lon", "lat"), check_vma=False
    )
```

profile of v0, /device:TPU:1, one launch (start us, length us, event | category | flops | bytes accessed | tf_op | source)
XLA Modules:
  0.0 774.0 jit_solution(7997534222409227714)
XLA Ops:
  2.1 2.8 copy.27
  4.9 1.8 broadcast_multiply_fusion
  6.9 1.9 fusion.247
  10.4 3.3 collective-permute-start.1
  17.1 37.6 %cosine_convert_fusion.59 = bf16[4320,540]{0,1:T(8,128)(2,1)} fusion(s32[540]{0:T(1024)S(1)} %get-tuple-element.24), kind=kLoop, calls=%fused_computation.28.clone.clone.2 | loop fusion | flops 23328000 | bytes 4667760 | tf_op jit(solution)/shard_map/dot_general | solution.py:83
  54.7 37.9 %sine_convert_fusion.58 = bf16[4320,540]{0,1:T(8,128)(2,1)} fusion(s32[540]{0:T(1024)S(1)} %get-tuple-element.24), kind=kLoop, calls=%fused_computation.27.clone.clone | loop fusion | flops 23328000 | bytes 4667760 | tf_op jit(solution)/shard_map/dot_general | solution.py:83
  93.8 37.6 %cosine_convert_fusion.58 = bf16[4320,540]{0,1:T(8,128)(2,1)} fusion(s32[540]{0:T(1024)S(1)} %get-tuple-element.26), kind=kLoop, calls=%fused_computation.23.clone.clone | loop fusion | flops 23328000 | bytes 4667760 | tf_op jit(solution)/shard_map/dot_general | solution.py:83
  131.4 37.9 %sine_convert_fusion.57 = bf16[4320,540]{0,1:T(8,128)(2,1)} fusion(s32[540]{0:T(1024)S(1)} %get-tuple-element.26), kind=kLoop, calls=%fused_computation.22.clone.clone | loop fusion | flops 23328000 | bytes 4667760 | tf_op jit(solution)/shard_map/dot_general | solution.py:83
  170.5 37.6 %cosine_convert_fusion.57 = bf16[4320,540]{0,1:T(8,128)(2,1)} fusion(s32[540]{0:T(1024)S(1)} %get-tuple-element.28), kind=kLoop, calls=%fused_computation.18.clone.clone | loop fusion | flops 23328000 | bytes 4667760 | tf_op jit(solution)/shard_map/dot_general | solution.py:83
  208.1 38.2 %sine_convert_fusion.56 = bf16[4320,540]{0,1:T(8,128)(2,1)} fusion(s32[540]{0:T(1024)S(1)} %get-tuple-element.28), kind=kLoop, calls=%fused_computation.17.clone.clone.2 | loop fusion | flops 23328000 | bytes 4667760 | tf_op jit(solution)/shard_map/dot_general | solution.py:83
  246.3 37.7 %cosine_convert_fusion.56 = bf16[4320,540]{0,1:T(8,128)(2,1)} fusion(s32[540]{0:T(1024)S(1)} %get-tuple-element.30), kind=kLoop, calls=%fused_computation.13.clone.clone.2 | loop fusion | flops 23328000 | bytes 4667760 | tf_op jit(solution)/shard_map/dot_general | solution.py:83
  284.0 37.9 %sine_convert_fusion.59 = bf16[4320,540]{0,1:T(8,128)(2,1)} fusion(s32[540]{0:T(1024)S(1)} %get-tuple-element.30), kind=kLoop, calls=%fused_computation.12.clone.clone.2 | loop fusion | flops 23328000 | bytes 4667760 | tf_op jit(solution)/shard_map/dot_general | solution.py:83
  328.2 5.5 collective-permute-start.2
  342.2 10.4 %all-to-all-start = ((bf16[135,32,16]{0,2,1:T(8,128)(2,1)}), bf16[135,32,16]{0,2,1:T(8,128)(2,1)}, u32[]{:S(2)}, u32[]{:S(2)}) async-start(bf16[135,32,16]{0,2,1:T(8,128)(2,1)} %bitcast.95), calls=%async_computation | async-start | bytes 524288 | tf_op jit(solution)/shard_map/all_to_all | solution.py:143
  352.6 3.4 fusion.60
  356.0 7.9 %all-to-all-done = bf16[135,32,16]{0,2,1:T(8,128)(2,1)} async-done(((bf16[135,32,16]{0,2,1:T(8,128)(2,1)}), bf16[135,32,16]{0,2,1:T(8,128)(2,1)}, u32[]{:S(2)}, u32[]{:S(2)}) %all-to-all-start) | async-done | bytes 138272 | tf_op jit(solution)/shard_map/all_to_all | solution.py:143
  363.9 1.7 copy.35
  365.6 2.0 all_to_all.24
  367.6 46.9 %fusion.27 = f32[4320,16]{0,1:T(8,128)} fusion(s32[540]{0:T(1024)S(1)} %get-tuple-element.24, bf16[4320,16]{0,1:T(8,128)(2,1)} %all_to_all.24, f32[540]{0:T(1024)S(1)} %copy-done.11, f32[540]{0:T(1024)S(1)} %copy-done.10, f32[16]{0:T(128)S(1)} %copy-done.13, bf16[4320,540]{0,1:T(8,128)(2,1)} %cosine_convert_fusion.59), kind=kOutput, calls=%fused_computation.50 | convolution fusion | flops 172687680 | bytes 5086864 | tf_op jit(solution)/shard_map/dot_general | solution.py:83
  414.5 47.7 %convolution_add_fusion.6 = f32[4320,16]{0,1:T(8,128)} fusion(f32[4320,16]{0,1:T(8,128)} %fusion.27, s32[540]{0:T(1024)S(1)} %get-tuple-element.24, bf16[4320,16]{0,1:T(8,128)(2,1)} %all_to_all.24, f32[540]{0:T(1024)S(1)} %copy-done.11, f32[540]{0:T(1024)S(1)} %copy-done.10, f32[16]{0:T(128)S(1)} %copy-done.13, bf16[4320,540]{0,1:T(8,128)(2,1)} %sine_convert_fusion.58), kind=kOutput, calls=%fused_computation.42 | convolution fusion | flops 172756800 | bytes 5363344 | tf_op jit(solution)/shard_map/dot_general | solution.py:83
  462.2 47.2 %convolution_add_fusion.5 = f32[4320,16]{0,1:T(8,128)} fusion(f32[4320,16]{0,1:T(8,128)} %convolution_add_fusion.6, s32[540]{0:T(1024)S(1)} %get-tuple-element.26, bf16[4320,16]{0,1:T(8,128)(2,1)} %all_to_all.24, f32[540]{0:T(1024)S(1)} %copy-done.9, f32[540]{0:T(1024)S(1)} %copy-done.8, f32[16]{0:T(128)S(1)} %copy-done.13, ...), kind=kOutput, calls=%fused_computation.41 | convolution fusion | flops 172756800 | bytes 5363344 | tf_op jit(solution)/shard_map/dot_general | solution.py:83
  509.4 47.5 %convolution_add_fusion.4 = f32[4320,16]{0,1:T(8,128)} fusion(f32[4320,16]{0,1:T(8,128)} %convolution_add_fusion.5, s32[540]{0:T(1024)S(1)} %get-tuple-element.26, bf16[4320,16]{0,1:T(8,128)(2,1)} %all_to_all.24, f32[540]{0:T(1024)S(1)} %copy-done.9, f32[540]{0:T(1024)S(1)} %copy-done.8, f32[16]{0:T(128)S(1)} %copy-done.13, ...), kind=kOutput, calls=%fused_computation.40 | convolution fusion | flops 172756800 | bytes 5363344 | tf_op jit(solution)/shard_map/dot_general | solution.py:83
  557.0 47.4 %convolution_add_fusion.3 = f32[4320,16]{0,1:T(8,128)} fusion(f32[4320,16]{0,1:T(8,128)} %convolution_add_fusion.4, s32[540]{0:T(1024)S(1)} %get-tuple-element.28, bf16[4320,16]{0,1:T(8,128)(2,1)} %all_to_all.24, f32[540]{0:T(1024)S(1)} %copy-done.7, f32[540]{0:T(1024)S(1)} %copy-done.6, f32[16]{0:T(128)S(1)} %copy-done.13, ...), kind=kOutput, calls=%fused_computation.39 | convolution fusion | flops 172756800 | bytes 5363344 | tf_op jit(solution)/shard_map/dot_general | solution.py:83
  604.4 47.5 %convolution_add_fusion.2 = f32[4320,16]{0,1:T(8,128)} fusion(f32[4320,16]{0,1:T(8,128)} %convolution_add_fusion.3, s32[540]{0:T(1024)S(1)} %get-tuple-element.28, bf16[4320,16]{0,1:T(8,128)(2,1)} %all_to_all.24, f32[540]{0:T(1024)S(1)} %copy-done.7, f32[540]{0:T(1024)S(1)} %copy-done.6, f32[16]{0:T(128)S(1)} %copy-done.13, ...), kind=kOutput, calls=%fused_computation.38 | convolution fusion | flops 172756800 | bytes 5363344 | tf_op jit(solution)/shard_map/dot_general | solution.py:83
  651.8 47.2 %convolution_add_fusion.1 = f32[4320,16]{0,1:T(8,128)} fusion(f32[4320,16]{0,1:T(8,128)} %convolution_add_fusion.2, s32[540]{0:T(1024)S(1)} %get-tuple-element.30, bf16[4320,16]{0,1:T(8,128)(2,1)} %all_to_all.24, f32[540]{0:T(1024)S(1)} %copy-done.5, f32[540]{0:T(1024)S(1)} %get-tuple-element.31, f32[16]{0:T(128)S(1)} %copy-done.13, ...), kind=kOutput, calls=%fused_computation.37 | convolution fusion | flops 172756800 | bytes 5363344 | tf_op jit(solution)/shard_map/dot_general | solution.py:83
  699.0 47.5 %fusion.20 = bf16[4320,16]{0,1:T(8,128)(2,1)} fusion(f32[4320,16]{0,1:T(8,128)} %convolution_add_fusion.1, s32[540]{0:T(1024)S(1)} %get-tuple-element.30, bf16[4320,16]{0,1:T(8,128)(2,1)} %all_to_all.24, f32[540]{0:T(1024)S(1)} %copy-done.5, f32[540]{0:T(1024)S(1)} %get-tuple-element.31, f32[16]{0:T(128)S(1)} %copy-done.13, ...), kind=kOutput, calls=%fused_computation.43 | convolution fusion | flops 172825920 | bytes 5225104 | tf_op jit(solution)/shard_map/dot_general | solution.py:83
  746.5 2.4 all_to_all.25
  748.9 1.8 copy.36
  750.7 5.2 all-to-all-start.1
  755.9 3.3 fusion.73
  759.2 8.2 %all-to-all-done.1 = bf16[32,135,16]{1,2,0:T(8,128)(2,1)} async-done(((bf16[32,135,16]{1,2,0:T(8,128)(2,1)}), bf16[32,135,16]{1,2,0:T(8,128)(2,1)}, u32[]{:S(2)}, u32[]{:S(2)}) %all-to-all-start.1) | async-done | bytes 138272 | tf_op jit(solution)/shard_map/all_to_all | solution.py:147
  768.4 1.9 subtract_dynamic-update-slice_fusion
  (66 shorter events, 28.8 us)
Async XLA Ops:
  1.0 5.8 copy-start.1
  10.4 312.9 %collective-permute-start.1 = (f32[19,1,128]{2,1,0:T(1,128)S(1)}, f32[19,1,128]{2,1,0:T(1,128)S(1)}, u32[]{:S(2)}, u32[]{:S(2)}) collective-permute-start(f32[19,1,128]{2,1,0:T(1,128)S(1)} %copy.30), channel_id=1, source_target_pairs={{8,0},{16,8},{24,16},{32,24},{40,32},{48,40},{56,48},{64,56},{72,6... | collective-permute-start | bytes 29192 | tf_op jit(solution)/shard_map/ppermute | solution.py:26
  15.4 308.3 %collective-permute-start = (f32[19,1,128]{2,1,0:T(1,128)S(1)}, f32[19,1,128]{2,1,0:T(1,128)S(1)}, u32[]{:S(2)}, u32[]{:S(2)}) collective-permute-start(f32[19,1,128]{2,1,0:T(1,128)S(1)} %copy.29), channel_id=1, source_target_pairs={{0,8},{8,16},{16,24},{24,32},{32,40},{40,48},{48,56},{56,64},{64,7... | collective-permute-start | bytes 29192 | tf_op jit(solution)/shard_map/ppermute | solution.py:23
  246.3 76.2 %copy-start.12 = (s32[128]{0:T(128)S(1)}, s32[128]{0:T(128)}, u32[]{:S(2)}) copy-start(s32[128]{0:T(128)} %param.7) | copy-start | bytes 1540
  326.9 8.1 %collective-permute-start.3 = (f32[19,137,1]{1,2,0:T(1,128)}, f32[19,137,1]{1,2,0:T(1,128)S(1)}, u32[]{:S(2)}, u32[]{:S(2)}) collective-permute-start(f32[19,137,1]{1,2,0:T(1,128)} %get-tuple-element.8), channel_id=1, source_target_pairs={{1,0},{2,1},{3,2},{4,3},{5,4},{6,5},{7,6},{9,8},{10,9},{11,10},{12... | collective-permute-start | bytes 31244 | tf_op jit(solution)/shard_map/ppermute | solution.py:26
  328.2 6.8 collective-permute-start.2
  334.9 1.5 copy-start
  334.9 1.5 copy-start.2
  338.4 2.6 copy-start.3
  339.2 3.0 copy-start.4
  342.2 25.4 %copy-start.10 = (f32[540]{0:T(1024)S(1)}, f32[540]{0:T(1024)}, u32[]{:S(2)}) copy-start(f32[540]{0:T(1024)} %get-tuple-element.25) | copy-start | bytes 6484
  342.2 25.4 %copy-start.11 = (f32[540]{0:T(1024)S(1)}, f32[540]{0:T(1024)}, u32[]{:S(2)}) copy-start(f32[540]{0:T(1024)} %compare_select_fusion.3) | copy-start | bytes 6484
  342.2 25.4 %copy-start.13 = (f32[16]{0:T(128)S(1)}, f32[16]{0:T(128)}, u32[]{:S(2)}) copy-start(f32[16]{0:T(128)} %dynamic-slice_convert_fusion) | copy-start | bytes 196
  342.2 21.7 %all-to-all-start = ((bf16[135,32,16]{0,2,1:T(8,128)(2,1)}), bf16[135,32,16]{0,2,1:T(8,128)(2,1)}, u32[]{:S(2)}, u32[]{:S(2)}) async-start(bf16[135,32,16]{0,2,1:T(8,128)(2,1)} %bitcast.95), calls=%async_computation | async-start | bytes 524288 | tf_op jit(solution)/shard_map/all_to_all | solution.py:143
  414.5 47.7 %copy-start.8 = (f32[540]{0:T(1024)S(1)}, f32[540]{0:T(1024)}, u32[]{:S(2)}) copy-start(f32[540]{0:T(1024)} %get-tuple-element.27) | copy-start | bytes 6484
  414.5 47.7 %copy-start.9 = (f32[540]{0:T(1024)S(1)}, f32[540]{0:T(1024)}, u32[]{:S(2)}) copy-start(f32[540]{0:T(1024)} %compare_select_fusion.2) | copy-start | bytes 6484
  509.4 47.5 %copy-start.6 = (f32[540]{0:T(1024)S(1)}, f32[540]{0:T(1024)}, u32[]{:S(2)}) copy-start(f32[540]{0:T(1024)} %get-tuple-element.29) | copy-start | bytes 6484
  509.4 47.5 %copy-start.7 = (f32[540]{0:T(1024)S(1)}, f32[540]{0:T(1024)}, u32[]{:S(2)}) copy-start(f32[540]{0:T(1024)} %compare_select_fusion.1) | copy-start | bytes 6484
  604.4 47.5 %copy-start.5 = (f32[540]{0:T(1024)S(1)}, f32[540]{0:T(1024)}, u32[]{:S(2)}) copy-start(f32[540]{0:T(1024)} %compare_select_fusion) | copy-start | bytes 6484
  750.7 16.7 %all-to-all-start.1 = ((bf16[32,135,16]{1,2,0:T(8,128)(2,1)}), bf16[32,135,16]{1,2,0:T(8,128)(2,1)}, u32[]{:S(2)}, u32[]{:S(2)}) async-start(bf16[32,135,16]{1,2,0:T(8,128)(2,1)} %copy.36), calls=%async_computation.1 | async-start | bytes 524288 | tf_op jit(solution)/shard_map/all_to_all | solution.py:147
where the time goes:
time: 781 us; the launch traced here: 774 us
  matrix products  379 us (49%)
  other arithmetic  330 us (42%)
  starting transfers between devices  26.2 us (3%)
  local copies, waits for them, and re-layouts  22.4 us (3%)
  waiting for transfers between devices  16.1 us (2%)
    dot_general x8, matrix products, back_product(): lax.dot_general(coefs, table, (((1,), (1,)), ((), ())), preferred_element...  379 us
    dot_general x8, other arithmetic, back_product(): lax.dot_general(coefs, table, (((1,), (1,)), ((), ())), preferred_element...  302 us
  transfers between devices with their start and end apart: 6, of which 2 were waited for; matrix products, arithmetic and copies ran while one was open for 41% of the time, Pallas kernels for 0%

commit v1 on v0

v1 whole, which is shorter than its diff:
```python
import math

import jax
import jax.numpy as jnp
import numpy as np
from jax import lax
from jax.experimental import pallas as pl
from jax.experimental.pallas import tpu as pltpu
from jax.sharding import PartitionSpec as P

PROWS = 64
PRESSURE = 0.3
ALPHA_T = 1.0
BETA_S = 0.8

RING = 32
COLS = 135
NLON = RING * COLS
INV = 23
CRT_RING = 3105
CRT_COLS = 1216
WAVES = 68
ROWS = 16
CHUNK = 24

MAIN = [lane + 1 for lane in range(128)]
EXTRA = [0] + list(range(129, 135))

F32 = jnp.float32
BF16 = jnp.bfloat16


def tables():
    order = np.array(MAIN + EXTRA + [0] * 121)
    used = np.array([1.0] * 135 + [0.0] * 121)
    waves = np.arange(WAVES)
    angle = 2.0 * math.pi * ((38 * order[:, None] * waves[None, :]) % COLS) / COLS
    forward = np.zeros((256, 256))
    forward[:, :WAVES] = np.cos(angle) * used[:, None]
    forward[:, 128 : 128 + WAVES] = -np.sin(angle) * used[:, None]
    weight = np.where(waves == 0, 1.0, 2.0) / NLON
    backward = forward.copy().T
    backward[:WAVES] *= NLON * weight[:, None]
    backward[128 : 128 + WAVES] *= NLON * weight[:, None]
    inverse_square = np.ones((RING, 128))
    for place in range(RING):
        kappa = int(format(place, "05b")[::-1], 2)
        ring_wave = 7 * kappa % RING
        k = (CRT_RING * ring_wave + CRT_COLS * waves) % NLON
        k = np.minimum(k, NLON - k)
        inverse_square[place, :WAVES] = np.where(k == 0, 1e6, 1.0 / np.maximum(k, 1) ** 2)
    return (
        jnp.asarray(forward, BF16),
        jnp.asarray(backward, BF16),
        jnp.asarray(inverse_square, F32),
    )


def turn(value, shift):
    size = value.shape[-1]
    shift %= size
    return value if shift == 0 else pltpu.roll(value, shift, value.ndim - 1)


def lanes(shape):
    return lax.broadcasted_iota(jnp.int32, shape, len(shape) - 1)


def sublanes(shape):
    return lax.broadcasted_iota(jnp.int32, shape, len(shape) - 2)


def faces(mask, kappa, mask_near, kappa_near):
    return 0.5 * (kappa + kappa_near) * mask * mask_near


def pack_kernel(north_ref, adjoint_ref, land_ref, kappa_ref, out_ref, field, part):
    north = north_ref[0] != 0
    whole = (COLS, 128)
    low, high = pl.ds(7, COLS), pl.ds(9, COLS)
    centre = pl.ds(8, COLS)
    zero = jnp.zeros((8, 128), F32)
    for ref in (field,):
        ref[0:8] = zero
        ref[136:144] = zero
        ref[144:152] = zero
    lane = lanes(whole)
    mask = land_ref[...].astype(F32)
    kappa = kappa_ref[0]

    field[centre] = kappa
    kappa_west, kappa_east = field[low], field[high]
    field[centre] = mask
    mask_west, mask_east = field[low], field[high]
    west = faces(mask, kappa, mask_west, kappa_west)
    east = faces(mask, kappa, mask_east, kappa_east)
    up = faces(mask, kappa, jnp.where(lane == 127, 0.0, turn(mask, -1)), turn(kappa, -1))
    down = faces(mask, kappa, jnp.where(lane == 0, 0.0, turn(mask, 1)), turn(kappa, 1))
    own = 1.0 - (west + east + up + down)

    group = (8, 128)
    slot = sublanes(group)
    lane8 = lanes(group)
    edge_fixed = jnp.zeros(group, F32)
    for place, row in ((1, kappa[134:135]), (2, mask[134:135]), (4, kappa[0:1]), (5, mask[0:1])):
        edge_fixed = jnp.where(slot == place, row, edge_fixed)
    part[136:144] = zero
    for index in range(8):
        tilde = adjoint_ref[index // 4, index % 4] * mask
        field[centre] = tilde
        partial = (
            own * tilde
            + west * field[low]
            + east * field[high]
            + up * turn(tilde, -1)
            + down * turn(tilde, 1)
        )
        part[0:COLS] = partial
        turned = part[pl.ds(1, 128)].T
        chosen = jnp.where(north, turned[64:128], turned[0:64])
        others = jnp.where(slot == 0, partial[0:1], part[128:136])
        others = jnp.where(slot == 7, 0.0, others)
        edges = jnp.where(slot == 0, tilde[134:135], jnp.where(slot == 3, tilde[0:1], edge_fixed))
        others = jnp.where(north, turn(others, 64), others)
        edges = jnp.where(north, turn(edges, 64), edges)
        for quarter in range(4):
            place = 4 * index + quarter
            out_ref[place, 0:ROWS] = chosen[16 * quarter : 16 * quarter + 16].astype(BF16)
            out_ref[place, ROWS:CHUNK] = jnp.where(
                lane8 < 16, turn(others, -16 * quarter), turn(edges, 16 - 16 * quarter)
            ).astype(BF16)


def pack(north, adjoint, land, diffusivity):
    return pl.pallas_call(
        pack_kernel,
        grid=(1,),
        out_shape=jax.ShapeDtypeStruct((RING, CHUNK, 128), BF16),
        in_specs=[
            pl.BlockSpec(memory_space=pltpu.SMEM),
            pl.BlockSpec((2, 4, COLS, 128), lambda i: (0, 0, 0, 0)),
            pl.BlockSpec((COLS, 128), lambda i: (0, 0)),
            pl.BlockSpec((1, COLS, 128), lambda i: (0, 0, 0)),
        ],
        out_specs=pl.BlockSpec((RING, CHUNK, 128), lambda i: (0, 0, 0)),
        scratch_shapes=[pltpu.VMEM((152, 128), F32), pltpu.VMEM((144, 128), F32)],
        compiler_params=pltpu.CompilerParams(vmem_limit_bytes=24 * 2**20),
        name="pack",
    )(north, adjoint, land, diffusivity)


def times(re, im, angle_index, count, sign):
    eighth = 8 * angle_index // count if 8 * angle_index % count == 0 else None
    half = math.sqrt(0.5)
    if eighth == 0:
        return re, im
    if eighth == 2:
        return (-im, re) if sign > 0 else (im, -re)
    if eighth == 1:
        if sign > 0:
            return half * (re - im), half * (re + im)
        return half * (re + im), half * (im - re)
    if eighth == 3:
        if sign > 0:
            return -half * (re + im), half * (re - im)
        return half * (im - re), -half * (re + im)
    cos = math.cos(2.0 * math.pi * angle_index / count)
    sin = sign * math.sin(2.0 * math.pi * angle_index / count)
    return cos * re - sin * im, sin * re + cos * im


def fourier(values):
    half = RING // 2
    while half:
        for start in range(0, RING, 2 * half):
            for i in range(half):
                a, b = start + i, start + i + half
                (ar, ai), (br, bi) = values[a], values[b]
                values[a] = (ar + br, ai + bi)
                values[b] = times(ar - br, ai - bi, i, 2 * half, -1)
        half //= 2


def fourier_back(values):
    half = 1
    while half < RING:
        for start in range(0, RING, 2 * half):
            for i in range(half):
                a, b = start + i, start + i + half
                ar, ai = values[a]
                br, bi = times(*values[b], i, 2 * half, 1)
                values[a] = (ar + br, ai + bi)
                values[b] = (ar - br, ai - bi)
        half *= 2


def slot_shift(value, sign):
    slot = lanes(value.shape) % 8
    for bit in range(5):
        moved = turn(value, sign * 8 * 2**bit)
        picked = jnp.zeros(value.shape, jnp.bool_)
        for place, column in enumerate(EXTRA):
            if (INV * column % RING) >> bit & 1:
                picked = jnp.logical_or(picked, slot == place)
        value = jnp.where(picked, moved, value)
    return value


def filter_kernel(in_ref, square_ref, forward_ref, backward_ref, inverse_ref, out_ref, held, wave):
    tile = (ROWS, 128)
    spare = in_ref[:, ROWS:CHUNK, :].astype(F32).reshape(256, 128)
    spare = jnp.concatenate([spare[0:128].T[0:32], spare[128:256].T[0:32]], axis=1)
    others, edges = spare[0:16], spare[16:32]
    slot = lanes(others.shape) % 8
    beyond = turn(edges, -11)
    flux = (beyond - edges) * turn(0.5 * (beyond + edges), -1) * turn(beyond * edges, -2)
    others = others + jnp.where(slot == 6, turn(flux, 6), 0.0)
    others = others - jnp.where(slot == 0, turn(flux, 8), 0.0)
    others = slot_shift(others, 1)

    column = lanes(tile) + 1
    rows = [in_ref[INV * t % RING, 0:ROWS, :] for t in range(RING)]
    for bit in range(5):
        picked = (column >> bit) & 1 == 1
        rows = [jnp.where(picked, rows[(t - 2**bit) % RING], rows[t]) for t in range(RING)]
    for t in range(RING):
        place = INV * t % RING
        held[pl.ds(ROWS * t, ROWS), 0:128] = rows[t]
        side = others[:, 128 * (place // 16) : 128 * (place // 16) + 128]
        held[pl.ds(ROWS * t, ROWS), 128:256] = turn(side, -8 * (place % 16)).astype(BF16)

    wave[...] = jnp.dot(held[...], forward_ref[...], preferred_element_type=F32)
    for half in range(2):
        rows_of = [pl.ds(ROWS * t + 8 * half, 8) for t in range(RING)]
        values = [(wave[r, 0:128], wave[r, 128:256]) for r in rows_of]
        fourier(values)
        square = square_ref[8 * half : 8 * half + 8]
        for t in range(RING):
            keep = jnp.maximum(0.0, 1.0 - square * inverse_ref[t : t + 1]) * (1.0 / NLON)
            values[t] = (values[t][0] * keep, values[t][1] * keep)
        fourier_back(values)
        for t in range(RING):
            wave[rows_of[t], 0:128] = values[t][0]
            wave[rows_of[t], 128:256] = values[t][1]
    wave[...] = jnp.dot(wave[...].astype(BF16), backward_ref[...], preferred_element_type=F32)

    rows = [wave[pl.ds(ROWS * t, ROWS), 0:128] for t in range(RING)]
    for bit in range(5):
        picked = (column >> bit) & 1 == 1
        rows = [jnp.where(picked, rows[(t + 2**bit) % RING], rows[t]) for t in range(RING)]
    for d in range(RING):
        out_ref[d, 0:ROWS] = rows[7 * d % RING].astype(BF16)
    sides = [jnp.zeros(tile, F32), jnp.zeros(tile, F32)]
    for t in range(RING):
        place = INV * t % RING
        sides[place // 16] += turn(wave[pl.ds(ROWS * t, ROWS), 128:256], 8 * (place % 16))
    others = slot_shift(jnp.concatenate(sides, axis=1), -1)
    blank = jnp.zeros((112, 128), F32)
    for half in range(2):
        back = jnp.concatenate([others[:, 128 * half : 128 * half + 128], blank], axis=0).T
        out_ref[16 * half : 16 * half + 16, ROWS:CHUNK] = back.reshape(16, 8, 128).astype(BF16)


def filter_rows(chunks, square):
    forward, backward, inverse_square = tables()
    return pl.pallas_call(
        filter_kernel,
        out_shape=jax.ShapeDtypeStruct((RING, CHUNK, 128), BF16),
        in_specs=[pl.BlockSpec(memory_space=pltpu.VMEM)] * 5,
        out_specs=pl.BlockSpec(memory_space=pltpu.VMEM),
        scratch_shapes=[
            pltpu.VMEM((RING * ROWS, 256), BF16),
            pltpu.VMEM((RING * ROWS, 256), F32),
        ],
        compiler_params=pltpu.CompilerParams(vmem_limit_bytes=24 * 2**20),
        name="filter",
    )(chunks, square, forward, backward, inverse_square)


def edge_kernel(adjoint_ref, land_ref, kappa_ref, first_ref, last_ref, side_ref):
    whole = (COLS, 128)
    lane = lanes(whole)
    mask = land_ref[...].astype(F32)
    sides = jnp.zeros(whole, F32)
    first_ref[...] = jnp.zeros((24, 128), F32)
    last_ref[...] = jnp.zeros((24, 128), F32)
    for index in range(19):
        if index < 16:
            value = adjoint_ref[index // 4, index % 4] * mask
        elif index == 16:
            value = mask
        else:
            value = kappa_ref[index - 17]
        first_ref[index : index + 1] = value[0:1]
        last_ref[index : index + 1] = value[134:135]
        sides = jnp.where(lane // 2 == index, turn(value, 2 * index + 1), sides)
    side_ref[...] = sides


def edge(adjoint, land, diffusivity):
    return pl.pallas_call(
        edge_kernel,
        out_shape=(
            jax.ShapeDtypeStruct((24, 128), F32),
            jax.ShapeDtypeStruct((24, 128), F32),
            jax.ShapeDtypeStruct((COLS, 128), F32),
        ),
        in_specs=[pl.BlockSpec(memory_space=pltpu.VMEM)] * 3,
        out_specs=[pl.BlockSpec(memory_space=pltpu.VMEM)] * 3,
        compiler_params=pltpu.CompilerParams(vmem_limit_bytes=24 * 2**20),
        name="edge",
    )(adjoint, land, diffusivity)


def stencil_kernel(
    adjoint_ref, land_ref, kappa_ref, west_ref, east_ref, south_ref, north_ref, out_ref, field
):
    whole = (COLS, 128)
    lane = lanes(whole)
    centre, low, high = pl.ds(8, COLS), pl.ds(7, COLS), pl.ds(9, COLS)
    south_all, north_all = south_ref[...], north_ref[...]
    mask = land_ref[...].astype(F32)

    def around(value, index):
        field[centre] = value
        field[7:8] = west_ref[index : index + 1]
        field[143:144] = east_ref[index : index + 1]
        above = jnp.where(lane == 127, turn(north_all, 126 - 2 * index), turn(value, -1))
        below = jnp.where(lane == 0, turn(south_all, -2 * index), turn(value, 1))
        return field[low], field[high], above, below

    mask_around = around(mask, 16)
    weights = []
    for number in range(2):
        kappa = kappa_ref[number]
        near = around(kappa, 17 + number)
        four = [faces(mask, kappa, m, k) for m, k in zip(mask_around, near)]
        weights.append((1.0 - (four[0] + four[1] + four[2] + four[3]), *four))
    pressure_mask = PRESSURE * mask
    pressure_east, pressure_north = PRESSURE * mask_around[1], PRESSURE * mask_around[2]

    for level in range(4):
        density = None
        for name in range(4):
            own, *four = weights[name // 2]
            tilde = adjoint_ref[name, level] * mask
            near = around(tilde, 4 * name + level)
            total = own * tilde
            for weight, value in zip(four, near):
                total = total + weight * value
            if name == 0:
                density = pressure_east * tilde - pressure_mask * near[0]
            elif name == 1:
                density = density + pressure_north * tilde - pressure_mask * near[3]
            elif name == 2:
                total = total - ALPHA_T * density
            else:
                total = total + BETA_S * density
            out_ref[name, level] = total


def stencil(adjoint, land, diffusivity, west, east, south, north):
    return pl.pallas_call(
        stencil_kernel,
        out_shape=jax.ShapeDtypeStruct(adjoint.shape, F32),
        in_specs=[pl.BlockSpec(memory_space=pltpu.VMEM)] * 7,
        out_specs=pl.BlockSpec(memory_space=pltpu.VMEM),
        scratch_shapes=[pltpu.VMEM((152, 128), F32)],
        compiler_params=pltpu.CompilerParams(vmem_limit_bytes=24 * 2**20),
        name="stencil",
    )(adjoint, land, diffusivity, west, east, south, north)


def remove_kernel(pole_ref, chunks_ref, middle_ref, out_ref, high):
    south, north = pole_ref[0] != 0, pole_ref[1] != 0
    base = jnp.where(north, 64, 0)
    group = (8, 128)
    lane = lanes(group)
    polar = jnp.logical_or(south, north)
    for level in range(4):
        first = (pl.program_id(0) * 4 + level) * 4
        rows = chunks_ref[pl.ds(first, 4), 0:ROWS, :].astype(F32).reshape(64, 128)
        both = jnp.concatenate(
            [jnp.where(south, rows, 0.0), jnp.where(north, rows, 0.0)], axis=0
        )
        others = jnp.zeros(group, F32)
        for quarter in range(4):
            block = chunks_ref[first + quarter, ROWS:CHUNK, :].astype(F32)
            others = jnp.where(lane // 16 == quarter, turn(block, 16 * quarter), others)
        others = jnp.where(lane < 64, others, turn(others, 64))
        others = jnp.where(jnp.logical_and(lane // 64 == base // 64, polar), others, 0.0)
        high[1:129] = both.T
        high[0:1] = others[0:1]
        high[129:135] = others[1:7]
        out_ref[0, level] = middle_ref[0, level] - high[0:COLS]


def remove(pole, chunks, middle):
    return pl.pallas_call(
        remove_kernel,
        grid=(2,),
        out_shape=jax.ShapeDtypeStruct(middle.shape, F32),
        in_specs=[
            pl.BlockSpec(memory_space=pltpu.SMEM),
            pl.BlockSpec((RING, CHUNK, 128), lambda i: (0, 0, 0)),
            pl.BlockSpec((1, 4, COLS, 128), lambda i: (i, 0, 0, 0)),
        ],
        out_specs=pl.BlockSpec((1, 4, COLS, 128), lambda i: (i, 0, 0, 0)),
        scratch_shapes=[pltpu.VMEM((136, 128), F32)],
        input_output_aliases={2: 0},
        compiler_params=pltpu.CompilerParams(vmem_limit_bytes=24 * 2**20),
        name="remove",
    )(pole, chunks, middle)


def shift(value, axis, step, periodic):
    count = lax.axis_size(axis)
    pairs = [(i, (i + step) % count) for i in range(count) if periodic or 0 <= i + step < count]
    return lax.ppermute(value, axis, pairs)


def exchange(chunks):
    return lax.all_to_all(chunks, "lon", split_axis=0, concat_axis=0, tiled=True)


def local(adjoint, land, diffusivity, cutoff):
    lat_index = lax.axis_index("lat")
    northern = (lat_index == lax.axis_size("lat") - 1).astype(jnp.int32)
    southern = (lat_index == 0).astype(jnp.int32)
    quarter = lax.axis_index("lon") % 4
    cuts = lax.dynamic_slice_in_dim(cutoff, northern * PROWS + quarter * ROWS, ROWS, 0)
    square = jnp.broadcast_to(jnp.square(cuts.astype(F32))[:, None], (ROWS, 128))

    chunks = pack(northern[None], adjoint, land, diffusivity)
    circles = exchange(chunks)

    first, last, sides = edge(adjoint, land, diffusivity)
    west = shift(last, "lon", 1, True)
    east = shift(first, "lon", -1, True)
    south = shift(sides, "lat", 1, False)
    north = shift(sides, "lat", -1, False)
    middle = stencil(adjoint, land, diffusivity, west, east, south, north)

    removed = exchange(filter_rows(circles, square))
    return remove(jnp.stack([southern, northern]), removed, middle)


def solution(mesh):
    placed = (P(None, None, "lon", "lat"), P("lon", "lat"), P(None, "lon", "lat"), P())
    return jax.shard_map(
        local, mesh=mesh, in_specs=placed, out_specs=P(None, None, "lon", "lat"), check_vma=False
    )
```

time: 781 us -> 51.4 us (0.07)
  the two profiles are of different devices: /device:TPU:1 before, /device:TPU:107 now
where the time goes in v1:
time: 51.4 us; the launch traced here: 51.1 us
  starting transfers between devices  26.8 us (52%)
  waiting for transfers between devices  12.9 us (25%)
  Pallas kernels  8.32 us (16%)
  local copies, waits for them, and re-layouts  2.75 us (5%)
    all_to_all x2, starting transfers between devices, exchange(): lax.all_to_all(chunks, 'lon', split_axis=0, concat_axis=0, tiled=True)  15.9 us
    ppermute x4, starting transfers between devices, shift(): return lax.ppermute(value, axis, pairs)  11 us
    all_to_all x2, waiting for transfers between devices, exchange(): lax.all_to_all(chunks, 'lon', split_axis=0, concat_axis=0, tiled=True)  7.72 us
    ppermute x4, waiting for transfers between devices, shift(): return lax.ppermute(value, axis, pairs)  5.16 us
    pallas_call x1, Pallas kernels, filter_rows(): pl.pallas_call(filter_kernel, out_shape=jax.ShapeDtypeStruct((RING, CHUNK...  2.57 us
    pallas_call x1, Pallas kernels, pack(): pl.pallas_call(pack_kernel, grid=(1,), out_shape=jax.ShapeDtypeStruct((RI...  2.43 us
    pallas_call x1, Pallas kernels, stencil(): pl.pallas_call(stencil_kernel, out_shape=jax.ShapeDtypeStruct(adjoint.sha...  1.83 us
    unnamed x14, local copies, waits for them, and re-layouts  1.41 us
  transfers between devices with their start and end apart: 6, of which 3 were waited for; matrix products, arithmetic and copies ran while one was open for 0% of the time, Pallas kernels for 4%

profile of v1, /device:TPU:107, one launch (start us, length us, event | category | flops | bytes accessed | tf_op | source)
XLA Modules:
  0.0 51.1 jit_solution(8026859179248850980)
XLA Ops:
  0.0 1.4 %copy.9.adjoint_ref = f32[4,4,135,128]{3,2,1,0:T(8,128)S(1)} copy(f32[4,4,135,128]{3,1,2,0:T(4,128)} %param.7) | data formatting | bytes 2211840 | tf_op args[0]
  1.4 0.0 copy-done.4
  1.4 0.0 copy-start.5
  1.4 0.0 copy-start.1
  1.4 0.0 copy-start.2
  1.4 0.0 copy-start.3
  1.4 0.0 copy-done
  1.5 2.4 %pack.1 = bf16[32,24,128]{2,1,0:T(8,128)(2,1)} custom-call(s32[1]{0:T(128)} %bitcast.1.north_ref, f32[4,4,135,128]{3,2,1,0:T(8,128)S(1)} %copy.9.adjoint_ref, s32[135,128]{1,0:T(8,128)S(1)} %copy-done, f32[2,135,128]{2,1,0:T(8,128)S(1)} %copy.10.kappa_ref), custom_call_target="tpu_custom_call" | custom-call | tf_op jit(solution)/shard_map/pack/pallas_call | solution.py:135
  3.9 9.0 %all-to-all-start = ((bf16[32,24,128]{2,1,0:T(8,128)(2,1)}), bf16[32,24,128]{2,1,0:T(8,128)(2,1)S(1)}, u32[]{:S(2)}, u32[]{:S(2)}) async-start(bf16[32,24,128]{2,1,0:T(8,128)(2,1)} %pack.1), calls=%async_computation | async-start | bytes 393216 | tf_op jit(solution)/shard_map/all_to_all | solution.py:423
  13.0 0.0 copy-done.5
  13.0 0.1 convert_multiply_fusion
  13.0 7.7 %all-to-all-done.in_ref = bf16[32,24,128]{2,1,0:T(8,128)(2,1)S(1)} async-done(((bf16[32,24,128]{2,1,0:T(8,128)(2,1)}), bf16[32,24,128]{2,1,0:T(8,128)(2,1)S(1)}, u32[]{:S(2)}, u32[]{:S(2)}) %all-to-all-start) | async-done | bytes 196640 | tf_op jit(solution)/shard_map/all_to_all | solution.py:423
  20.8 0.1 broadcast_in_dim.2.square_ref
  20.8 0.0 copy-done.1
  20.8 0.0 copy-done.2
  20.8 0.0 copy-done.3
  20.8 2.6 %filter.1 = bf16[32,24,128]{2,1,0:T(8,128)(2,1)} custom-call(bf16[32,24,128]{2,1,0:T(8,128)(2,1)S(1)} %all-to-all-done.in_ref, f32[16,128]{1,0:T(8,128)S(1)} %broadcast_in_dim.2.square_ref, bf16[256,256]{1,0:T(8,128)(2,1)S(1)} %copy-done.1, bf16[256,256]{1,0:T(8,128)(2,1)S(1)} %copy-done.2, f32[32,128]{1,0:T(8,128)S(1)} %copy-done.3), custom_call_target="tpu_custom_call" | custom-call | tf_op jit(solution)/shard_map/filter/pallas_call | solution.py:266
  23.4 6.8 %all-to-all-start.1 = ((bf16[32,24,128]{2,1,0:T(8,128)(2,1)}), bf16[32,24,128]{2,1,0:T(8,128)(2,1)S(1)}, u32[]{:S(2)}, u32[]{:S(2)}) async-start(bf16[32,24,128]{2,1,0:T(8,128)(2,1)} %filter.1), calls=%async_computation.1 | async-start | bytes 393216 | tf_op jit(solution)/shard_map/all_to_all | solution.py:423
  30.2 0.4 edge.1
  30.7 3.9 %collective-permute-start.2 = (f32[135,128]{1,0:T(8,128)S(1)}, f32[135,128]{1,0:T(8,128)S(1)}, u32[]{:S(2)}, u32[]{:S(2)}) collective-permute-start(f32[135,128]{1,0:T(8,128)S(1)} %get-tuple-element.10), channel_id=1, source_target_pairs={{0,1},{1,2},{2,3},{3,4},{4,5},{5,6},{6,7},{8,9},{9,10},{10,11},{11... | collective-permute-start | bytes 207368 | tf_op jit(solution)/shard_map/ppermute | solution.py:419
  34.6 3.8 %collective-permute-start.3 = (f32[135,128]{1,0:T(8,128)S(1)}, f32[135,128]{1,0:T(8,128)S(1)}, u32[]{:S(2)}, u32[]{:S(2)}) collective-permute-start(f32[135,128]{1,0:T(8,128)S(1)} %get-tuple-element.10), channel_id=1, source_target_pairs={{1,0},{2,1},{3,2},{4,3},{5,4},{6,5},{7,6},{9,8},{10,9},{11,10},{12... | collective-permute-start | bytes 207368 | tf_op jit(solution)/shard_map/ppermute | solution.py:419
  38.4 3.3 %collective-permute-start = (f32[24,128]{1,0:T(8,128)S(1)}, f32[24,128]{1,0:T(8,128)S(1)}, u32[]{:S(2)}, u32[]{:S(2)}) collective-permute-start(f32[24,128]{1,0:T(8,128)S(1)} %get-tuple-element.8), channel_id=1, source_target_pairs={{0,8},{8,16},{16,24},{24,32},{32,40},{40,48},{48,56},{56,64},{64,7... | collective-permute-start | bytes 36872 | tf_op jit(solution)/shard_map/ppermute | solution.py:419
  41.7 0.0 collective-permute-start.1
  41.7 0.1 pad_add_fusion.pole_ref
  41.7 0.8 %collective-permute-done.west_ref = f32[24,128]{1,0:T(8,128)S(1)} collective-permute-done((f32[24,128]{1,0:T(8,128)S(1)}, f32[24,128]{1,0:T(8,128)S(1)}, u32[]{:S(2)}, u32[]{:S(2)}) %collective-permute-start) | collective-permute-done | bytes 12320 | tf_op jit(solution)/shard_map/ppermute | solution.py:419
  42.5 4.4 %collective-permute-done.1.east_ref = f32[24,128]{1,0:T(8,128)S(1)} collective-permute-done((f32[24,128]{1,0:T(8,128)S(1)}, f32[24,128]{1,0:T(8,128)S(1)}, u32[]{:S(2)}, u32[]{:S(2)}) %collective-permute-start.1) | collective-permute-done | bytes 12320 | tf_op jit(solution)/shard_map/ppermute | solution.py:419
  46.9 0.0 collective-permute-done.2.south_ref
  46.9 0.0 collective-permute-done.3.north_ref
  46.9 1.8 %stencil.1.middle_ref = f32[4,4,135,128]{3,2,1,0:T(8,128)S(1)} custom-call(f32[4,4,135,128]{3,2,1,0:T(8,128)S(1)} %copy.9.adjoint_ref, s32[135,128]{1,0:T(8,128)S(1)} %copy-done, f32[2,135,128]{2,1,0:T(8,128)S(1)} %copy.10.kappa_ref, f32[24,128]{1,0:T(8,128)S(1)} %collective-permute-done.west_ref, f32[24,128]{1,0:T(8,128)S(1)} %collective-permute-done.1.east_ref, ...), custom_call_target="tpu_custom_call" | custom-call | tf_op jit(solution)/shard_map/stencil/pallas_call | solution.py:363
  48.7 0.0 all-to-all-done.1.chunks_ref
  48.7 1.1 %remove.1 = f32[4,4,135,128]{3,2,1,0:T(8,128)S(1)} custom-call(s32[2]{0:T(128)S(1)} %pad_add_fusion.pole_ref, bf16[32,24,128]{2,1,0:T(8,128)(2,1)S(1)} %all-to-all-done.1.chunks_ref, f32[4,4,135,128]{3,2,1,0:T(8,128)S(1)} %stencil.1.middle_ref), custom_call_target="tpu_custom_call", output_to_operand_aliasing={{}: (2, {})} | custom-call | tf_op jit(solution)/shard_map/remove/pallas_call | solution.py:399
  49.8 1.3 %copy.15 = f32[4,4,135,128]{3,1,2,0:T(4,128)} copy(f32[4,4,135,128]{3,2,1,0:T(8,128)S(1)} %remove.1) | data formatting | bytes 2211840 | tf_op jit(solution)/shard_map/remove/pallas_call | solution.py:399
  (3 shorter events, 0.0 us)
Async XLA Ops:
  0.0 1.4 %copy-start.4 = (f32[2,135,128]{2,0,1:T(2,128)S(1)}, f32[2,135,128]{2,0,1:T(2,128)}, u32[]{:S(2)}) copy-start(f32[2,135,128]{2,0,1:T(2,128)} %param.9) | copy-start | bytes 414724
  0.0 1.4 %copy-start = (s32[135,128]{1,0:T(8,128)S(1)}, s32[135,128]{1,0:T(8,128)}, u32[]{:S(2)}) copy-start(s32[135,128]{1,0:T(8,128)} %land_ref.5) | copy-start | bytes 207364
  1.4 11.6 %copy-start.5 = (s32[128]{0:T(128)S(1)}, s32[128]{0:T(128)}, u32[]{:S(2)}) copy-start(s32[128]{0:T(128)} %param.10) | copy-start | bytes 1540
  1.4 19.4 %copy-start.1 = (bf16[256,256]{1,0:T(8,128)(2,1)S(1)}, bf16[256,256]{1,0:T(8,128)(2,1)}, u32[]{:S(2)}) copy-start(bf16[256,256]{1,0:T(8,128)(2,1)} %constant.38.clone.forward_ref) | copy-start | bytes 393220
  1.4 19.4 %copy-start.2 = (bf16[256,256]{1,0:T(8,128)(2,1)S(1)}, bf16[256,256]{1,0:T(8,128)(2,1)}, u32[]{:S(2)}) copy-start(bf16[256,256]{1,0:T(8,128)(2,1)} %constant.39.clone.backward_ref) | copy-start | bytes 393220
  1.4 19.4 %copy-start.3 = (f32[32,128]{1,0:T(8,128)S(1)}, f32[32,128]{1,0:T(8,128)}, u32[]{:S(2)}) copy-start(f32[32,128]{1,0:T(8,128)} %constant.40.clone.inverse_ref) | copy-start | bytes 49156
  3.9 16.9 %all-to-all-start = ((bf16[32,24,128]{2,1,0:T(8,128)(2,1)}), bf16[32,24,128]{2,1,0:T(8,128)(2,1)S(1)}, u32[]{:S(2)}, u32[]{:S(2)}) async-start(bf16[32,24,128]{2,1,0:T(8,128)(2,1)} %pack.1), calls=%async_computation | async-start | bytes 393216 | tf_op jit(solution)/shard_map/all_to_all | solution.py:423
  23.4 25.3 %all-to-all-start.1 = ((bf16[32,24,128]{2,1,0:T(8,128)(2,1)}), bf16[32,24,128]{2,1,0:T(8,128)(2,1)S(1)}, u32[]{:S(2)}, u32[]{:S(2)}) async-start(bf16[32,24,128]{2,1,0:T(8,128)(2,1)} %filter.1), calls=%async_computation.1 | async-start | bytes 393216 | tf_op jit(solution)/shard_map/all_to_all | solution.py:423
  30.7 16.2 %collective-permute-start.2 = (f32[135,128]{1,0:T(8,128)S(1)}, f32[135,128]{1,0:T(8,128)S(1)}, u32[]{:S(2)}, u32[]{:S(2)}) collective-permute-start(f32[135,128]{1,0:T(8,128)S(1)} %get-tuple-element.10), channel_id=1, source_target_pairs={{0,1},{1,2},{2,3},{3,4},{4,5},{5,6},{6,7},{8,9},{9,10},{10,11},{11... | collective-permute-start | bytes 207368 | tf_op jit(solution)/shard_map/ppermute | solution.py:419
  34.6 12.3 %collective-permute-start.3 = (f32[135,128]{1,0:T(8,128)S(1)}, f32[135,128]{1,0:T(8,128)S(1)}, u32[]{:S(2)}, u32[]{:S(2)}) collective-permute-start(f32[135,128]{1,0:T(8,128)S(1)} %get-tuple-element.10), channel_id=1, source_target_pairs={{1,0},{2,1},{3,2},{4,3},{5,4},{6,5},{7,6},{9,8},{10,9},{11,10},{12... | collective-permute-start | bytes 207368 | tf_op jit(solution)/shard_map/ppermute | solution.py:419
  38.4 4.1 %collective-permute-start = (f32[24,128]{1,0:T(8,128)S(1)}, f32[24,128]{1,0:T(8,128)S(1)}, u32[]{:S(2)}, u32[]{:S(2)}) collective-permute-start(f32[24,128]{1,0:T(8,128)S(1)} %get-tuple-element.8), channel_id=1, source_target_pairs={{0,8},{8,16},{16,24},{24,32},{32,40},{40,48},{48,56},{56,64},{64,7... | collective-permute-start | bytes 36872 | tf_op jit(solution)/shard_map/ppermute | solution.py:419
  41.7 5.2 %collective-permute-start.1 = (f32[24,128]{1,0:T(8,128)S(1)}, f32[24,128]{1,0:T(8,128)S(1)}, u32[]{:S(2)}, u32[]{:S(2)}) collective-permute-start(f32[24,128]{1,0:T(8,128)S(1)} %get-tuple-element.9), channel_id=1, source_target_pairs={{0,248},{8,0},{16,8},{24,16},{32,24},{40,32},{48,40},{56,48},{64,5... | collective-permute-start | bytes 36872 | tf_op jit(solution)/shard_map/ppermute | solution.py:419

commit v2 on v1

--- a/solution.py
+++ b/solution.py
@@ -21,6 +21,9 @@
 CRT_COLS = 1216
 WAVES = 68
 ROWS = 16
+LEVELS = 4
+FIELD = COLS * LEVELS
+RIM = (0, FIELD - 4, 2 * FIELD - 8)
 CHUNK = 24
 
 MAIN = [lane + 1 for lane in range(128)]
@@ -70,23 +73,46 @@
     return lax.broadcasted_iota(jnp.int32, shape, len(shape) - 2)
 
 
+def level_rows(field, level):
+    return pl.ds(FIELD * field + level, COLS, stride=LEVELS)
+
+
 def faces(mask, kappa, mask_near, kappa_near):
     return 0.5 * (kappa + kappa_near) * mask * mask_near
 
 
-def pack_kernel(north_ref, adjoint_ref, land_ref, kappa_ref, out_ref, field, part):
-    north = north_ref[0] != 0
+def poles():
+    index = lax.axis_index("lat")
+    return index == 0, index == lax.axis_size("lat") - 1
+
+
+def at_pole():
+    south, north = poles()
+    return jnp.logical_or(south, north)
+
+
+def even(axis):
+    return lax.axis_index(axis) % 2 == 0
+
+
+def pack_kernel(*refs):
+    @pl.when(at_pole())
+    def _():
+        pack_rows(*refs)
+
+
+def pack_rows(adjoint_ref, land_ref, kappa_ref, out_ref, field, part):
+    north = poles()[1]
     whole = (COLS, 128)
     low, high = pl.ds(7, COLS), pl.ds(9, COLS)
     centre = pl.ds(8, COLS)
     zero = jnp.zeros((8, 128), F32)
-    for ref in (field,):
-        ref[0:8] = zero
-        ref[136:144] = zero
-        ref[144:152] = zero
+    field[0:8] = zero
+    field[136:144] = zero
+    field[144:152] = zero
     lane = lanes(whole)
     mask = land_ref[...].astype(F32)
-    kappa = kappa_ref[0]
+    kappa = kappa_ref[:, 0, :]
 
     field[centre] = kappa
     kappa_west, kappa_east = field[low], field[high]
@@ -106,7 +132,7 @@
         edge_fixed = jnp.where(slot == place, row, edge_fixed)
     part[136:144] = zero
     for index in range(8):
-        tilde = adjoint_ref[index // 4, index % 4] * mask
+        tilde = adjoint_ref[level_rows(index // 4, index % 4)] * mask
         field[centre] = tilde
         partial = (
             own * tilde
@@ -131,22 +157,21 @@
             ).astype(BF16)
 
 
-def pack(north, adjoint, land, diffusivity):
+def pack(adjoint, land, diffusivity):
     return pl.pallas_call(
         pack_kernel,
         grid=(1,),
         out_shape=jax.ShapeDtypeStruct((RING, CHUNK, 128), BF16),
         in_specs=[
-            pl.BlockSpec(memory_space=pltpu.SMEM),
-            pl.BlockSpec((2, 4, COLS, 128), lambda i: (0, 0, 0, 0)),
+            pl.BlockSpec((2 * FIELD, 128), lambda i: (0, 0)),
             pl.BlockSpec((COLS, 128), lambda i: (0, 0)),
-            pl.BlockSpec((1, COLS, 128), lambda i: (0, 0, 0)),
+            pl.BlockSpec((COLS, 2, 128), lambda i: (0, 0, 0)),
         ],
         out_specs=pl.BlockSpec((RING, CHUNK, 128), lambda i: (0, 0, 0)),
         scratch_shapes=[pltpu.VMEM((152, 128), F32), pltpu.VMEM((144, 128), F32)],
-        compiler_params=pltpu.CompilerParams(vmem_limit_bytes=24 * 2**20),
+        compiler_params=pltpu.CompilerParams(vmem_limit_bytes=60 * 2**20),
         name="pack",
-    )(north, adjoint, land, diffusivity)
+    )(adjoint, land, diffusivity)
 
 
 def times(re, im, angle_index, count, sign):
@@ -206,7 +231,13 @@
     return value
 
 
-def filter_kernel(in_ref, square_ref, forward_ref, backward_ref, inverse_ref, out_ref, held, wave):
+def filter_kernel(*refs):
+    @pl.when(at_pole())
+    def _():
+        filter_circles(*refs)
+
+
+def filter_circles(in_ref, square_ref, forward_ref, backward_ref, inverse_ref, out_ref, held, wave):
     tile = (ROWS, 128)
     spare = in_ref[:, ROWS:CHUNK, :].astype(F32).reshape(256, 128)
     spare = jnp.concatenate([spare[0:128].T[0:32], spare[128:256].T[0:32]], axis=1)
@@ -277,22 +308,23 @@
     )(chunks, square, forward, backward, inverse_square)
 
 
-def edge_kernel(adjoint_ref, land_ref, kappa_ref, first_ref, last_ref, side_ref):
+def edge_kernel(adjoint_ref, land_ref, kappa_ref, near_ref, far_ref, side_ref):
+    lon_even = even("lon")
     whole = (COLS, 128)
     lane = lanes(whole)
     mask = land_ref[...].astype(F32)
     sides = jnp.zeros(whole, F32)
-    first_ref[...] = jnp.zeros((24, 128), F32)
-    last_ref[...] = jnp.zeros((24, 128), F32)
+    near_ref[...] = jnp.zeros((24, 128), F32)
+    far_ref[...] = jnp.zeros((24, 128), F32)
     for index in range(19):
         if index < 16:
-            value = adjoint_ref[index // 4, index % 4] * mask
+            value = adjoint_ref[level_rows(index // 4, index % 4)] * mask
         elif index == 16:
             value = mask
         else:
-            value = kappa_ref[index - 17]
-        first_ref[index : index + 1] = value[0:1]
-        last_ref[index : index + 1] = value[134:135]
+            value = kappa_ref[:, index - 17, :]
+        near_ref[index : index + 1] = jnp.where(lon_even, value[134:135], value[0:1])
+        far_ref[index : index + 1] = jnp.where(lon_even, value[0:1], value[134:135])
         sides = jnp.where(lane // 2 == index, turn(value, 2 * index + 1), sides)
     side_ref[...] = sides
 
@@ -313,18 +345,29 @@
 
 
 def stencil_kernel(
-    adjoint_ref, land_ref, kappa_ref, west_ref, east_ref, south_ref, north_ref, out_ref, field
+    adjoint_ref,
+    land_ref,
+    kappa_ref,
+    near_side_ref,
+    far_side_ref,
+    out_ref,
+    flow_ref,
+    rim_ref,
+    field,
 ):
     whole = (COLS, 128)
     lane = lanes(whole)
     centre, low, high = pl.ds(8, COLS), pl.ds(7, COLS), pl.ds(9, COLS)
-    south_all, north_all = south_ref[...], north_ref[...]
+    lat_even = even("lat")
+    south_all = jnp.where(lat_even, far_side_ref[...], near_side_ref[...])
+    north_all = jnp.where(lat_even, near_side_ref[...], far_side_ref[...])
     mask = land_ref[...].astype(F32)
+    field[0:8] = jnp.zeros((8, 128), F32)
+    field[136:144] = jnp.zeros((8, 128), F32)
+    field[144:152] = jnp.zeros((8, 128), F32)
 
     def around(value, index):
         field[centre] = value
-        field[7:8] = west_ref[index : index + 1]
-        field[143:144] = east_ref[index : index + 1]
         above = jnp.where(lane == 127, turn(north_all, 126 - 2 * index), turn(value, -1))
         below = jnp.where(lane == 0, turn(south_all, -2 * index), turn(value, 1))
         return field[low], field[high], above, below
@@ -332,7 +375,7 @@
     mask_around = around(mask, 16)
     weights = []
     for number in range(2):
-        kappa = kappa_ref[number]
+        kappa = kappa_ref[:, number, :]
         near = around(kappa, 17 + number)
         four = [faces(mask, kappa, m, k) for m, k in zip(mask_around, near)]
         weights.append((1.0 - (four[0] + four[1] + four[2] + four[3]), *four))
@@ -343,7 +386,7 @@
         density = None
         for name in range(4):
             own, *four = weights[name // 2]
-            tilde = adjoint_ref[name, level] * mask
+            tilde = adjoint_ref[level_rows(name, level)] * mask
             near = around(tilde, 4 * name + level)
             total = own * tilde
             for weight, value in zip(four, near):
@@ -356,66 +399,160 @@
                 total = total - ALPHA_T * density
             else:
                 total = total + BETA_S * density
-            out_ref[name, level] = total
-
-
-def stencil(adjoint, land, diffusivity, west, east, south, north):
+            if name < 2:
+                flow_ref[level_rows(name, level)] = total
+            else:
+                out_ref[level_rows(name - 2, level)] = total
+    for number, start in enumerate(RIM):
+        rim_ref[8 * number : 8 * number + 8] = out_ref[start : start + 8]
+
+
+def stencil(adjoint, land, diffusivity, near_side, far_side):
     return pl.pallas_call(
         stencil_kernel,
-        out_shape=jax.ShapeDtypeStruct(adjoint.shape, F32),
-        in_specs=[pl.BlockSpec(memory_space=pltpu.VMEM)] * 7,
-        out_specs=pl.BlockSpec(memory_space=pltpu.VMEM),
+        grid=(1,),
+        out_shape=(
+            jax.ShapeDtypeStruct(adjoint.shape, F32),
+            jax.ShapeDtypeStruct((2 * FIELD, 128), F32),
+            jax.ShapeDtypeStruct((24, 128), F32),
+        ),
+        in_specs=[pl.BlockSpec(memory_space=pltpu.VMEM)] * 5,
+        out_specs=[
+            pl.BlockSpec((2 * FIELD, 128), lambda i: (1, 0)),
+            pl.BlockSpec(memory_space=pltpu.VMEM),
+            pl.BlockSpec(memory_space=pltpu.VMEM),
+        ],
         scratch_shapes=[pltpu.VMEM((152, 128), F32)],
         compiler_params=pltpu.CompilerParams(vmem_limit_bytes=24 * 2**20),
         name="stencil",
-    )(adjoint, land, diffusivity, west, east, south, north)
-
-
-def remove_kernel(pole_ref, chunks_ref, middle_ref, out_ref, high):
-    south, north = pole_ref[0] != 0, pole_ref[1] != 0
-    base = jnp.where(north, 64, 0)
+    )(adjoint, land, diffusivity, near_side, far_side)
+
+
+def crossing(own_near, own_far, near, far):
+    lon_even = even("lon")
+    own_west, own_east = jnp.where(lon_even, own_far, own_near), jnp.where(lon_even, own_near, own_far)
+    west, east = jnp.where(lon_even, far, near), jnp.where(lon_even, near, far)
+
+    def flux(own, other):
+        masks = own[16:17] * other[16:17]
+        first, second = (0.5 * (own[k : k + 1] + other[k : k + 1]) * masks for k in (17, 18))
+        step = other[0:16] - own[0:16]
+        return first * step[0:8], second * step[8:16]
+
+    west_flow, west_tracer = flux(own_west, west)
+    east_flow, east_tracer = flux(own_east, east)
+    west_density = -PRESSURE * own_west[16:17] * west[0:4]
+    east_density = PRESSURE * east[16:17] * own_east[0:4]
+    west_tracer += jnp.concatenate([-ALPHA_T * west_density, BETA_S * west_density], axis=0)
+    east_tracer += jnp.concatenate([-ALPHA_T * east_density, BETA_S * east_density], axis=0)
+    return west_flow, east_flow, west_tracer, east_tracer
+
+
+def remove_kernel(
+    chunks_ref,
+    flow_ref,
+    rim_ref,
+    own_near_ref,
+    own_far_ref,
+    near_ref,
+    far_ref,
+    whole_ref,
+    out_ref,
+    new_flow,
+    new_rim,
+    high,
+    done,
+):
+    del whole_ref
+    west, east, west_tracer, east_tracer = crossing(
+        own_near_ref[...], own_far_ref[...], near_ref[...], far_ref[...]
+    )
+    none = jnp.zeros((4, 128), F32)
+    new_rim[...] = rim_ref[...] + jnp.concatenate(
+        [west_tracer[0:4], none, east_tracer[0:4], west_tracer[4:8], none, east_tracer[4:8]], axis=0
+    )
+    copies = [
+        pltpu.make_async_copy(
+            new_rim.at[pl.ds(8 * number, 8)],
+            out_ref.at[pl.ds(2 * FIELD + start, 8)],
+            done.at[number],
+        )
+        for number, start in enumerate(RIM)
+    ]
+    polar = at_pole()
+    for copy in copies:
+        copy.start()
+    for name, (start, size) in enumerate(((0, FIELD - 4), (FIELD - 4, FIELD + 4))):
+
+        @pl.when(polar)
+        def _():
+            remove_waves(name, chunks_ref, flow_ref, new_flow, high)
+
+        rows = pl.ds(FIELD * name, FIELD)
+
+        @pl.when(jnp.logical_not(polar))
+        def _():
+            new_flow[rows] = flow_ref[rows]
+
+        first, last = pl.ds(FIELD * name, 4), pl.ds(FIELD * name + FIELD - 4, 4)
+        new_flow[first] = new_flow[first] + west[4 * name : 4 * name + 4]
+        new_flow[last] = new_flow[last] + east[4 * name : 4 * name + 4]
+        rows = pl.ds(start, size)
+        copy = pltpu.make_async_copy(new_flow.at[rows], out_ref.at[rows], done.at[3 + name])
+        copy.start()
+        copies.append(copy)
+    for copy in copies:
+        copy.wait()
+
+
+def remove_waves(name, chunks_ref, flow_ref, out_ref, high):
+    south, north = poles()
     group = (8, 128)
     lane = lanes(group)
-    polar = jnp.logical_or(south, north)
     for level in range(4):
-        first = (pl.program_id(0) * 4 + level) * 4
-        rows = chunks_ref[pl.ds(first, 4), 0:ROWS, :].astype(F32).reshape(64, 128)
-        both = jnp.concatenate(
-            [jnp.where(south, rows, 0.0), jnp.where(north, rows, 0.0)], axis=0
-        )
+        first = 16 * name + 4 * level
+        rows = chunks_ref[first : first + 4, 0:ROWS, :].astype(F32).reshape(64, 128)
+        both = jnp.concatenate([jnp.where(south, rows, 0.0), jnp.where(north, rows, 0.0)], axis=0)
         others = jnp.zeros(group, F32)
         for quarter in range(4):
             block = chunks_ref[first + quarter, ROWS:CHUNK, :].astype(F32)
             others = jnp.where(lane // 16 == quarter, turn(block, 16 * quarter), others)
-        others = jnp.where(lane < 64, others, turn(others, 64))
-        others = jnp.where(jnp.logical_and(lane // 64 == base // 64, polar), others, 0.0)
+        others = jnp.where(north, turn(others, 64), others)
         high[1:129] = both.T
         high[0:1] = others[0:1]
         high[129:135] = others[1:7]
-        out_ref[0, level] = middle_ref[0, level] - high[0:COLS]
-
-
-def remove(pole, chunks, middle):
+        rows_of = level_rows(name, level)
+        out_ref[rows_of] = flow_ref[rows_of] - high[0:COLS]
+
+
+def remove(chunks, flow, rim, own_near, own_far, near, far, whole):
     return pl.pallas_call(
         remove_kernel,
-        grid=(2,),
-        out_shape=jax.ShapeDtypeStruct(middle.shape, F32),
-        in_specs=[
-            pl.BlockSpec(memory_space=pltpu.SMEM),
-            pl.BlockSpec((RING, CHUNK, 128), lambda i: (0, 0, 0)),
-            pl.BlockSpec((1, 4, COLS, 128), lambda i: (i, 0, 0, 0)),
+        out_shape=jax.ShapeDtypeStruct(whole.shape, F32),
+        in_specs=[pl.BlockSpec(memory_space=pltpu.VMEM)] * 7 + [pl.BlockSpec(memory_space=pl.ANY)],
+        out_specs=pl.BlockSpec(memory_space=pl.ANY),
+        scratch_shapes=[
+            pltpu.VMEM((2 * FIELD, 128), F32),
+            pltpu.VMEM((24, 128), F32),
+            pltpu.VMEM((136, 128), F32),
+            pltpu.SemaphoreType.DMA((5,)),
         ],
-        out_specs=pl.BlockSpec((1, 4, COLS, 128), lambda i: (i, 0, 0, 0)),
-        scratch_shapes=[pltpu.VMEM((136, 128), F32)],
-        input_output_aliases={2: 0},
+        input_output_aliases={7: 0},
         compiler_params=pltpu.CompilerParams(vmem_limit_bytes=24 * 2**20),
         name="remove",
-    )(pole, chunks, middle)
-
-
-def shift(value, axis, step, periodic):
+    )(chunks, flow, rim, own_near, own_far, near, far, whole)
+
+
+def swap(value, axis, first):
     count = lax.axis_size(axis)
-    pairs = [(i, (i + step) % count) for i in range(count) if periodic or 0 <= i + step < count]
+    pairs = []
+    for a in range(first, count, 2):
+        b = a + 1
+        if b == count:
+            if axis == "lat":
+                continue
+            b = 0
+        pairs += [(a, b), (b, a)]
     return lax.ppermute(value, axis, pairs)
 
 
@@ -424,25 +561,31 @@
 
 
 def local(adjoint, land, diffusivity, cutoff):
-    lat_index = lax.axis_index("lat")
-    northern = (lat_index == lax.axis_size("lat") - 1).astype(jnp.int32)
-    southern = (lat_index == 0).astype(jnp.int32)
-    quarter = lax.axis_index("lon") % 4
-    cuts = lax.dynamic_slice_in_dim(cutoff, northern * PROWS + quarter * ROWS, ROWS, 0)
+    lon_index, lat_index = lax.axis_index("lon"), lax.axis_index("lat")
+    first_cut = jnp.where(lat_index == lax.axis_size("lat") - 1, PROWS, 0) + lon_index % 4 * ROWS
+    cuts = lax.dynamic_slice_in_dim(cutoff, first_cut, ROWS, 0)
     square = jnp.broadcast_to(jnp.square(cuts.astype(F32))[:, None], (ROWS, 128))
 
-    chunks = pack(northern[None], adjoint, land, diffusivity)
+    shape = adjoint.shape
+    fields = jnp.transpose(adjoint, (0, 2, 1, 3)).reshape(-1, shape[3])
+    kappas = jnp.transpose(diffusivity, (1, 0, 2))
+
+    chunks = pack(fields, land, kappas)
     circles = exchange(chunks)
-
-    first, last, sides = edge(adjoint, land, diffusivity)
-    west = shift(last, "lon", 1, True)
-    east = shift(first, "lon", -1, True)
-    south = shift(sides, "lat", 1, False)
-    north = shift(sides, "lat", -1, False)
-    middle = stencil(adjoint, land, diffusivity, west, east, south, north)
-
-    removed = exchange(filter_rows(circles, square))
-    return remove(jnp.stack([southern, northern]), removed, middle)
+    own_near, own_far, sides = edge(fields, land, kappas)
+    near_side = swap(sides, "lat", 0)
+    far_side = swap(sides, "lat", 1)
+    circles, near_side, far_side = lax.optimization_barrier((circles, near_side, far_side))
+
+    filtered = filter_rows(circles, square)
+    filtered, own_near, own_far = lax.optimization_barrier((filtered, own_near, own_far))
+    removed = exchange(filtered)
+    near = swap(own_near, "lon", 0)
+    far = swap(own_far, "lon", 1)
+    whole, flow, rim = stencil(fields, land, kappas, near_side, far_side)
+
+    out = remove(removed, flow, rim, own_near, own_far, near, far, whole)
+    return jnp.transpose(out.reshape(shape[0], shape[2], shape[1], shape[3]), (0, 2, 1, 3))
 
 
 def solution(mesh):

time: 51.4 us -> 45.3 us (0.88)
  the two profiles are of different devices: /device:TPU:107 before, /device:TPU:1 now
where the time goes in v2:
time: 45.3 us; the launch traced here: 45 us
  starting transfers between devices  22.6 us (50%)
  waiting for transfers between devices  11.5 us (25%)
  Pallas kernels  10.6 us (23%)
    all_to_all x2, starting transfers between devices, exchange(): lax.all_to_all(chunks, 'lon', split_axis=0, concat_axis=0, tiled=True)  16.6 us
    all_to_all x2, waiting for transfers between devices, exchange(): lax.all_to_all(chunks, 'lon', split_axis=0, concat_axis=0, tiled=True)  7.91 us
    ppermute x4, starting transfers between devices, swap(): return lax.ppermute(value, axis, pairs)  5.95 us
    pallas_call x1, Pallas kernels, pack(): pl.pallas_call(pack_kernel, grid=(1,), out_shape=jax.ShapeDtypeStruct((RI...  3.69 us
    ppermute x4, waiting for transfers between devices, swap(): return lax.ppermute(value, axis, pairs)  3.63 us
    pallas_call x1, Pallas kernels, stencil(): pl.pallas_call(stencil_kernel, grid=(1,), out_shape=(jax.ShapeDtypeStruct...  2.61 us
    pallas_call x1, Pallas kernels, filter_rows(): pl.pallas_call(filter_kernel, out_shape=jax.ShapeDtypeStruct((RING, CHUNK...  2.58 us
    pallas_call x1, Pallas kernels, remove(): pl.pallas_call(remove_kernel, out_shape=jax.ShapeDtypeStruct(whole.shape,...  1.26 us
  transfers between devices with their start and end apart: 6, of which 3 were waited for; matrix products, arithmetic and copies ran while one was open for 0% of the time, Pallas kernels for 7%

profile of v2, /device:TPU:1, one launch (start us, length us, event | category | flops | bytes accessed | tf_op | source)
XLA Modules:
  0.0 45.0 jit_solution(13840653311907677565)
XLA Ops:
  0.0 0.0 copy-start.2
  0.0 0.0 copy-start.1
  0.0 0.0 copy-start
  0.0 3.7 %pack.1 = bf16[32,24,128]{2,1,0:T(8,128)(2,1)} custom-call(f32[2160,128]{1,0:T(8,128)} %bitcast.7, s32[135,128]{1,0:T(8,128)} %land_ref.3, f32[135,2,128]{2,1,0:T(2,128)} %bitcast.10), custom_call_target="tpu_custom_call" | custom-call | tf_op jit(solution)/shard_map/pack/pallas_call | solution.py:161
  3.7 0.0 copy-start.6
  3.7 0.0 copy-start.3
  3.7 0.0 copy-start.4
  3.7 11.3 %all-to-all-start = ((bf16[32,24,128]{2,1,0:T(8,128)(2,1)}), bf16[32,24,128]{2,1,0:T(8,128)(2,1)S(1)}, u32[]{:S(2)}, u32[]{:S(2)}) async-start(bf16[32,24,128]{2,1,0:T(8,128)(2,1)} %pack.1), calls=%async_computation | async-start | bytes 393216 | tf_op jit(solution)/shard_map/all_to_all | solution.py:560
  15.0 0.0 copy-done.2
  15.0 0.0 copy-done.1
  15.0 0.0 copy-done
  15.0 0.4 edge.1
  15.5 0.7 %collective-permute-start.1 = (f32[135,128]{1,0:T(8,128)S(1)}, f32[135,128]{1,0:T(8,128)S(1)}, u32[]{:S(2)}, u32[]{:S(2)}) collective-permute-start(f32[135,128]{1,0:T(8,128)S(1)} %get-tuple-element.17), channel_id=1, source_target_pairs={{1,2},{2,1},{3,4},{4,3},{5,6},{6,5},{9,10},{10,9},{11,12},{12,11},... | collective-permute-start | bytes 207368 | tf_op jit(solution)/shard_map/ppermute | solution.py:556
  16.2 3.4 %collective-permute-start = (f32[135,128]{1,0:T(8,128)S(1)}, f32[135,128]{1,0:T(8,128)S(1)}, u32[]{:S(2)}, u32[]{:S(2)}) collective-permute-start(f32[135,128]{1,0:T(8,128)S(1)} %get-tuple-element.17), channel_id=1, source_target_pairs={{0,1},{1,0},{2,3},{3,2},{4,5},{5,4},{6,7},{7,6},{8,9},{9,8},{10,11... | collective-permute-start | bytes 207368 | tf_op jit(solution)/shard_map/ppermute | solution.py:556
  19.6 0.0 copy-done.6
  19.6 0.1 convert_multiply_fusion
  19.7 0.0 collective-permute-done.1.far_side_ref
  19.7 3.6 %collective-permute-done.near_side_ref = f32[135,128]{1,0:T(8,128)S(1)} collective-permute-done((f32[135,128]{1,0:T(8,128)S(1)}, f32[135,128]{1,0:T(8,128)S(1)}, u32[]{:S(2)}, u32[]{:S(2)}) %collective-permute-start) | collective-permute-done | bytes 69152 | tf_op jit(solution)/shard_map/ppermute | solution.py:556
  23.3 2.1 %all-to-all-done.refs_0_ = bf16[32,24,128]{2,1,0:T(8,128)(2,1)S(1)} async-done(((bf16[32,24,128]{2,1,0:T(8,128)(2,1)}), bf16[32,24,128]{2,1,0:T(8,128)(2,1)S(1)}, u32[]{:S(2)}, u32[]{:S(2)}) %all-to-all-start) | async-done | bytes 196640 | tf_op jit(solution)/shard_map/all_to_all | solution.py:560
  25.4 0.1 broadcast_in_dim.2.refs_1_
  25.4 0.0 copy-done.3
  25.4 0.0 copy-done.4
  25.4 0.0 copy-done.5
  25.4 2.6 %filter.1 = bf16[32,24,128]{2,1,0:T(8,128)(2,1)} custom-call(bf16[32,24,128]{2,1,0:T(8,128)(2,1)S(1)} %all-to-all-done.refs_0_, f32[16,128]{1,0:T(8,128)S(1)} %broadcast_in_dim.2.refs_1_, bf16[256,256]{1,0:T(8,128)(2,1)S(1)} %copy-done.4, bf16[256,256]{1,0:T(8,128)(2,1)S(1)} %copy-done.3, f32[32,128]{1,0:T(8,128)S(1)} %copy-done.5), custom_call_target="tpu_custom_call" | custom-call | tf_op jit(solution)/shard_map/filter/pallas_call | solution.py:297
  28.0 5.4 %all-to-all-start.1 = ((bf16[32,24,128]{2,1,0:T(8,128)(2,1)}), bf16[32,24,128]{2,1,0:T(8,128)(2,1)S(1)}, u32[]{:S(2)}, u32[]{:S(2)}) async-start(bf16[32,24,128]{2,1,0:T(8,128)(2,1)} %filter.1), calls=%async_computation.1 | async-start | bytes 393216 | tf_op jit(solution)/shard_map/all_to_all | solution.py:560
  33.4 0.3 collective-permute-start.2
  33.7 1.5 %collective-permute-start.3 = (f32[24,128]{1,0:T(8,128)S(1)}, f32[24,128]{1,0:T(8,128)S(1)}, u32[]{:S(2)}, u32[]{:S(2)}) collective-permute-start(f32[24,128]{1,0:T(8,128)S(1)} %get-tuple-element.27.own_far_ref), channel_id=1, source_target_pairs={{8,16},{16,8},{24,32},{32,24},{40,48},{48,40},{56,64},{64,56},{72,... | collective-permute-start | bytes 36872 | tf_op jit(solution)/shard_map/ppermute | solution.py:556
  35.2 2.6 %stencil.1 = (f32[2160,128]{1,0:T(8,128)}, f32[1080,128]{1,0:T(8,128)S(1)}, f32[24,128]{1,0:T(8,128)S(1)}) custom-call(f32[2160,128]{1,0:T(8,128)S(1)} %bitcast.9, s32[135,128]{1,0:T(8,128)S(1)} %copy-done.2, f32[135,2,128]{2,1,0:T(2,128)S(1)} %bitcast.12, f32[135,128]{1,0:T(8,128)S(1)} %collective-permute-done.near_side_ref, ...), custom_call_target="tpu_custom_call" | custom-call | tf_op jit(solution)/shard_map/stencil/pallas_call | solution.py:411
  37.9 0.0 collective-permute-done.2.near_ref
  37.9 0.0 collective-permute-done.3.far_ref
  37.9 5.9 %all-to-all-done.1.chunks_ref = bf16[32,24,128]{2,1,0:T(8,128)(2,1)S(1)} async-done(((bf16[32,24,128]{2,1,0:T(8,128)(2,1)}), bf16[32,24,128]{2,1,0:T(8,128)(2,1)S(1)}, u32[]{:S(2)}, u32[]{:S(2)}) %all-to-all-start.1) | async-done | bytes 196640 | tf_op jit(solution)/shard_map/all_to_all | solution.py:560
  43.7 1.3 %remove.1 = f32[2160,128]{1,0:T(8,128)} custom-call(bf16[32,24,128]{2,1,0:T(8,128)(2,1)S(1)} %all-to-all-done.1.chunks_ref, f32[1080,128]{1,0:T(8,128)S(1)} %get-tuple-element.24.flow_ref, f32[24,128]{1,0:T(8,128)S(1)} %get-tuple-element.25.rim_ref, f32[24,128]{1,0:T(8,128)S(1)} %get-tuple-element.26.own_near_ref, ...), custom_call_target="tpu_custom_call", output_to_operand_aliasing={{}: (7, {})} | custom-call | tf_op jit(solution)/shard_map/remove/pallas_call | solution.py:529
  (1 shorter events, 0.0 us)
Async XLA Ops:
  0.0 15.0 %copy-start.2 = (s32[135,128]{1,0:T(8,128)S(1)}, s32[135,128]{1,0:T(8,128)}, u32[]{:S(2)}) copy-start(s32[135,128]{1,0:T(8,128)} %land_ref.3) | copy-start | bytes 207364
  0.0 15.0 %copy-start.1 = (f32[2,135,128]{2,0,1:T(2,128)S(1)}, f32[2,135,128]{2,0,1:T(2,128)}, u32[]{:S(2)}) copy-start(f32[2,135,128]{2,0,1:T(2,128)} %param.9) | copy-start | bytes 414724
  0.0 15.0 %copy-start = (f32[4,4,135,128]{3,1,2,0:T(4,128)S(1)}, f32[4,4,135,128]{3,1,2,0:T(4,128)}, u32[]{:S(2)}) copy-start(f32[4,4,135,128]{3,1,2,0:T(4,128)} %param.7) | copy-start | bytes 3317764
  3.7 15.9 %copy-start.6 = (s32[128]{0:T(128)S(1)}, s32[128]{0:T(128)}, u32[]{:S(2)}) copy-start(s32[128]{0:T(128)} %param.10) | copy-start | bytes 1540
  3.7 21.7 %copy-start.3 = (bf16[256,256]{1,0:T(8,128)(2,1)S(1)}, bf16[256,256]{1,0:T(8,128)(2,1)}, u32[]{:S(2)}) copy-start(bf16[256,256]{1,0:T(8,128)(2,1)} %constant.38.clone.refs_3_) | copy-start | bytes 393220
  3.7 21.7 %copy-start.4 = (bf16[256,256]{1,0:T(8,128)(2,1)S(1)}, bf16[256,256]{1,0:T(8,128)(2,1)}, u32[]{:S(2)}) copy-start(bf16[256,256]{1,0:T(8,128)(2,1)} %constant.37.clone.refs_2_) | copy-start | bytes 393220
  3.7 21.7 %copy-start.5 = (f32[32,128]{1,0:T(8,128)S(1)}, f32[32,128]{1,0:T(8,128)}, u32[]{:S(2)}) copy-start(f32[32,128]{1,0:T(8,128)} %constant.39.clone.refs_4_) | copy-start | bytes 49156
  3.7 21.6 %all-to-all-start = ((bf16[32,24,128]{2,1,0:T(8,128)(2,1)}), bf16[32,24,128]{2,1,0:T(8,128)(2,1)S(1)}, u32[]{:S(2)}, u32[]{:S(2)}) async-start(bf16[32,24,128]{2,1,0:T(8,128)(2,1)} %pack.1), calls=%async_computation | async-start | bytes 393216 | tf_op jit(solution)/shard_map/all_to_all | solution.py:560
  15.5 4.2 %collective-permute-start.1 = (f32[135,128]{1,0:T(8,128)S(1)}, f32[135,128]{1,0:T(8,128)S(1)}, u32[]{:S(2)}, u32[]{:S(2)}) collective-permute-start(f32[135,128]{1,0:T(8,128)S(1)} %get-tuple-element.17), channel_id=1, source_target_pairs={{1,2},{2,1},{3,4},{4,3},{5,6},{6,5},{9,10},{10,9},{11,12},{12,11},... | collective-permute-start | bytes 207368 | tf_op jit(solution)/shard_map/ppermute | solution.py:556
  16.2 7.1 %collective-permute-start = (f32[135,128]{1,0:T(8,128)S(1)}, f32[135,128]{1,0:T(8,128)S(1)}, u32[]{:S(2)}, u32[]{:S(2)}) collective-permute-start(f32[135,128]{1,0:T(8,128)S(1)} %get-tuple-element.17), channel_id=1, source_target_pairs={{0,1},{1,0},{2,3},{3,2},{4,5},{5,4},{6,7},{7,6},{8,9},{9,8},{10,11... | collective-permute-start | bytes 207368 | tf_op jit(solution)/shard_map/ppermute | solution.py:556
  28.0 15.7 %all-to-all-start.1 = ((bf16[32,24,128]{2,1,0:T(8,128)(2,1)}), bf16[32,24,128]{2,1,0:T(8,128)(2,1)S(1)}, u32[]{:S(2)}, u32[]{:S(2)}) async-start(bf16[32,24,128]{2,1,0:T(8,128)(2,1)} %filter.1), calls=%async_computation.1 | async-start | bytes 393216 | tf_op jit(solution)/shard_map/all_to_all | solution.py:560
  33.4 4.5 %collective-permute-start.2 = (f32[24,128]{1,0:T(8,128)S(1)}, f32[24,128]{1,0:T(8,128)S(1)}, u32[]{:S(2)}, u32[]{:S(2)}) collective-permute-start(f32[24,128]{1,0:T(8,128)S(1)} %get-tuple-element.26.own_near_ref), channel_id=1, source_target_pairs={{0,8},{8,0},{16,24},{24,16},{32,40},{40,32},{48,56},{56,48},{64,72... | collective-permute-start | bytes 36872 | tf_op jit(solution)/shard_map/ppermute | solution.py:556
  33.7 4.2 %collective-permute-start.3 = (f32[24,128]{1,0:T(8,128)S(1)}, f32[24,128]{1,0:T(8,128)S(1)}, u32[]{:S(2)}, u32[]{:S(2)}) collective-permute-start(f32[24,128]{1,0:T(8,128)S(1)} %get-tuple-element.27.own_far_ref), channel_id=1, source_target_pairs={{8,16},{16,8},{24,32},{32,24},{40,48},{48,40},{56,64},{64,56},{72,... | collective-permute-start | bytes 36872 | tf_op jit(solution)/shard_map/ppermute | solution.py:556

commit v3 on v2

--- a/solution.py
+++ b/solution.py
@@ -24,27 +24,32 @@
 LEVELS = 4
 FIELD = COLS * LEVELS
 RIM = (0, FIELD - 4, 2 * FIELD - 8)
-CHUNK = 24
+CHUNK = ROWS + 2
+THIRD = 48
+PART = 8 * CHUNK
 
 MAIN = [lane + 1 for lane in range(128)]
-EXTRA = [0] + list(range(129, 135))
+EXTRA = [0] + list(range(129, 135)) + [None]
 
 F32 = jnp.float32
 BF16 = jnp.bfloat16
 
 
 def tables():
-    order = np.array(MAIN + EXTRA + [0] * 121)
-    used = np.array([1.0] * 135 + [0.0] * 121)
     waves = np.arange(WAVES)
-    angle = 2.0 * math.pi * ((38 * order[:, None] * waves[None, :]) % COLS) / COLS
-    forward = np.zeros((256, 256))
-    forward[:, :WAVES] = np.cos(angle) * used[:, None]
-    forward[:, 128 : 128 + WAVES] = -np.sin(angle) * used[:, None]
-    weight = np.where(waves == 0, 1.0, 2.0) / NLON
-    backward = forward.copy().T
-    backward[:WAVES] *= NLON * weight[:, None]
-    backward[128 : 128 + WAVES] *= NLON * weight[:, None]
+
+    def transform(slots):
+        columns = MAIN + [column for column in slots for _ in range(ROWS)]
+        used = np.array([[float(column is not None)] for column in columns])
+        order = np.array([[column or 0] for column in columns])
+        angle = 2.0 * math.pi * ((38 * order * waves) % COLS) / COLS
+        table = np.zeros((256, 256))
+        table[:, :WAVES] = np.cos(angle) * used
+        table[:, 128 : 128 + WAVES] = -np.sin(angle) * used
+        return table
+
+    forward, backward = transform(EXTRA), transform(EXTRA[::-1]).T
+    backward *= np.where(np.arange(256) % 128 == 0, 1.0, 2.0)[:, None]
     inverse_square = np.ones((RING, 128))
     for place in range(RING):
         kappa = int(format(place, "05b")[::-1], 2)
@@ -95,13 +100,30 @@
     return lax.axis_index(axis) % 2 == 0
 
 
+def spread(value):
+    return pltpu.roll(value, 0, 1, stride=ROWS, stride_axis=0)
+
+
 def pack_kernel(*refs):
     @pl.when(at_pole())
     def _():
         pack_rows(*refs)
 
 
-def pack_rows(adjoint_ref, land_ref, kappa_ref, out_ref, field, part):
+def pack_rows(
+    adjoint_hbm, land_hbm, kappa_hbm, out_hbm, rows, land, kappas, field, part, chunks, arrived, left
+):
+    def arrival(source, target, number):
+        copy = pltpu.make_async_copy(source, target, arrived.at[number])
+        copy.start()
+        return copy
+
+    first = arrival(land_hbm, land, 0), arrival(kappa_hbm, kappas, 1)
+    half = FIELD + 4
+    fields = [
+        arrival(adjoint_hbm.at[pl.ds(start, size)], rows.at[pl.ds(start, size)], number)
+        for number, start, size in ((2, 0, half), (3, half, 2 * FIELD - half))
+    ]
     north = poles()[1]
     whole = (COLS, 128)
     low, high = pl.ds(7, COLS), pl.ds(9, COLS)
@@ -111,9 +133,15 @@
     field[136:144] = zero
     field[144:152] = zero
     lane = lanes(whole)
-    mask = land_ref[...].astype(F32)
-    kappa = kappa_ref[:, 0, :]
-
+    chosen = (lanes((PROWS, 128)) == sublanes((PROWS, 128)) + jnp.where(north, 64, 0)).astype(BF16)
+    group = (8, 128)
+    slot = sublanes(group)
+    in_slot = lanes(group) // ROWS == slot
+
+    for copy in first:
+        copy.wait()
+    mask = land[...].astype(F32)
+    kappa = kappas[:, 0, :]
     field[centre] = kappa
     kappa_west, kappa_east = field[low], field[high]
     field[centre] = mask
@@ -123,52 +151,71 @@
     up = faces(mask, kappa, jnp.where(lane == 127, 0.0, turn(mask, -1)), turn(kappa, -1))
     down = faces(mask, kappa, jnp.where(lane == 0, 0.0, turn(mask, 1)), turn(kappa, 1))
     own = 1.0 - (west + east + up + down)
-
-    group = (8, 128)
-    slot = sublanes(group)
-    lane8 = lanes(group)
     edge_fixed = jnp.zeros(group, F32)
     for place, row in ((1, kappa[134:135]), (2, mask[134:135]), (4, kappa[0:1]), (5, mask[0:1])):
         edge_fixed = jnp.where(slot == place, row, edge_fixed)
-    part[136:144] = zero
-    for index in range(8):
-        tilde = adjoint_ref[level_rows(index // 4, index % 4)] * mask
-        field[centre] = tilde
-        partial = (
-            own * tilde
-            + west * field[low]
-            + east * field[high]
-            + up * turn(tilde, -1)
-            + down * turn(tilde, 1)
-        )
-        part[0:COLS] = partial
-        turned = part[pl.ds(1, 128)].T
-        chosen = jnp.where(north, turned[64:128], turned[0:64])
-        others = jnp.where(slot == 0, partial[0:1], part[128:136])
-        others = jnp.where(slot == 7, 0.0, others)
-        edges = jnp.where(slot == 0, tilde[134:135], jnp.where(slot == 3, tilde[0:1], edge_fixed))
-        others = jnp.where(north, turn(others, 64), others)
-        edges = jnp.where(north, turn(edges, 64), edges)
-        for quarter in range(4):
-            place = 4 * index + quarter
-            out_ref[place, 0:ROWS] = chosen[16 * quarter : 16 * quarter + 16].astype(BF16)
-            out_ref[place, ROWS:CHUNK] = jnp.where(
-                lane8 < 16, turn(others, -16 * quarter), turn(edges, 16 - 16 * quarter)
+
+    copies = []
+    for name in range(2):
+        fields[name].wait()
+        for level in range(4):
+            tilde = rows[level_rows(name, level)] * mask
+            field[centre] = tilde
+            partial = (
+                own * tilde
+                + west * field[low]
+                + east * field[high]
+                + up * turn(tilde, -1)
+                + down * turn(tilde, 1)
+            )
+            part[pl.ds(7, COLS)] = partial
+            turned = lax.dot_general(
+                chosen,
+                part[8:136].astype(BF16),
+                (((1,), (1,)), ((), ())),
+                preferred_element_type=F32,
             ).astype(BF16)
+            others = jnp.where(slot == 0, partial[0:1], part[pl.ds(135, 8)])
+            others = jnp.where(slot == 7, 0.0, others)
+            edges = jnp.where(slot == 0, tilde[134:135], jnp.where(slot == 3, tilde[0:1], edge_fixed))
+            others = spread(jnp.where(north, turn(others, 64), others))
+            edges = spread(jnp.where(north, turn(edges, 64), edges))
+            for quarter in range(4):
+                place = CHUNK * (16 * name + 4 * level + quarter)
+                chunks[place : place + ROWS] = turned[ROWS * quarter : ROWS * quarter + ROWS]
+                two = [
+                    jnp.sum(
+                        jnp.where(in_slot, turn(value, -ROWS * quarter), 0.0), axis=0, keepdims=True
+                    )
+                    for value in (others, edges)
+                ]
+                chunks[place + ROWS : place + CHUNK] = jnp.concatenate(two, axis=0).astype(BF16)
+            if level % 2:
+                number = 2 * name + level // 2
+                span = pl.ds(PART * number, PART)
+                copy = pltpu.make_async_copy(chunks.at[span], out_hbm.at[span], left.at[number])
+                copy.start()
+                copies.append(copy)
+    for copy in copies:
+        copy.wait()
 
 
 def pack(adjoint, land, diffusivity):
     return pl.pallas_call(
         pack_kernel,
-        grid=(1,),
-        out_shape=jax.ShapeDtypeStruct((RING, CHUNK, 128), BF16),
-        in_specs=[
-            pl.BlockSpec((2 * FIELD, 128), lambda i: (0, 0)),
-            pl.BlockSpec((COLS, 128), lambda i: (0, 0)),
-            pl.BlockSpec((COLS, 2, 128), lambda i: (0, 0, 0)),
+        out_shape=jax.ShapeDtypeStruct((RING * CHUNK, 128), BF16),
+        in_specs=[pl.BlockSpec(memory_space=pl.ANY)] * 3,
+        out_specs=pl.BlockSpec(memory_space=pl.ANY),
+        scratch_shapes=[
+            pltpu.VMEM((2 * FIELD, 128), F32),
+            pltpu.VMEM((COLS, 128), jnp.int32),
+            pltpu.VMEM((COLS, 2, 128), F32),
+            pltpu.VMEM((152, 128), F32),
+            pltpu.VMEM((144, 128), F32),
+            pltpu.VMEM((RING * CHUNK, 128), BF16),
+            pltpu.SemaphoreType.DMA((4,)),
+            pltpu.SemaphoreType.DMA((4,)),
         ],
-        out_specs=pl.BlockSpec((RING, CHUNK, 128), lambda i: (0, 0, 0)),
-        scratch_shapes=[pltpu.VMEM((152, 128), F32), pltpu.VMEM((144, 128), F32)],
         compiler_params=pltpu.CompilerParams(vmem_limit_bytes=60 * 2**20),
         name="pack",
     )(adjoint, land, diffusivity)
@@ -219,13 +266,13 @@
         half *= 2
 
 
-def slot_shift(value, sign):
-    slot = lanes(value.shape) % 8
+def ring_shift(value, step, columns):
+    slot = lanes(value.shape) // ROWS
     for bit in range(5):
-        moved = turn(value, sign * 8 * 2**bit)
+        moved = pltpu.roll(value, step * 2**bit % RING, 0)
         picked = jnp.zeros(value.shape, jnp.bool_)
-        for place, column in enumerate(EXTRA):
-            if (INV * column % RING) >> bit & 1:
+        for place, column in enumerate(columns):
+            if (column or 0) >> bit & 1:
                 picked = jnp.logical_or(picked, slot == place)
         value = jnp.where(picked, moved, value)
     return value
@@ -237,28 +284,33 @@
         filter_circles(*refs)
 
 
-def filter_circles(in_ref, square_ref, forward_ref, backward_ref, inverse_ref, out_ref, held, wave):
+def filter_circles(
+    in_ref, square_ref, forward_ref, backward_ref, inverse_ref, out_hbm, held, wave, pair, chunks, left
+):
     tile = (ROWS, 128)
-    spare = in_ref[:, ROWS:CHUNK, :].astype(F32).reshape(256, 128)
-    spare = jnp.concatenate([spare[0:128].T[0:32], spare[128:256].T[0:32]], axis=1)
-    others, edges = spare[0:16], spare[16:32]
-    slot = lanes(others.shape) % 8
-    beyond = turn(edges, -11)
-    flux = (beyond - edges) * turn(0.5 * (beyond + edges), -1) * turn(beyond * edges, -2)
-    others = others + jnp.where(slot == 6, turn(flux, 6), 0.0)
-    others = others - jnp.where(slot == 0, turn(flux, 8), 0.0)
-    others = slot_shift(others, 1)
-
+    own_row = lanes(tile) % ROWS == sublanes(tile)
     column = lanes(tile) + 1
-    rows = [in_ref[INV * t % RING, 0:ROWS, :] for t in range(RING)]
+    rows = []
+    for t in range(RING):
+        start = CHUNK * (INV * t % RING)
+        rows.append(in_ref[start : start + ROWS])
+        pair[2 * t : 2 * t + 2] = in_ref[start + ROWS : start + CHUNK].astype(F32)
     for bit in range(5):
         picked = (column >> bit) & 1 == 1
         rows = [jnp.where(picked, rows[(t - 2**bit) % RING], rows[t]) for t in range(RING)]
     for t in range(RING):
-        place = INV * t % RING
-        held[pl.ds(ROWS * t, ROWS), 0:128] = rows[t]
-        side = others[:, 128 * (place // 16) : 128 * (place // 16) + 128]
-        held[pl.ds(ROWS * t, ROWS), 128:256] = turn(side, -8 * (place % 16)).astype(BF16)
+        held[ROWS * t : ROWS * t + ROWS, 0:128] = rows[t]
+
+    others, edges = pair[pl.ds(0, RING, stride=2)], pair[pl.ds(1, RING, stride=2)]
+    slot = lanes(others.shape) // ROWS
+    beyond = turn(pltpu.roll(edges, RING - 7, 0), -3 * ROWS)
+    flux = (beyond - edges) * turn(0.5 * (beyond + edges), -ROWS) * turn(beyond * edges, -2 * ROWS)
+    others = others + jnp.where(slot == 6, turn(flux, 6 * ROWS), 0.0)
+    others = others - jnp.where(slot == 0, pltpu.roll(flux, 7, 0), 0.0)
+    pair[0:RING] = ring_shift(others, 1, EXTRA)
+    for t in range(RING):
+        side = jnp.where(own_row, pair[t : t + 1], 0.0)
+        held[ROWS * t : ROWS * t + ROWS, 128:256] = side.astype(BF16)
 
     wave[...] = jnp.dot(held[...], forward_ref[...], preferred_element_type=F32)
     for half in range(2):
@@ -275,40 +327,53 @@
             wave[rows_of[t], 128:256] = values[t][1]
     wave[...] = jnp.dot(wave[...].astype(BF16), backward_ref[...], preferred_element_type=F32)
 
-    rows = [wave[pl.ds(ROWS * t, ROWS), 0:128] for t in range(RING)]
+    for t in range(RING):
+        side = jnp.where(own_row, wave[ROWS * t : ROWS * t + ROWS, 128:256], 0.0)
+        held[ROWS * t : ROWS * t + ROWS, 128:256] = side.astype(BF16)
+    shape = (RING, RING * ROWS)
+    gather = (lanes(shape) // ROWS == sublanes(shape)).astype(BF16)
+    others = jnp.dot(gather, held[:, 128:256], preferred_element_type=F32)
+    pair[0:RING] = ring_shift(others, -1, EXTRA[::-1])
+
+    rows = [wave[ROWS * t : ROWS * t + ROWS, 0:128].astype(BF16) for t in range(RING)]
     for bit in range(5):
         picked = (column >> bit) & 1 == 1
         rows = [jnp.where(picked, rows[(t + 2**bit) % RING], rows[t]) for t in range(RING)]
+    copies = []
     for d in range(RING):
-        out_ref[d, 0:ROWS] = rows[7 * d % RING].astype(BF16)
-    sides = [jnp.zeros(tile, F32), jnp.zeros(tile, F32)]
-    for t in range(RING):
-        place = INV * t % RING
-        sides[place // 16] += turn(wave[pl.ds(ROWS * t, ROWS), 128:256], 8 * (place % 16))
-    others = slot_shift(jnp.concatenate(sides, axis=1), -1)
-    blank = jnp.zeros((112, 128), F32)
-    for half in range(2):
-        back = jnp.concatenate([others[:, 128 * half : 128 * half + 128], blank], axis=0).T
-        out_ref[16 * half : 16 * half + 16, ROWS:CHUNK] = back.reshape(16, 8, 128).astype(BF16)
+        place = 7 * d % RING
+        chunks[CHUNK * d : CHUNK * d + ROWS] = rows[place]
+        last = jnp.broadcast_to(pair[place : place + 1], (2, 128))
+        chunks[CHUNK * d + ROWS : CHUNK * d + CHUNK] = last.astype(BF16)
+        if d % 8 == 7:
+            span = pl.ds(PART * (d // 8), PART)
+            copy = pltpu.make_async_copy(chunks.at[span], out_hbm.at[span], left.at[d // 8])
+            copy.start()
+            copies.append(copy)
+    for copy in copies:
+        copy.wait()
 
 
 def filter_rows(chunks, square):
     forward, backward, inverse_square = tables()
     return pl.pallas_call(
         filter_kernel,
-        out_shape=jax.ShapeDtypeStruct((RING, CHUNK, 128), BF16),
+        out_shape=jax.ShapeDtypeStruct((RING * CHUNK, 128), BF16),
         in_specs=[pl.BlockSpec(memory_space=pltpu.VMEM)] * 5,
-        out_specs=pl.BlockSpec(memory_space=pltpu.VMEM),
+        out_specs=pl.BlockSpec(memory_space=pl.ANY),
         scratch_shapes=[
             pltpu.VMEM((RING * ROWS, 256), BF16),
             pltpu.VMEM((RING * ROWS, 256), F32),
+            pltpu.VMEM((2 * RING, 128), F32),
+            pltpu.VMEM((RING * CHUNK, 128), BF16),
+            pltpu.SemaphoreType.DMA((4,)),
         ],
         compiler_params=pltpu.CompilerParams(vmem_limit_bytes=24 * 2**20),
         name="filter",
     )(chunks, square, forward, backward, inverse_square)
 
 
-def edge_kernel(adjoint_ref, land_ref, kappa_ref, near_ref, far_ref, side_ref):
+def edge_kernel(adjoint_ref, land_ref, kappa_ref, near_ref, far_ref, side_ref, unfolded):
     lon_even = even("lon")
     whole = (COLS, 128)
     lane = lanes(whole)
@@ -326,7 +391,16 @@
         near_ref[index : index + 1] = jnp.where(lon_even, value[134:135], value[0:1])
         far_ref[index : index + 1] = jnp.where(lon_even, value[0:1], value[134:135])
         sides = jnp.where(lane // 2 == index, turn(value, 2 * index + 1), sides)
-    side_ref[...] = sides
+    unfolded[0:COLS] = sides
+    lane = lanes((THIRD, 128))
+    second, third = turn(unfolded[THIRD : 2 * THIRD], 40), turn(unfolded[2 * THIRD : 3 * THIRD], 80)
+    side_ref[...] = jnp.where(
+        lane < 40, unfolded[0:THIRD], jnp.where(lane < 80, second, third)
+    )
+
+
+def unfold(value):
+    return jnp.concatenate([value, turn(value, -40), turn(value, -80)], axis=0)[0:COLS]
 
 
 def edge(adjoint, land, diffusivity):
@@ -335,10 +409,11 @@
         out_shape=(
             jax.ShapeDtypeStruct((24, 128), F32),
             jax.ShapeDtypeStruct((24, 128), F32),
-            jax.ShapeDtypeStruct((COLS, 128), F32),
+            jax.ShapeDtypeStruct((THIRD, 128), F32),
         ),
         in_specs=[pl.BlockSpec(memory_space=pltpu.VMEM)] * 3,
         out_specs=[pl.BlockSpec(memory_space=pltpu.VMEM)] * 3,
+        scratch_shapes=[pltpu.VMEM((3 * THIRD, 128), F32)],
         compiler_params=pltpu.CompilerParams(vmem_limit_bytes=24 * 2**20),
         name="edge",
     )(adjoint, land, diffusivity)
@@ -359,8 +434,8 @@
     lane = lanes(whole)
     centre, low, high = pl.ds(8, COLS), pl.ds(7, COLS), pl.ds(9, COLS)
     lat_even = even("lat")
-    south_all = jnp.where(lat_even, far_side_ref[...], near_side_ref[...])
-    north_all = jnp.where(lat_even, near_side_ref[...], far_side_ref[...])
+    south_all = unfold(jnp.where(lat_even, far_side_ref[...], near_side_ref[...]))
+    north_all = unfold(jnp.where(lat_even, near_side_ref[...], far_side_ref[...]))
     mask = land_ref[...].astype(F32)
     field[0:8] = jnp.zeros((8, 128), F32)
     field[136:144] = jnp.zeros((8, 128), F32)
@@ -506,23 +581,29 @@
 
 
 def remove_waves(name, chunks_ref, flow_ref, out_ref, high):
-    south, north = poles()
-    group = (8, 128)
-    lane = lanes(group)
-    for level in range(4):
+    north = poles()[1]
+    group, square = (8, 128), (128, 128)
+    quarter_of = (lanes(group) // ROWS + sublanes(group)) % 8
+    here = (lanes(square) >= 64) == north
+    for level in range(0, 4, 2):
         first = 16 * name + 4 * level
-        rows = chunks_ref[first : first + 4, 0:ROWS, :].astype(F32).reshape(64, 128)
-        both = jnp.concatenate([jnp.where(south, rows, 0.0), jnp.where(north, rows, 0.0)], axis=0)
-        others = jnp.zeros(group, F32)
-        for quarter in range(4):
-            block = chunks_ref[first + quarter, ROWS:CHUNK, :].astype(F32)
-            others = jnp.where(lane // 16 == quarter, turn(block, 16 * quarter), others)
-        others = jnp.where(north, turn(others, 64), others)
-        high[1:129] = both.T
-        high[0:1] = others[0:1]
-        high[129:135] = others[1:7]
-        rows_of = level_rows(name, level)
-        out_ref[rows_of] = flow_ref[rows_of] - high[0:COLS]
+        starts = [CHUNK * (first + place) for place in range(8)]
+        both = jnp.concatenate([chunks_ref[a : a + ROWS].astype(F32) for a in starts], axis=0).T
+        across = turn(both, 64)
+        for second in range(2):
+            others = jnp.zeros(group, F32)
+            for quarter in range(4):
+                start = starts[4 * second + quarter] + ROWS
+                row = turn(chunks_ref[start : start + 2].astype(F32)[0:1], ROWS * (quarter + 1))
+                others = jnp.where(quarter_of == quarter, row, others)
+            others = spread(others)
+            others = jnp.where(north, turn(others, 64), others)
+            straight = jnp.where(north, across, both) if second == 0 else jnp.where(north, both, across)
+            high[1:129] = jnp.where(here, straight, 0.0)
+            high[0:1] = others[0:1]
+            high[129:135] = others[1:7]
+            rows_of = level_rows(name, level + second)
+            out_ref[rows_of] = flow_ref[rows_of] - high[0:COLS]
 
 
 def remove(chunks, flow, rim, own_near, own_far, near, far, whole):
@@ -557,7 +638,8 @@
 
 
 def exchange(chunks):
-    return lax.all_to_all(chunks, "lon", split_axis=0, concat_axis=0, tiled=True)
+    pairs = chunks.reshape(-1, 2, chunks.shape[1])
+    return lax.all_to_all(pairs, "lon", split_axis=0, concat_axis=0, tiled=True).reshape(chunks.shape)
 
 
 def local(adjoint, land, diffusivity, cutoff):

time: 45.3 us -> 42.4 us (0.936)
  Pallas kernels: 10.6 us -> 9.27 us
  starting transfers between devices: 22.6 us -> 21.6 us
  waiting for transfers between devices: 11.5 us -> 10.9 us
    ppermute x4, waiting for transfers between devices: 3.63 us -> 2.11 us  [swap(): return lax.ppermute(value, axis, pairs)]
    pallas_call x2, Pallas kernels: 6.27 us -> 4.84 us  [the longest x1 2.86 us: pack(): pl.pallas_call(pack_kernel, out_shape=jax.ShapeDtypeStruct((RING * CHUNK,...]
    ppermute x4, starting transfers between devices: 5.95 us -> 4.98 us  [swap(): return lax.ppermute(value, axis, pairs)]
    all_to_all x2, waiting for transfers between devices: 7.91 us -> 8.8 us  [exchange(): lax.all_to_all(pairs, 'lon', split_axis=0, concat_axis=0, tiled=True)]
where the time goes in v3:
time: 42.4 us; the launch traced here: 42.1 us
  starting transfers between devices  21.6 us (51%)
  waiting for transfers between devices  10.9 us (26%)
  Pallas kernels  9.27 us (22%)
    all_to_all x2, starting transfers between devices, exchange(): lax.all_to_all(pairs, 'lon', split_axis=0, concat_axis=0, tiled=True)  16.7 us
    all_to_all x2, waiting for transfers between devices, exchange(): lax.all_to_all(pairs, 'lon', split_axis=0, concat_axis=0, tiled=True)  8.8 us
    ppermute x4, starting transfers between devices, swap(): return lax.ppermute(value, axis, pairs)  4.98 us
    pallas_call x1, Pallas kernels, pack(): pl.pallas_call(pack_kernel, out_shape=jax.ShapeDtypeStruct((RING * CHUNK,...  2.86 us
    pallas_call x1, Pallas kernels, stencil(): pl.pallas_call(stencil_kernel, grid=(1,), out_shape=(jax.ShapeDtypeStruct...  2.63 us
    ppermute x4, waiting for transfers between devices, swap(): return lax.ppermute(value, axis, pairs)  2.11 us
    pallas_call x1, Pallas kernels, filter_rows(): pl.pallas_call(filter_kernel, out_shape=jax.ShapeDtypeStruct((RING * CHUN...  1.98 us
    pallas_call x1, Pallas kernels, remove(): pl.pallas_call(remove_kernel, out_shape=jax.ShapeDtypeStruct(whole.shape,...  1.32 us
  transfers between devices with their start and end apart: 6, of which 3 were waited for; matrix products, arithmetic and copies ran while one was open for 0% of the time, Pallas kernels for 7%

profile of v3, /device:TPU:1, one launch (start us, length us, event | category | flops | bytes accessed | tf_op | source)
XLA Modules:
  0.0 42.1 jit_solution(14727723602733790940)
XLA Ops:
  0.0 0.0 copy-start.2
  0.0 0.0 copy-start.1
  0.0 2.9 %pack.1 = bf16[576,128]{1,0:T(8,128)(2,1)} custom-call(f32[2160,128]{1,0:T(8,128)} %bitcast.11, s32[135,128]{1,0:T(8,128)} %land_ref.3, f32[135,2,128]{2,1,0:T(2,128)} %bitcast.14), custom_call_target="tpu_custom_call" | custom-call | tf_op jit(solution)/shard_map/pack/pallas_call | solution.py:204
  2.9 0.0 copy-start.6
  2.9 0.0 copy-start.3
  2.9 0.0 copy-start.4
  2.9 0.0 copy-start.5
  2.9 11.3 %all-to-all-start = ((bf16[288,2,128]{2,1,0:T(2,128)(2,1)}), bf16[288,2,128]{2,1,0:T(2,128)(2,1)S(1)}, u32[]{:S(2)}, u32[]{:S(2)}) async-start(bf16[288,2,128]{2,1,0:T(2,128)(2,1)} %bitcast.19), calls=%async_computation | async-start | bytes 294912 | tf_op jit(solution)/shard_map/all_to_all | solution.py:642
  14.2 0.0 copy-done.2
  14.2 0.0 copy-done.1
  14.2 0.0 copy-done
  14.2 0.5 %edge.1 = (f32[24,128]{1,0:T(8,128)S(1)}, f32[24,128]{1,0:T(8,128)S(1)}, f32[48,128]{1,0:T(8,128)S(1)}) custom-call(f32[2160,128]{1,0:T(8,128)S(1)} %bitcast.12, s32[135,128]{1,0:T(8,128)S(1)} %copy-done.2, f32[135,2,128]{2,1,0:T(2,128)S(1)} %bitcast.15), custom_call_target="tpu_custom_call" | custom-call | tf_op jit(solution)/shard_map/edge/pallas_call | solution.py:407
  14.7 0.7 %collective-permute-start.1 = (f32[48,128]{1,0:T(8,128)S(1)}, f32[48,128]{1,0:T(8,128)S(1)}, u32[]{:S(2)}, u32[]{:S(2)}) collective-permute-start(f32[48,128]{1,0:T(8,128)S(1)} %get-tuple-element.17), channel_id=1, source_target_pairs={{1,2},{2,1},{3,4},{4,3},{5,6},{6,5},{9,10},{10,9},{11,12},{12,11},... | collective-permute-start | bytes 73736 | tf_op jit(solution)/shard_map/ppermute | solution.py:637
  15.4 2.5 %collective-permute-start = (f32[48,128]{1,0:T(8,128)S(1)}, f32[48,128]{1,0:T(8,128)S(1)}, u32[]{:S(2)}, u32[]{:S(2)}) collective-permute-start(f32[48,128]{1,0:T(8,128)S(1)} %get-tuple-element.17), channel_id=1, source_target_pairs={{0,1},{1,0},{2,3},{3,2},{4,5},{5,4},{6,7},{7,6},{8,9},{9,8},{10,11... | collective-permute-start | bytes 73736 | tf_op jit(solution)/shard_map/ppermute | solution.py:637
  17.9 0.0 copy-done.6
  17.9 0.1 convert_multiply_fusion
  17.9 0.0 collective-permute-done.1.far_side_ref
  17.9 2.1 %collective-permute-done.near_side_ref = f32[48,128]{1,0:T(8,128)S(1)} collective-permute-done((f32[48,128]{1,0:T(8,128)S(1)}, f32[48,128]{1,0:T(8,128)S(1)}, u32[]{:S(2)}, u32[]{:S(2)}) %collective-permute-start) | collective-permute-done | bytes 24608 | tf_op jit(solution)/shard_map/ppermute | solution.py:637
  20.0 3.7 %all-to-all-done = bf16[288,2,128]{2,1,0:T(2,128)(2,1)S(1)} async-done(((bf16[288,2,128]{2,1,0:T(2,128)(2,1)}), bf16[288,2,128]{2,1,0:T(2,128)(2,1)S(1)}, u32[]{:S(2)}, u32[]{:S(2)}) %all-to-all-start) | async-done | bytes 147488 | tf_op jit(solution)/shard_map/all_to_all | solution.py:642
  23.7 0.1 broadcast_in_dim.2.refs_1_
  23.8 0.0 copy-done.3
  23.8 0.0 copy-done.4
  23.8 0.0 copy-done.5
  23.8 2.0 %filter.1 = bf16[576,128]{1,0:T(8,128)(2,1)} custom-call(bf16[576,128]{1,0:T(8,128)(2,1)S(1)} %bitcast.18, f32[16,128]{1,0:T(8,128)S(1)} %broadcast_in_dim.2.refs_1_, bf16[256,256]{1,0:T(8,128)(2,1)S(1)} %copy-done.4, bf16[256,256]{1,0:T(8,128)(2,1)S(1)} %copy-done.3, f32[32,128]{1,0:T(8,128)S(1)} %copy-done.5), custom_call_target="tpu_custom_call" | custom-call | tf_op jit(solution)/shard_map/filter/pallas_call | solution.py:359
  25.8 5.4 %all-to-all-start.1 = ((bf16[288,2,128]{2,1,0:T(2,128)(2,1)}), bf16[288,2,128]{2,1,0:T(2,128)(2,1)S(1)}, u32[]{:S(2)}, u32[]{:S(2)}) async-start(bf16[288,2,128]{2,1,0:T(2,128)(2,1)} %bitcast.6), calls=%async_computation.1 | async-start | bytes 294912 | tf_op jit(solution)/shard_map/all_to_all | solution.py:642
  31.2 0.3 collective-permute-start.2
  31.5 1.5 %collective-permute-start.3 = (f32[24,128]{1,0:T(8,128)S(1)}, f32[24,128]{1,0:T(8,128)S(1)}, u32[]{:S(2)}, u32[]{:S(2)}) collective-permute-start(f32[24,128]{1,0:T(8,128)S(1)} %get-tuple-element.27.own_far_ref), channel_id=1, source_target_pairs={{8,16},{16,8},{24,32},{32,24},{40,48},{48,40},{56,64},{64,56},{72,... | collective-permute-start | bytes 36872 | tf_op jit(solution)/shard_map/ppermute | solution.py:637
  33.1 2.6 %stencil.1 = (f32[2160,128]{1,0:T(8,128)}, f32[1080,128]{1,0:T(8,128)S(1)}, f32[24,128]{1,0:T(8,128)S(1)}) custom-call(f32[2160,128]{1,0:T(8,128)S(1)} %bitcast.13, s32[135,128]{1,0:T(8,128)S(1)} %copy-done.2, f32[135,2,128]{2,1,0:T(2,128)S(1)} %bitcast.16, f32[48,128]{1,0:T(8,128)S(1)} %collective-permute-done.near_side_ref, ...), custom_call_target="tpu_custom_call" | custom-call | tf_op jit(solution)/shard_map/stencil/pallas_call | solution.py:486
  35.7 0.0 collective-permute-done.2.near_ref
  35.7 0.0 collective-permute-done.3.far_ref
  35.7 5.1 %all-to-all-done.1 = bf16[288,2,128]{2,1,0:T(2,128)(2,1)S(1)} async-done(((bf16[288,2,128]{2,1,0:T(2,128)(2,1)}), bf16[288,2,128]{2,1,0:T(2,128)(2,1)S(1)}, u32[]{:S(2)}, u32[]{:S(2)}) %all-to-all-start.1) | async-done | bytes 147488 | tf_op jit(solution)/shard_map/all_to_all | solution.py:642
  40.8 1.3 %remove.1 = f32[2160,128]{1,0:T(8,128)} custom-call(bf16[576,128]{1,0:T(8,128)(2,1)S(1)} %bitcast.17, f32[1080,128]{1,0:T(8,128)S(1)} %get-tuple-element.24.flow_ref, f32[24,128]{1,0:T(8,128)S(1)} %get-tuple-element.25.rim_ref, f32[24,128]{1,0:T(8,128)S(1)} %get-tuple-element.26.own_near_ref, ...), custom_call_target="tpu_custom_call", output_to_operand_aliasing={{}: (7, {})} | custom-call | tf_op jit(solution)/shard_map/remove/pallas_call | solution.py:610
  (1 shorter events, 0.0 us)
Async XLA Ops:
  0.0 14.2 %copy-start.2 = (s32[135,128]{1,0:T(8,128)S(1)}, s32[135,128]{1,0:T(8,128)}, u32[]{:S(2)}) copy-start(s32[135,128]{1,0:T(8,128)} %land_ref.3) | copy-start | bytes 207364
  0.0 14.2 %copy-start.1 = (f32[2,135,128]{2,0,1:T(2,128)S(1)}, f32[2,135,128]{2,0,1:T(2,128)}, u32[]{:S(2)}) copy-start(f32[2,135,128]{2,0,1:T(2,128)} %param.9) | copy-start | bytes 414724
  0.0 14.2 %copy-start = (f32[4,4,135,128]{3,1,2,0:T(4,128)S(1)}, f32[4,4,135,128]{3,1,2,0:T(4,128)}, u32[]{:S(2)}) copy-start(f32[4,4,135,128]{3,1,2,0:T(4,128)} %param.7) | copy-start | bytes 3317764
  2.9 15.0 %copy-start.6 = (s32[128]{0:T(128)S(1)}, s32[128]{0:T(128)}, u32[]{:S(2)}) copy-start(s32[128]{0:T(128)} %param.10) | copy-start | bytes 1540
  2.9 20.9 %copy-start.3 = (bf16[256,256]{1,0:T(8,128)(2,1)S(1)}, bf16[256,256]{1,0:T(8,128)(2,1)}, u32[]{:S(2)}) copy-start(bf16[256,256]{1,0:T(8,128)(2,1)} %constant.38.clone.refs_3_) | copy-start | bytes 393220
  2.9 20.9 %copy-start.4 = (bf16[256,256]{1,0:T(8,128)(2,1)S(1)}, bf16[256,256]{1,0:T(8,128)(2,1)}, u32[]{:S(2)}) copy-start(bf16[256,256]{1,0:T(8,128)(2,1)} %constant.37.clone.refs_2_) | copy-start | bytes 393220
  2.9 20.9 %copy-start.5 = (f32[32,128]{1,0:T(8,128)S(1)}, f32[32,128]{1,0:T(8,128)}, u32[]{:S(2)}) copy-start(f32[32,128]{1,0:T(8,128)} %constant.39.clone.refs_4_) | copy-start | bytes 49156
  2.9 20.8 %all-to-all-start = ((bf16[288,2,128]{2,1,0:T(2,128)(2,1)}), bf16[288,2,128]{2,1,0:T(2,128)(2,1)S(1)}, u32[]{:S(2)}, u32[]{:S(2)}) async-start(bf16[288,2,128]{2,1,0:T(2,128)(2,1)} %bitcast.19), calls=%async_computation | async-start | bytes 294912 | tf_op jit(solution)/shard_map/all_to_all | solution.py:642
  14.7 3.2 %collective-permute-start.1 = (f32[48,128]{1,0:T(8,128)S(1)}, f32[48,128]{1,0:T(8,128)S(1)}, u32[]{:S(2)}, u32[]{:S(2)}) collective-permute-start(f32[48,128]{1,0:T(8,128)S(1)} %get-tuple-element.17), channel_id=1, source_target_pairs={{1,2},{2,1},{3,4},{4,3},{5,6},{6,5},{9,10},{10,9},{11,12},{12,11},... | collective-permute-start | bytes 73736 | tf_op jit(solution)/shard_map/ppermute | solution.py:637
  15.4 4.6 %collective-permute-start = (f32[48,128]{1,0:T(8,128)S(1)}, f32[48,128]{1,0:T(8,128)S(1)}, u32[]{:S(2)}, u32[]{:S(2)}) collective-permute-start(f32[48,128]{1,0:T(8,128)S(1)} %get-tuple-element.17), channel_id=1, source_target_pairs={{0,1},{1,0},{2,3},{3,2},{4,5},{5,4},{6,7},{7,6},{8,9},{9,8},{10,11... | collective-permute-start | bytes 73736 | tf_op jit(solution)/shard_map/ppermute | solution.py:637
  25.8 15.0 %all-to-all-start.1 = ((bf16[288,2,128]{2,1,0:T(2,128)(2,1)}), bf16[288,2,128]{2,1,0:T(2,128)(2,1)S(1)}, u32[]{:S(2)}, u32[]{:S(2)}) async-start(bf16[288,2,128]{2,1,0:T(2,128)(2,1)} %bitcast.6), calls=%async_computation.1 | async-start | bytes 294912 | tf_op jit(solution)/shard_map/all_to_all | solution.py:642
  31.2 4.5 %collective-permute-start.2 = (f32[24,128]{1,0:T(8,128)S(1)}, f32[24,128]{1,0:T(8,128)S(1)}, u32[]{:S(2)}, u32[]{:S(2)}) collective-permute-start(f32[24,128]{1,0:T(8,128)S(1)} %get-tuple-element.26.own_near_ref), channel_id=1, source_target_pairs={{0,8},{8,0},{16,24},{24,16},{32,40},{40,32},{48,56},{56,48},{64,72... | collective-permute-start | bytes 36872 | tf_op jit(solution)/shard_map/ppermute | solution.py:637
  31.5 4.2 %collective-permute-start.3 = (f32[24,128]{1,0:T(8,128)S(1)}, f32[24,128]{1,0:T(8,128)S(1)}, u32[]{:S(2)}, u32[]{:S(2)}) collective-permute-start(f32[24,128]{1,0:T(8,128)S(1)} %get-tuple-element.27.own_far_ref), channel_id=1, source_target_pairs={{8,16},{16,8},{24,32},{32,24},{40,48},{48,40},{56,64},{64,56},{72,... | collective-permute-start | bytes 36872 | tf_op jit(solution)/shard_map/ppermute | solution.py:637

commit v4 on v3

--- a/solution.py
+++ b/solution.py
@@ -100,6 +100,12 @@
     return lax.axis_index(axis) % 2 == 0
 
 
+def clear_ends(field):
+    for place in range(field.shape[0]):
+        field[place, 0:8] = jnp.zeros((8, 128), F32)
+        field[place, 136:144] = jnp.zeros((8, 128), F32)
+
+
 def spread(value):
     return pltpu.roll(value, 0, 1, stride=ROWS, stride_axis=0)
 
@@ -128,10 +134,7 @@
     whole = (COLS, 128)
     low, high = pl.ds(7, COLS), pl.ds(9, COLS)
     centre = pl.ds(8, COLS)
-    zero = jnp.zeros((8, 128), F32)
-    field[0:8] = zero
-    field[136:144] = zero
-    field[144:152] = zero
+    clear_ends(field)
     lane = lanes(whole)
     chosen = (lanes((PROWS, 128)) == sublanes((PROWS, 128)) + jnp.where(north, 64, 0)).astype(BF16)
     group = (8, 128)
@@ -142,10 +145,10 @@
         copy.wait()
     mask = land[...].astype(F32)
     kappa = kappas[:, 0, :]
-    field[centre] = kappa
-    kappa_west, kappa_east = field[low], field[high]
-    field[centre] = mask
-    mask_west, mask_east = field[low], field[high]
+    field[0, centre] = kappa
+    kappa_west, kappa_east = field[0, low], field[0, high]
+    field[1, centre] = mask
+    mask_west, mask_east = field[1, low], field[1, high]
     west = faces(mask, kappa, mask_west, kappa_west)
     east = faces(mask, kappa, mask_east, kappa_east)
     up = faces(mask, kappa, jnp.where(lane == 127, 0.0, turn(mask, -1)), turn(kappa, -1))
@@ -160,22 +163,23 @@
         fields[name].wait()
         for level in range(4):
             tilde = rows[level_rows(name, level)] * mask
-            field[centre] = tilde
+            place = 2 + 4 * name + level
+            field[place, centre] = tilde
             partial = (
                 own * tilde
-                + west * field[low]
-                + east * field[high]
+                + west * field[place, low]
+                + east * field[place, high]
                 + up * turn(tilde, -1)
                 + down * turn(tilde, 1)
             )
-            part[pl.ds(7, COLS)] = partial
+            part[place, pl.ds(7, COLS)] = partial
             turned = lax.dot_general(
                 chosen,
-                part[8:136].astype(BF16),
+                part[place, 8:136].astype(BF16),
                 (((1,), (1,)), ((), ())),
                 preferred_element_type=F32,
             ).astype(BF16)
-            others = jnp.where(slot == 0, partial[0:1], part[pl.ds(135, 8)])
+            others = jnp.where(slot == 0, partial[0:1], part[place, pl.ds(135, 8)])
             others = jnp.where(slot == 7, 0.0, others)
             edges = jnp.where(slot == 0, tilde[134:135], jnp.where(slot == 3, tilde[0:1], edge_fixed))
             others = spread(jnp.where(north, turn(others, 64), others))
@@ -210,8 +214,8 @@
             pltpu.VMEM((2 * FIELD, 128), F32),
             pltpu.VMEM((COLS, 128), jnp.int32),
             pltpu.VMEM((COLS, 2, 128), F32),
-            pltpu.VMEM((152, 128), F32),
-            pltpu.VMEM((144, 128), F32),
+            pltpu.VMEM((10, 152, 128), F32),
+            pltpu.VMEM((10, 144, 128), F32),
             pltpu.VMEM((RING * CHUNK, 128), BF16),
             pltpu.SemaphoreType.DMA((4,)),
             pltpu.SemaphoreType.DMA((4,)),
@@ -285,7 +289,7 @@
 
 
 def filter_circles(
-    in_ref, square_ref, forward_ref, backward_ref, inverse_ref, out_hbm, held, wave, pair, chunks, left
+    in_ref, square_ref, forward_ref, backward_ref, inverse_ref, out_ref, held, wave, pair
 ):
     tile = (ROWS, 128)
     own_row = lanes(tile) % ROWS == sublanes(tile)
@@ -339,19 +343,11 @@
     for bit in range(5):
         picked = (column >> bit) & 1 == 1
         rows = [jnp.where(picked, rows[(t + 2**bit) % RING], rows[t]) for t in range(RING)]
-    copies = []
     for d in range(RING):
         place = 7 * d % RING
-        chunks[CHUNK * d : CHUNK * d + ROWS] = rows[place]
+        out_ref[CHUNK * d : CHUNK * d + ROWS] = rows[place]
         last = jnp.broadcast_to(pair[place : place + 1], (2, 128))
-        chunks[CHUNK * d + ROWS : CHUNK * d + CHUNK] = last.astype(BF16)
-        if d % 8 == 7:
-            span = pl.ds(PART * (d // 8), PART)
-            copy = pltpu.make_async_copy(chunks.at[span], out_hbm.at[span], left.at[d // 8])
-            copy.start()
-            copies.append(copy)
-    for copy in copies:
-        copy.wait()
+        out_ref[CHUNK * d + ROWS : CHUNK * d + CHUNK] = last.astype(BF16)
 
 
 def filter_rows(chunks, square):
@@ -360,13 +356,11 @@
         filter_kernel,
         out_shape=jax.ShapeDtypeStruct((RING * CHUNK, 128), BF16),
         in_specs=[pl.BlockSpec(memory_space=pltpu.VMEM)] * 5,
-        out_specs=pl.BlockSpec(memory_space=pl.ANY),
+        out_specs=pl.BlockSpec(memory_space=pltpu.VMEM),
         scratch_shapes=[
             pltpu.VMEM((RING * ROWS, 256), BF16),
             pltpu.VMEM((RING * ROWS, 256), F32),
             pltpu.VMEM((2 * RING, 128), F32),
-            pltpu.VMEM((RING * CHUNK, 128), BF16),
-            pltpu.SemaphoreType.DMA((4,)),
         ],
         compiler_params=pltpu.CompilerParams(vmem_limit_bytes=24 * 2**20),
         name="filter",
@@ -436,16 +430,16 @@
     lat_even = even("lat")
     south_all = unfold(jnp.where(lat_even, far_side_ref[...], near_side_ref[...]))
     north_all = unfold(jnp.where(lat_even, near_side_ref[...], far_side_ref[...]))
+    halos = jnp.where(lane % 2 == 0, south_all, turn(north_all, -2))
     mask = land_ref[...].astype(F32)
-    field[0:8] = jnp.zeros((8, 128), F32)
-    field[136:144] = jnp.zeros((8, 128), F32)
-    field[144:152] = jnp.zeros((8, 128), F32)
+    clear_ends(field)
 
     def around(value, index):
-        field[centre] = value
-        above = jnp.where(lane == 127, turn(north_all, 126 - 2 * index), turn(value, -1))
-        below = jnp.where(lane == 0, turn(south_all, -2 * index), turn(value, 1))
-        return field[low], field[high], above, below
+        field[index, centre] = value
+        halo = turn(halos, -2 * index)
+        above = jnp.where(lane == 127, halo, turn(value, -1))
+        below = jnp.where(lane == 0, halo, turn(value, 1))
+        return field[index, low], field[index, high], above, below
 
     mask_around = around(mask, 16)
     weights = []
@@ -497,7 +491,7 @@
             pl.BlockSpec(memory_space=pltpu.VMEM),
             pl.BlockSpec(memory_space=pltpu.VMEM),
         ],
-        scratch_shapes=[pltpu.VMEM((152, 128), F32)],
+        scratch_shapes=[pltpu.VMEM((19, 152, 128), F32)],
         compiler_params=pltpu.CompilerParams(vmem_limit_bytes=24 * 2**20),
         name="stencil",
     )(adjoint, land, diffusivity, near_side, far_side)
@@ -599,11 +593,12 @@
             others = spread(others)
             others = jnp.where(north, turn(others, 64), others)
             straight = jnp.where(north, across, both) if second == 0 else jnp.where(north, both, across)
-            high[1:129] = jnp.where(here, straight, 0.0)
-            high[0:1] = others[0:1]
-            high[129:135] = others[1:7]
-            rows_of = level_rows(name, level + second)
-            out_ref[rows_of] = flow_ref[rows_of] - high[0:COLS]
+            place = level + second
+            high[place, 1:129] = jnp.where(here, straight, 0.0)
+            high[place, 0:1] = others[0:1]
+            high[place, 129:135] = others[1:7]
+            rows_of = level_rows(name, place)
+            out_ref[rows_of] = flow_ref[rows_of] - high[place, 0:COLS]
 
 
 def remove(chunks, flow, rim, own_near, own_far, near, far, whole):
@@ -615,7 +610,7 @@
         scratch_shapes=[
             pltpu.VMEM((2 * FIELD, 128), F32),
             pltpu.VMEM((24, 128), F32),
-            pltpu.VMEM((136, 128), F32),
+            pltpu.VMEM((4, 136, 128), F32),
             pltpu.SemaphoreType.DMA((5,)),
         ],
         input_output_aliases={7: 0},
@@ -652,16 +647,12 @@
     fields = jnp.transpose(adjoint, (0, 2, 1, 3)).reshape(-1, shape[3])
     kappas = jnp.transpose(diffusivity, (1, 0, 2))
 
-    chunks = pack(fields, land, kappas)
-    circles = exchange(chunks)
+    filtered = filter_rows(exchange(pack(fields, land, kappas)), square)
+    filtered, fields, land, kappas = lax.optimization_barrier((filtered, fields, land, kappas))
+    removed = exchange(filtered)
     own_near, own_far, sides = edge(fields, land, kappas)
+    far_side = swap(sides, "lat", 1)
     near_side = swap(sides, "lat", 0)
-    far_side = swap(sides, "lat", 1)
-    circles, near_side, far_side = lax.optimization_barrier((circles, near_side, far_side))
-
-    filtered = filter_rows(circles, square)
-    filtered, own_near, own_far = lax.optimization_barrier((filtered, own_near, own_far))
-    removed = exchange(filtered)
     near = swap(own_near, "lon", 0)
     far = swap(own_far, "lon", 1)
     whole, flow, rim = stencil(fields, land, kappas, near_side, far_side)

time: 42.4 us -> 40.9 us (0.965)
  starting transfers between devices: 21.6 us -> 19.5 us
  waiting for transfers between devices: 10.9 us -> 12.1 us
  Pallas kernels: 9.27 us -> 8.71 us
    all_to_all x2, waiting for transfers between devices: 8.8 us -> 11 us  [exchange(): lax.all_to_all(pairs, 'lon', split_axis=0, concat_axis=0, tiled=True)]
    all_to_all x2, starting transfers between devices: 16.7 us -> 15.3 us  [exchange(): lax.all_to_all(pairs, 'lon', split_axis=0, concat_axis=0, tiled=True)]
    ppermute x4, waiting for transfers between devices: 2.11 us -> 1.12 us  [swap(): return lax.ppermute(value, axis, pairs)]
    ppermute x4, starting transfers between devices: 4.98 us -> 4.17 us  [swap(): return lax.ppermute(value, axis, pairs)]
    pallas_call x1, Pallas kernels: 2.63 us -> 2.17 us  [stencil(): pl.pallas_call(stencil_kernel, grid=(1,), out_shape=(jax.ShapeDtypeStruct...]
where the time goes in v4:
time: 40.9 us; the launch traced here: 40.7 us
  starting transfers between devices  19.5 us (48%)
  waiting for transfers between devices  12.1 us (30%)
  Pallas kernels  8.71 us (21%)
    all_to_all x2, starting transfers between devices, exchange(): lax.all_to_all(pairs, 'lon', split_axis=0, concat_axis=0, tiled=True)  15.3 us
    all_to_all x2, waiting for transfers between devices, exchange(): lax.all_to_all(pairs, 'lon', split_axis=0, concat_axis=0, tiled=True)  11 us
    ppermute x4, starting transfers between devices, swap(): return lax.ppermute(value, axis, pairs)  4.17 us
    pallas_call x1, Pallas kernels, pack(): pl.pallas_call(pack_kernel, out_shape=jax.ShapeDtypeStruct((RING * CHUNK,...  2.87 us
    pallas_call x1, Pallas kernels, stencil(): pl.pallas_call(stencil_kernel, grid=(1,), out_shape=(jax.ShapeDtypeStruct...  2.17 us
    pallas_call x1, Pallas kernels, filter_rows(): pl.pallas_call(filter_kernel, out_shape=jax.ShapeDtypeStruct((RING * CHUN...  1.94 us
    pallas_call x1, Pallas kernels, remove(): pl.pallas_call(remove_kernel, out_shape=jax.ShapeDtypeStruct(whole.shape,...  1.25 us
    ppermute x4, waiting for transfers between devices, swap(): return lax.ppermute(value, axis, pairs)  1.12 us
  transfers between devices with their start and end apart: 6, of which 3 were waited for; matrix products, arithmetic and copies ran while one was open for 0% of the time, Pallas kernels for 7%

profile of v4, /device:TPU:1, one launch (start us, length us, event | category | flops | bytes accessed | tf_op | source)
XLA Modules:
  0.0 40.7 jit_solution(16762455507740789535)
XLA Ops:
  0.0 0.0 copy-start.3
  0.0 0.0 copy-start.4
  0.0 0.0 copy-start.6
  0.0 0.0 copy-start
  0.0 0.0 copy-start.1
  0.0 0.0 copy-start.2
  0.0 2.9 %pack.1 = bf16[576,128]{1,0:T(8,128)(2,1)} custom-call(f32[2160,128]{1,0:T(8,128)} %bitcast.11, s32[135,128]{1,0:T(8,128)} %land_ref.1, f32[135,2,128]{2,1,0:T(2,128)} %bitcast.14), custom_call_target="tpu_custom_call" | custom-call | tf_op jit(solution)/shard_map/pack/pallas_call | solution.py:208
  2.9 11.1 %all-to-all-start = ((bf16[288,2,128]{2,1,0:T(2,128)(2,1)}), bf16[288,2,128]{2,1,0:T(2,128)(2,1)S(1)}, u32[]{:S(2)}, u32[]{:S(2)}) async-start(bf16[288,2,128]{2,1,0:T(2,128)(2,1)} %bitcast.19), calls=%async_computation | async-start | bytes 294912 | tf_op jit(solution)/shard_map/all_to_all | solution.py:637
  14.1 0.0 copy-done.6
  14.1 0.1 convert_multiply_fusion
  14.2 9.4 %all-to-all-done = bf16[288,2,128]{2,1,0:T(2,128)(2,1)S(1)} async-done(((bf16[288,2,128]{2,1,0:T(2,128)(2,1)}), bf16[288,2,128]{2,1,0:T(2,128)(2,1)S(1)}, u32[]{:S(2)}, u32[]{:S(2)}) %all-to-all-start) | async-done | bytes 147488 | tf_op jit(solution)/shard_map/all_to_all | solution.py:637
  23.6 0.1 broadcast_in_dim.2.refs_1_
  23.7 0.0 copy-done.5
  23.7 0.0 copy-done.3
  23.7 0.0 copy-done.4
  23.7 1.9 %filter.1 = bf16[576,128]{1,0:T(8,128)(2,1)} custom-call(bf16[576,128]{1,0:T(8,128)(2,1)S(1)} %bitcast.18, f32[16,128]{1,0:T(8,128)S(1)} %broadcast_in_dim.2.refs_1_, bf16[256,256]{1,0:T(8,128)(2,1)S(1)} %copy-done.4, bf16[256,256]{1,0:T(8,128)(2,1)S(1)} %copy-done.3, f32[32,128]{1,0:T(8,128)S(1)} %copy-done.5), custom_call_target="tpu_custom_call" | custom-call | tf_op jit(solution)/shard_map/filter/pallas_call | solution.py:355
  25.6 4.2 %all-to-all-start.1 = ((bf16[288,2,128]{2,1,0:T(2,128)(2,1)}), bf16[288,2,128]{2,1,0:T(2,128)(2,1)S(1)}, u32[]{:S(2)}, u32[]{:S(2)}) async-start(bf16[288,2,128]{2,1,0:T(2,128)(2,1)} %bitcast.5), calls=%async_computation.1 | async-start | bytes 294912 | tf_op jit(solution)/shard_map/all_to_all | solution.py:637
  29.8 0.0 copy-done
  29.8 0.0 copy-done.1
  29.8 0.0 copy-done.2
  29.9 0.5 %edge.1 = (f32[24,128]{1,0:T(8,128)S(1)}, f32[24,128]{1,0:T(8,128)S(1)}, f32[48,128]{1,0:T(8,128)S(1)}) custom-call(f32[2160,128]{1,0:T(8,128)S(1)} %bitcast.12, s32[135,128]{1,0:T(8,128)S(1)} %copy-done.2, f32[135,2,128]{2,1,0:T(2,128)S(1)} %bitcast.15), custom_call_target="tpu_custom_call" | custom-call | tf_op jit(solution)/shard_map/edge/pallas_call | solution.py:401
  30.3 0.7 %collective-permute-start.1 = (f32[48,128]{1,0:T(8,128)S(1)}, f32[48,128]{1,0:T(8,128)S(1)}, u32[]{:S(2)}, u32[]{:S(2)}) collective-permute-start(f32[48,128]{1,0:T(8,128)S(1)} %get-tuple-element.19), channel_id=1, source_target_pairs={{1,2},{2,1},{3,4},{4,3},{5,6},{6,5},{9,10},{10,9},{11,12},{12,11},... | collective-permute-start | bytes 73736 | tf_op jit(solution)/shard_map/ppermute | solution.py:632
  31.0 1.3 %collective-permute-start = (f32[48,128]{1,0:T(8,128)S(1)}, f32[48,128]{1,0:T(8,128)S(1)}, u32[]{:S(2)}, u32[]{:S(2)}) collective-permute-start(f32[48,128]{1,0:T(8,128)S(1)} %get-tuple-element.19), channel_id=1, source_target_pairs={{0,1},{1,0},{2,3},{3,2},{4,5},{5,4},{6,7},{7,6},{8,9},{9,8},{10,11... | collective-permute-start | bytes 73736 | tf_op jit(solution)/shard_map/ppermute | solution.py:632
  32.3 0.9 %collective-permute-start.2 = (f32[24,128]{1,0:T(8,128)S(1)}, f32[24,128]{1,0:T(8,128)S(1)}, u32[]{:S(2)}, u32[]{:S(2)}) collective-permute-start(f32[24,128]{1,0:T(8,128)S(1)} %get-tuple-element.22.own_near_ref), channel_id=1, source_target_pairs={{0,8},{8,0},{16,24},{24,16},{32,40},{40,32},{48,56},{56,48},{64,72... | collective-permute-start | bytes 36872 | tf_op jit(solution)/shard_map/ppermute | solution.py:632
  33.2 1.3 %collective-permute-start.3 = (f32[24,128]{1,0:T(8,128)S(1)}, f32[24,128]{1,0:T(8,128)S(1)}, u32[]{:S(2)}, u32[]{:S(2)}) collective-permute-start(f32[24,128]{1,0:T(8,128)S(1)} %get-tuple-element.23.own_far_ref), channel_id=1, source_target_pairs={{8,16},{16,8},{24,32},{32,24},{40,48},{48,40},{56,64},{64,56},{72,... | collective-permute-start | bytes 36872 | tf_op jit(solution)/shard_map/ppermute | solution.py:632
  34.5 0.0 collective-permute-done.1.far_side_ref
  34.5 1.1 %collective-permute-done.near_side_ref = f32[48,128]{1,0:T(8,128)S(1)} collective-permute-done((f32[48,128]{1,0:T(8,128)S(1)}, f32[48,128]{1,0:T(8,128)S(1)}, u32[]{:S(2)}, u32[]{:S(2)}) %collective-permute-start) | collective-permute-done | bytes 24608 | tf_op jit(solution)/shard_map/ppermute | solution.py:632
  35.6 2.2 %stencil.1 = (f32[2160,128]{1,0:T(8,128)}, f32[1080,128]{1,0:T(8,128)S(1)}, f32[24,128]{1,0:T(8,128)S(1)}) custom-call(f32[2160,128]{1,0:T(8,128)S(1)} %bitcast.13, s32[135,128]{1,0:T(8,128)S(1)} %copy-done.2, f32[135,2,128]{2,1,0:T(2,128)S(1)} %bitcast.16, f32[48,128]{1,0:T(8,128)S(1)} %collective-permute-done.near_side_ref, ...), custom_call_target="tpu_custom_call" | custom-call | tf_op jit(solution)/shard_map/stencil/pallas_call | solution.py:480
  37.8 0.0 collective-permute-done.2.near_ref
  37.8 0.0 collective-permute-done.3.far_ref
  37.8 1.6 %all-to-all-done.1 = bf16[288,2,128]{2,1,0:T(2,128)(2,1)S(1)} async-done(((bf16[288,2,128]{2,1,0:T(2,128)(2,1)}), bf16[288,2,128]{2,1,0:T(2,128)(2,1)S(1)}, u32[]{:S(2)}, u32[]{:S(2)}) %all-to-all-start.1) | async-done | bytes 147488 | tf_op jit(solution)/shard_map/all_to_all | solution.py:637
  39.4 1.3 %remove.1 = f32[2160,128]{1,0:T(8,128)} custom-call(bf16[576,128]{1,0:T(8,128)(2,1)S(1)} %bitcast.17, f32[1080,128]{1,0:T(8,128)S(1)} %get-tuple-element.20.flow_ref, f32[24,128]{1,0:T(8,128)S(1)} %get-tuple-element.21.rim_ref, f32[24,128]{1,0:T(8,128)S(1)} %get-tuple-element.22.own_near_ref, ...), custom_call_target="tpu_custom_call", output_to_operand_aliasing={{}: (7, {})} | custom-call | tf_op jit(solution)/shard_map/remove/pallas_call | solution.py:605
  (1 shorter events, 0.0 us)
Async XLA Ops:
  0.0 23.7 %copy-start.5 = (f32[32,128]{1,0:T(8,128)S(1)}, f32[32,128]{1,0:T(8,128)}, u32[]{:S(2)}) copy-start(f32[32,128]{1,0:T(8,128)} %constant.39.clone.refs_4_) | copy-start | bytes 49156
  0.0 23.7 %copy-start.3 = (bf16[256,256]{1,0:T(8,128)(2,1)S(1)}, bf16[256,256]{1,0:T(8,128)(2,1)}, u32[]{:S(2)}) copy-start(bf16[256,256]{1,0:T(8,128)(2,1)} %constant.38.clone.refs_3_) | copy-start | bytes 393220
  0.0 23.7 %copy-start.4 = (bf16[256,256]{1,0:T(8,128)(2,1)S(1)}, bf16[256,256]{1,0:T(8,128)(2,1)}, u32[]{:S(2)}) copy-start(bf16[256,256]{1,0:T(8,128)(2,1)} %constant.37.clone.refs_2_) | copy-start | bytes 393220
  0.0 14.1 %copy-start.6 = (s32[128]{0:T(128)S(1)}, s32[128]{0:T(128)}, u32[]{:S(2)}) copy-start(s32[128]{0:T(128)} %param.10) | copy-start | bytes 1540
  0.0 29.8 %copy-start = (f32[4,4,135,128]{3,1,2,0:T(4,128)S(1)}, f32[4,4,135,128]{3,1,2,0:T(4,128)}, u32[]{:S(2)}) copy-start(f32[4,4,135,128]{3,1,2,0:T(4,128)} %param.7) | copy-start | bytes 3317764
  0.0 29.8 %copy-start.1 = (f32[2,135,128]{2,0,1:T(2,128)S(1)}, f32[2,135,128]{2,0,1:T(2,128)}, u32[]{:S(2)}) copy-start(f32[2,135,128]{2,0,1:T(2,128)} %param.9) | copy-start | bytes 414724
  0.0 29.8 %copy-start.2 = (s32[135,128]{1,0:T(8,128)S(1)}, s32[135,128]{1,0:T(8,128)}, u32[]{:S(2)}) copy-start(s32[135,128]{1,0:T(8,128)} %land_ref.1) | copy-start | bytes 207364
  2.9 20.7 %all-to-all-start = ((bf16[288,2,128]{2,1,0:T(2,128)(2,1)}), bf16[288,2,128]{2,1,0:T(2,128)(2,1)S(1)}, u32[]{:S(2)}, u32[]{:S(2)}) async-start(bf16[288,2,128]{2,1,0:T(2,128)(2,1)} %bitcast.19), calls=%async_computation | async-start | bytes 294912 | tf_op jit(solution)/shard_map/all_to_all | solution.py:637
  25.6 13.8 %all-to-all-start.1 = ((bf16[288,2,128]{2,1,0:T(2,128)(2,1)}), bf16[288,2,128]{2,1,0:T(2,128)(2,1)S(1)}, u32[]{:S(2)}, u32[]{:S(2)}) async-start(bf16[288,2,128]{2,1,0:T(2,128)(2,1)} %bitcast.5), calls=%async_computation.1 | async-start | bytes 294912 | tf_op jit(solution)/shard_map/all_to_all | solution.py:637
  30.3 4.2 %collective-permute-start.1 = (f32[48,128]{1,0:T(8,128)S(1)}, f32[48,128]{1,0:T(8,128)S(1)}, u32[]{:S(2)}, u32[]{:S(2)}) collective-permute-start(f32[48,128]{1,0:T(8,128)S(1)} %get-tuple-element.19), channel_id=1, source_target_pairs={{1,2},{2,1},{3,4},{4,3},{5,6},{6,5},{9,10},{10,9},{11,12},{12,11},... | collective-permute-start | bytes 73736 | tf_op jit(solution)/shard_map/ppermute | solution.py:632
  31.0 4.6 %collective-permute-start = (f32[48,128]{1,0:T(8,128)S(1)}, f32[48,128]{1,0:T(8,128)S(1)}, u32[]{:S(2)}, u32[]{:S(2)}) collective-permute-start(f32[48,128]{1,0:T(8,128)S(1)} %get-tuple-element.19), channel_id=1, source_target_pairs={{0,1},{1,0},{2,3},{3,2},{4,5},{5,4},{6,7},{7,6},{8,9},{9,8},{10,11... | collective-permute-start | bytes 73736 | tf_op jit(solution)/shard_map/ppermute | solution.py:632
  32.3 5.5 %collective-permute-start.2 = (f32[24,128]{1,0:T(8,128)S(1)}, f32[24,128]{1,0:T(8,128)S(1)}, u32[]{:S(2)}, u32[]{:S(2)}) collective-permute-start(f32[24,128]{1,0:T(8,128)S(1)} %get-tuple-element.22.own_near_ref), channel_id=1, source_target_pairs={{0,8},{8,0},{16,24},{24,16},{32,40},{40,32},{48,56},{56,48},{64,72... | collective-permute-start | bytes 36872 | tf_op jit(solution)/shard_map/ppermute | solution.py:632
  33.2 4.6 %collective-permute-start.3 = (f32[24,128]{1,0:T(8,128)S(1)}, f32[24,128]{1,0:T(8,128)S(1)}, u32[]{:S(2)}, u32[]{:S(2)}) collective-permute-start(f32[24,128]{1,0:T(8,128)S(1)} %get-tuple-element.23.own_far_ref), channel_id=1, source_target_pairs={{8,16},{16,8},{24,32},{32,24},{40,48},{48,40},{56,64},{64,56},{72,... | collective-permute-start | bytes 36872 | tf_op jit(solution)/shard_map/ppermute | solution.py:632

commit v5 on v4

--- a/solution.py
+++ b/solution.py
@@ -19,6 +19,8 @@
 INV = 23
 CRT_RING = 3105
 CRT_COLS = 1216
+LEAD_OUT = 24
+LEAD_BACK = 16
 WAVES = 68
 ROWS = 16
 LEVELS = 4
@@ -62,6 +64,10 @@
         jnp.asarray(backward, BF16),
         jnp.asarray(inverse_square, F32),
     )
+
+
+def chunk_row(tile, lead):
+    return CHUNK * ((tile - lead) % RING)
 
 
 def turn(value, shift):
@@ -185,7 +191,7 @@
             others = spread(jnp.where(north, turn(others, 64), others))
             edges = spread(jnp.where(north, turn(edges, 64), edges))
             for quarter in range(4):
-                place = CHUNK * (16 * name + 4 * level + quarter)
+                place = chunk_row(16 * name + 4 * level + quarter, LEAD_OUT)
                 chunks[place : place + ROWS] = turned[ROWS * quarter : ROWS * quarter + ROWS]
                 two = [
                     jnp.sum(
@@ -196,7 +202,7 @@
                 chunks[place + ROWS : place + CHUNK] = jnp.concatenate(two, axis=0).astype(BF16)
             if level % 2:
                 number = 2 * name + level // 2
-                span = pl.ds(PART * number, PART)
+                span = pl.ds(chunk_row(8 * number, LEAD_OUT), PART)
                 copy = pltpu.make_async_copy(chunks.at[span], out_hbm.at[span], left.at[number])
                 copy.start()
                 copies.append(copy)
@@ -296,7 +302,7 @@
     column = lanes(tile) + 1
     rows = []
     for t in range(RING):
-        start = CHUNK * (INV * t % RING)
+        start = chunk_row(INV * t % RING, LEAD_OUT)
         rows.append(in_ref[start : start + ROWS])
         pair[2 * t : 2 * t + 2] = in_ref[start + ROWS : start + CHUNK].astype(F32)
     for bit in range(5):
@@ -345,9 +351,10 @@
         rows = [jnp.where(picked, rows[(t + 2**bit) % RING], rows[t]) for t in range(RING)]
     for d in range(RING):
         place = 7 * d % RING
-        out_ref[CHUNK * d : CHUNK * d + ROWS] = rows[place]
+        start = chunk_row(d, LEAD_BACK)
+        out_ref[start : start + ROWS] = rows[place]
         last = jnp.broadcast_to(pair[place : place + 1], (2, 128))
-        out_ref[CHUNK * d + ROWS : CHUNK * d + CHUNK] = last.astype(BF16)
+        out_ref[start + ROWS : start + CHUNK] = last.astype(BF16)
 
 
 def filter_rows(chunks, square):
@@ -581,7 +588,7 @@
     here = (lanes(square) >= 64) == north
     for level in range(0, 4, 2):
         first = 16 * name + 4 * level
-        starts = [CHUNK * (first + place) for place in range(8)]
+        starts = [chunk_row(first + place, LEAD_BACK) for place in range(8)]
         both = jnp.concatenate([chunks_ref[a : a + ROWS].astype(F32) for a in starts], axis=0).T
         across = turn(both, 64)
         for second in range(2):
@@ -632,9 +639,12 @@
     return lax.ppermute(value, axis, pairs)
 
 
-def exchange(chunks):
+def exchange(chunks, lead):
     pairs = chunks.reshape(-1, 2, chunks.shape[1])
-    return lax.all_to_all(pairs, "lon", split_axis=0, concat_axis=0, tiled=True).reshape(chunks.shape)
+    order = [[(place + lead) % RING for place in range(RING)]]
+    return lax.all_to_all(
+        pairs, "lon", split_axis=0, concat_axis=0, axis_index_groups=order, tiled=True
+    ).reshape(chunks.shape)
 
 
 def local(adjoint, land, diffusivity, cutoff):
@@ -647,12 +657,15 @@
     fields = jnp.transpose(adjoint, (0, 2, 1, 3)).reshape(-1, shape[3])
     kappas = jnp.transpose(diffusivity, (1, 0, 2))
 
-    filtered = filter_rows(exchange(pack(fields, land, kappas)), square)
-    filtered, fields, land, kappas = lax.optimization_barrier((filtered, fields, land, kappas))
-    removed = exchange(filtered)
+    circles = exchange(pack(fields, land, kappas), LEAD_OUT)
     own_near, own_far, sides = edge(fields, land, kappas)
     far_side = swap(sides, "lat", 1)
     near_side = swap(sides, "lat", 0)
+    circles, near_side, far_side = lax.optimization_barrier((circles, near_side, far_side))
+
+    filtered = filter_rows(circles, square)
+    filtered, own_near, own_far = lax.optimization_barrier((filtered, own_near, own_far))
+    removed = exchange(filtered, LEAD_BACK)
     near = swap(own_near, "lon", 0)
     far = swap(own_far, "lon", 1)
     whole, flow, rim = stencil(fields, land, kappas, near_side, far_side)

time: 40.9 us -> 38.6 us (0.944)
  waiting for transfers between devices: 12.1 us -> 5.09 us
  starting transfers between devices: 19.5 us -> 24.2 us
    all_to_all x2, waiting for transfers between devices: 11 us -> 2.96 us  [exchange(): lax.all_to_all(pairs, 'lon', split_axis=0, concat_axis=0, axis_index_grou...]
    all_to_all x2, starting transfers between devices: 15.3 us -> 19.4 us  [exchange(): lax.all_to_all(pairs, 'lon', split_axis=0, concat_axis=0, axis_index_grou...]
    ppermute x4, waiting for transfers between devices: 1.12 us -> 2.13 us  [swap(): return lax.ppermute(value, axis, pairs)]
    ppermute x4, starting transfers between devices: 4.17 us -> 4.79 us  [swap(): return lax.ppermute(value, axis, pairs)]
  transfers between devices with their start and end apart: 6 -> 6, of which waited for: 3 -> 4; matrix products, arithmetic and copies ran while one was open for 0% -> 0% of each run, Pallas kernels for 7% -> 7%
where the time goes in v5:
time: 38.6 us; the launch traced here: 38.3 us
  starting transfers between devices  24.2 us (63%)
  Pallas kernels  8.69 us (23%)
  waiting for transfers between devices  5.09 us (13%)
    all_to_all x2, starting transfers between devices, exchange(): lax.all_to_all(pairs, 'lon', split_axis=0, concat_axis=0, axis_index_grou...  19.4 us
    ppermute x4, starting transfers between devices, swap(): return lax.ppermute(value, axis, pairs)  4.79 us
    all_to_all x2, waiting for transfers between devices, exchange(): lax.all_to_all(pairs, 'lon', split_axis=0, concat_axis=0, axis_index_grou...  2.96 us
    pallas_call x1, Pallas kernels, pack(): pl.pallas_call(pack_kernel, out_shape=jax.ShapeDtypeStruct((RING * CHUNK,...  2.85 us
    pallas_call x1, Pallas kernels, stencil(): pl.pallas_call(stencil_kernel, grid=(1,), out_shape=(jax.ShapeDtypeStruct...  2.16 us
    ppermute x4, waiting for transfers between devices, swap(): return lax.ppermute(value, axis, pairs)  2.13 us
    pallas_call x1, Pallas kernels, filter_rows(): pl.pallas_call(filter_kernel, out_shape=jax.ShapeDtypeStruct((RING * CHUN...  1.94 us
    pallas_call x1, Pallas kernels, remove(): pl.pallas_call(remove_kernel, out_shape=jax.ShapeDtypeStruct(whole.shape,...  1.25 us
  transfers between devices with their start and end apart: 6, of which 4 were waited for; matrix products, arithmetic and copies ran while one was open for 0% of the time, Pallas kernels for 7%

profile of v5, /device:TPU:1, one launch (start us, length us, event | category | flops | bytes accessed | tf_op | source)
XLA Modules:
  0.0 38.3 jit_solution(1767174618510681965)
XLA Ops:
  0.0 0.0 copy-start.2
  0.0 0.0 copy-start.1
  0.0 2.9 %pack.1 = bf16[576,128]{1,0:T(8,128)(2,1)} custom-call(f32[2160,128]{1,0:T(8,128)} %bitcast.11, s32[135,128]{1,0:T(8,128)} %land_ref.3, f32[135,2,128]{2,1,0:T(2,128)} %bitcast.14), custom_call_target="tpu_custom_call" | custom-call | tf_op jit(solution)/shard_map/pack/pallas_call | solution.py:214
  2.9 0.0 copy-start.6
  2.9 0.0 copy-start.3
  2.9 0.0 copy-start.4
  2.9 0.0 copy-start.5
  2.9 11.5 %all-to-all-start = ((bf16[288,2,128]{2,1,0:T(2,128)(2,1)}), bf16[288,2,128]{2,1,0:T(2,128)(2,1)S(1)}, u32[]{:S(2)}, u32[]{:S(2)}) async-start(bf16[288,2,128]{2,1,0:T(2,128)(2,1)} %bitcast.19), calls=%async_computation | async-start | bytes 294912 | tf_op jit(solution)/shard_map/all_to_all | solution.py:645
  14.4 0.0 copy-done.2
  14.4 0.0 copy-done.1
  14.4 0.0 copy-done
  14.4 0.5 %edge.1 = (f32[24,128]{1,0:T(8,128)S(1)}, f32[24,128]{1,0:T(8,128)S(1)}, f32[48,128]{1,0:T(8,128)S(1)}) custom-call(f32[2160,128]{1,0:T(8,128)S(1)} %bitcast.12, s32[135,128]{1,0:T(8,128)S(1)} %copy-done.2, f32[135,2,128]{2,1,0:T(2,128)S(1)} %bitcast.15), custom_call_target="tpu_custom_call" | custom-call | tf_op jit(solution)/shard_map/edge/pallas_call | solution.py:408
  14.9 0.7 %collective-permute-start.1 = (f32[48,128]{1,0:T(8,128)S(1)}, f32[48,128]{1,0:T(8,128)S(1)}, u32[]{:S(2)}, u32[]{:S(2)}) collective-permute-start(f32[48,128]{1,0:T(8,128)S(1)} %get-tuple-element.17), channel_id=1, source_target_pairs={{1,2},{2,1},{3,4},{4,3},{5,6},{6,5},{9,10},{10,9},{11,12},{12,11},... | collective-permute-start | bytes 73736 | tf_op jit(solution)/shard_map/ppermute | solution.py:639
  15.6 2.5 %collective-permute-start = (f32[48,128]{1,0:T(8,128)S(1)}, f32[48,128]{1,0:T(8,128)S(1)}, u32[]{:S(2)}, u32[]{:S(2)}) collective-permute-start(f32[48,128]{1,0:T(8,128)S(1)} %get-tuple-element.17), channel_id=1, source_target_pairs={{0,1},{1,0},{2,3},{3,2},{4,5},{5,4},{6,7},{7,6},{8,9},{9,8},{10,11... | collective-permute-start | bytes 73736 | tf_op jit(solution)/shard_map/ppermute | solution.py:639
  18.1 0.0 copy-done.6
  18.1 0.1 convert_multiply_fusion
  18.1 0.0 collective-permute-done.1.far_side_ref
  18.1 1.9 %collective-permute-done.near_side_ref = f32[48,128]{1,0:T(8,128)S(1)} collective-permute-done((f32[48,128]{1,0:T(8,128)S(1)}, f32[48,128]{1,0:T(8,128)S(1)}, u32[]{:S(2)}, u32[]{:S(2)}) %collective-permute-start) | collective-permute-done | bytes 24608 | tf_op jit(solution)/shard_map/ppermute | solution.py:639
  20.0 1.3 %all-to-all-done = bf16[288,2,128]{2,1,0:T(2,128)(2,1)S(1)} async-done(((bf16[288,2,128]{2,1,0:T(2,128)(2,1)}), bf16[288,2,128]{2,1,0:T(2,128)(2,1)S(1)}, u32[]{:S(2)}, u32[]{:S(2)}) %all-to-all-start) | async-done | bytes 147488 | tf_op jit(solution)/shard_map/all_to_all | solution.py:645
  21.4 0.1 broadcast_in_dim.2.refs_1_
  21.4 0.0 copy-done.3
  21.4 0.0 copy-done.4
  21.4 0.0 copy-done.5
  21.4 1.9 %filter.1 = bf16[576,128]{1,0:T(8,128)(2,1)} custom-call(bf16[576,128]{1,0:T(8,128)(2,1)S(1)} %bitcast.18, f32[16,128]{1,0:T(8,128)S(1)} %broadcast_in_dim.2.refs_1_, bf16[256,256]{1,0:T(8,128)(2,1)S(1)} %copy-done.4, bf16[256,256]{1,0:T(8,128)(2,1)S(1)} %copy-done.3, f32[32,128]{1,0:T(8,128)S(1)} %copy-done.5), custom_call_target="tpu_custom_call" | custom-call | tf_op jit(solution)/shard_map/filter/pallas_call | solution.py:362
  23.4 8.0 %all-to-all-start.1 = ((bf16[288,2,128]{2,1,0:T(2,128)(2,1)}), bf16[288,2,128]{2,1,0:T(2,128)(2,1)S(1)}, u32[]{:S(2)}, u32[]{:S(2)}) async-start(bf16[288,2,128]{2,1,0:T(2,128)(2,1)} %bitcast.6), calls=%async_computation.1 | async-start | bytes 294912 | tf_op jit(solution)/shard_map/all_to_all | solution.py:645
  31.3 0.4 %collective-permute-start.2 = (f32[24,128]{1,0:T(8,128)S(1)}, f32[24,128]{1,0:T(8,128)S(1)}, u32[]{:S(2)}, u32[]{:S(2)}) collective-permute-start(f32[24,128]{1,0:T(8,128)S(1)} %get-tuple-element.26.own_near_ref), channel_id=1, source_target_pairs={{0,8},{8,0},{16,24},{24,16},{32,40},{40,32},{48,56},{56,48},{64,72... | collective-permute-start | bytes 36872 | tf_op jit(solution)/shard_map/ppermute | solution.py:639
  31.8 1.2 %collective-permute-start.3 = (f32[24,128]{1,0:T(8,128)S(1)}, f32[24,128]{1,0:T(8,128)S(1)}, u32[]{:S(2)}, u32[]{:S(2)}) collective-permute-start(f32[24,128]{1,0:T(8,128)S(1)} %get-tuple-element.27.own_far_ref), channel_id=1, source_target_pairs={{8,16},{16,8},{24,32},{32,24},{40,48},{48,40},{56,64},{64,56},{72,... | collective-permute-start | bytes 36872 | tf_op jit(solution)/shard_map/ppermute | solution.py:639
  33.0 2.2 %stencil.1 = (f32[2160,128]{1,0:T(8,128)}, f32[1080,128]{1,0:T(8,128)S(1)}, f32[24,128]{1,0:T(8,128)S(1)}) custom-call(f32[2160,128]{1,0:T(8,128)S(1)} %bitcast.13, s32[135,128]{1,0:T(8,128)S(1)} %copy-done.2, f32[135,2,128]{2,1,0:T(2,128)S(1)} %bitcast.16, f32[48,128]{1,0:T(8,128)S(1)} %collective-permute-done.near_side_ref, ...), custom_call_target="tpu_custom_call" | custom-call | tf_op jit(solution)/shard_map/stencil/pallas_call | solution.py:487
  35.2 0.0 collective-permute-done.2.near_ref
  35.2 0.3 collective-permute-done.3.far_ref
  35.4 1.6 %all-to-all-done.1 = bf16[288,2,128]{2,1,0:T(2,128)(2,1)S(1)} async-done(((bf16[288,2,128]{2,1,0:T(2,128)(2,1)}), bf16[288,2,128]{2,1,0:T(2,128)(2,1)S(1)}, u32[]{:S(2)}, u32[]{:S(2)}) %all-to-all-start.1) | async-done | bytes 147488 | tf_op jit(solution)/shard_map/all_to_all | solution.py:645
  37.1 1.3 %remove.1 = f32[2160,128]{1,0:T(8,128)} custom-call(bf16[576,128]{1,0:T(8,128)(2,1)S(1)} %bitcast.17, f32[1080,128]{1,0:T(8,128)S(1)} %get-tuple-element.24.flow_ref, f32[24,128]{1,0:T(8,128)S(1)} %get-tuple-element.25.rim_ref, f32[24,128]{1,0:T(8,128)S(1)} %get-tuple-element.26.own_near_ref, ...), custom_call_target="tpu_custom_call", output_to_operand_aliasing={{}: (7, {})} | custom-call | tf_op jit(solution)/shard_map/remove/pallas_call | solution.py:612
  (1 shorter events, 0.0 us)
Async XLA Ops:
  0.0 14.4 %copy-start.2 = (s32[135,128]{1,0:T(8,128)S(1)}, s32[135,128]{1,0:T(8,128)}, u32[]{:S(2)}) copy-start(s32[135,128]{1,0:T(8,128)} %land_ref.3) | copy-start | bytes 207364
  0.0 14.4 %copy-start.1 = (f32[2,135,128]{2,0,1:T(2,128)S(1)}, f32[2,135,128]{2,0,1:T(2,128)}, u32[]{:S(2)}) copy-start(f32[2,135,128]{2,0,1:T(2,128)} %param.9) | copy-start | bytes 414724
  0.0 14.4 %copy-start = (f32[4,4,135,128]{3,1,2,0:T(4,128)S(1)}, f32[4,4,135,128]{3,1,2,0:T(4,128)}, u32[]{:S(2)}) copy-start(f32[4,4,135,128]{3,1,2,0:T(4,128)} %param.7) | copy-start | bytes 3317764
  2.9 15.2 %copy-start.6 = (s32[128]{0:T(128)S(1)}, s32[128]{0:T(128)}, u32[]{:S(2)}) copy-start(s32[128]{0:T(128)} %param.10) | copy-start | bytes 1540
  2.9 18.5 %copy-start.3 = (bf16[256,256]{1,0:T(8,128)(2,1)S(1)}, bf16[256,256]{1,0:T(8,128)(2,1)}, u32[]{:S(2)}) copy-start(bf16[256,256]{1,0:T(8,128)(2,1)} %constant.38.clone.refs_3_) | copy-start | bytes 393220
  2.9 18.5 %copy-start.4 = (bf16[256,256]{1,0:T(8,128)(2,1)S(1)}, bf16[256,256]{1,0:T(8,128)(2,1)}, u32[]{:S(2)}) copy-start(bf16[256,256]{1,0:T(8,128)(2,1)} %constant.37.clone.refs_2_) | copy-start | bytes 393220
  2.9 18.5 %copy-start.5 = (f32[32,128]{1,0:T(8,128)S(1)}, f32[32,128]{1,0:T(8,128)}, u32[]{:S(2)}) copy-start(f32[32,128]{1,0:T(8,128)} %constant.39.clone.refs_4_) | copy-start | bytes 49156
  2.9 18.4 %all-to-all-start = ((bf16[288,2,128]{2,1,0:T(2,128)(2,1)}), bf16[288,2,128]{2,1,0:T(2,128)(2,1)S(1)}, u32[]{:S(2)}, u32[]{:S(2)}) async-start(bf16[288,2,128]{2,1,0:T(2,128)(2,1)} %bitcast.19), calls=%async_computation | async-start | bytes 294912 | tf_op jit(solution)/shard_map/all_to_all | solution.py:645
  14.9 3.2 %collective-permute-start.1 = (f32[48,128]{1,0:T(8,128)S(1)}, f32[48,128]{1,0:T(8,128)S(1)}, u32[]{:S(2)}, u32[]{:S(2)}) collective-permute-start(f32[48,128]{1,0:T(8,128)S(1)} %get-tuple-element.17), channel_id=1, source_target_pairs={{1,2},{2,1},{3,4},{4,3},{5,6},{6,5},{9,10},{10,9},{11,12},{12,11},... | collective-permute-start | bytes 73736 | tf_op jit(solution)/shard_map/ppermute | solution.py:639
  15.6 4.4 %collective-permute-start = (f32[48,128]{1,0:T(8,128)S(1)}, f32[48,128]{1,0:T(8,128)S(1)}, u32[]{:S(2)}, u32[]{:S(2)}) collective-permute-start(f32[48,128]{1,0:T(8,128)S(1)} %get-tuple-element.17), channel_id=1, source_target_pairs={{0,1},{1,0},{2,3},{3,2},{4,5},{5,4},{6,7},{7,6},{8,9},{9,8},{10,11... | collective-permute-start | bytes 73736 | tf_op jit(solution)/shard_map/ppermute | solution.py:639
  23.4 13.7 %all-to-all-start.1 = ((bf16[288,2,128]{2,1,0:T(2,128)(2,1)}), bf16[288,2,128]{2,1,0:T(2,128)(2,1)S(1)}, u32[]{:S(2)}, u32[]{:S(2)}) async-start(bf16[288,2,128]{2,1,0:T(2,128)(2,1)} %bitcast.6), calls=%async_computation.1 | async-start | bytes 294912 | tf_op jit(solution)/shard_map/all_to_all | solution.py:645
  31.3 3.8 %collective-permute-start.2 = (f32[24,128]{1,0:T(8,128)S(1)}, f32[24,128]{1,0:T(8,128)S(1)}, u32[]{:S(2)}, u32[]{:S(2)}) collective-permute-start(f32[24,128]{1,0:T(8,128)S(1)} %get-tuple-element.26.own_near_ref), channel_id=1, source_target_pairs={{0,8},{8,0},{16,24},{24,16},{32,40},{40,32},{48,56},{56,48},{64,72... | collective-permute-start | bytes 36872 | tf_op jit(solution)/shard_map/ppermute | solution.py:639
  31.8 3.6 %collective-permute-start.3 = (f32[24,128]{1,0:T(8,128)S(1)}, f32[24,128]{1,0:T(8,128)S(1)}, u32[]{:S(2)}, u32[]{:S(2)}) collective-permute-start(f32[24,128]{1,0:T(8,128)S(1)} %get-tuple-element.27.own_far_ref), channel_id=1, source_target_pairs={{8,16},{16,8},{24,32},{32,24},{40,48},{48,40},{56,64},{64,56},{72,... | collective-permute-start | bytes 36872 | tf_op jit(solution)/shard_map/ppermute | solution.py:639

commit v6 on v5

--- a/solution.py
+++ b/solution.py
@@ -19,8 +19,8 @@
 INV = 23
 CRT_RING = 3105
 CRT_COLS = 1216
-LEAD_OUT = 24
-LEAD_BACK = 16
+ORDER_OUT = [(place + 24) % RING for place in range(RING)]
+ORDER_BACK = [16] + [tile for tile in reversed(range(RING)) if tile != 16]
 WAVES = 68
 ROWS = 16
 LEVELS = 4
@@ -66,8 +66,8 @@
     )
 
 
-def chunk_row(tile, lead):
-    return CHUNK * ((tile - lead) % RING)
+def chunk_row(tile, order):
+    return CHUNK * order.index(tile)
 
 
 def turn(value, shift):
@@ -191,7 +191,7 @@
             others = spread(jnp.where(north, turn(others, 64), others))
             edges = spread(jnp.where(north, turn(edges, 64), edges))
             for quarter in range(4):
-                place = chunk_row(16 * name + 4 * level + quarter, LEAD_OUT)
+                place = chunk_row(16 * name + 4 * level + quarter, ORDER_OUT)
                 chunks[place : place + ROWS] = turned[ROWS * quarter : ROWS * quarter + ROWS]
                 two = [
                     jnp.sum(
@@ -202,7 +202,7 @@
                 chunks[place + ROWS : place + CHUNK] = jnp.concatenate(two, axis=0).astype(BF16)
             if level % 2:
                 number = 2 * name + level // 2
-                span = pl.ds(chunk_row(8 * number, LEAD_OUT), PART)
+                span = pl.ds(chunk_row(8 * number, ORDER_OUT), PART)
                 copy = pltpu.make_async_copy(chunks.at[span], out_hbm.at[span], left.at[number])
                 copy.start()
                 copies.append(copy)
@@ -302,7 +302,7 @@
     column = lanes(tile) + 1
     rows = []
     for t in range(RING):
-        start = chunk_row(INV * t % RING, LEAD_OUT)
+        start = chunk_row(INV * t % RING, ORDER_OUT)
         rows.append(in_ref[start : start + ROWS])
         pair[2 * t : 2 * t + 2] = in_ref[start + ROWS : start + CHUNK].astype(F32)
     for bit in range(5):
@@ -351,7 +351,7 @@
         rows = [jnp.where(picked, rows[(t + 2**bit) % RING], rows[t]) for t in range(RING)]
     for d in range(RING):
         place = 7 * d % RING
-        start = chunk_row(d, LEAD_BACK)
+        start = chunk_row(d, ORDER_BACK)
         out_ref[start : start + ROWS] = rows[place]
         last = jnp.broadcast_to(pair[place : place + 1], (2, 128))
         out_ref[start + ROWS : start + CHUNK] = last.astype(BF16)
@@ -530,8 +530,8 @@
     rim_ref,
     own_near_ref,
     own_far_ref,
+    far_ref,
     near_ref,
-    far_ref,
     whole_ref,
     out_ref,
     new_flow,
@@ -588,7 +588,7 @@
     here = (lanes(square) >= 64) == north
     for level in range(0, 4, 2):
         first = 16 * name + 4 * level
-        starts = [chunk_row(first + place, LEAD_BACK) for place in range(8)]
+        starts = [chunk_row(first + place, ORDER_BACK) for place in range(8)]
         both = jnp.concatenate([chunks_ref[a : a + ROWS].astype(F32) for a in starts], axis=0).T
         across = turn(both, 64)
         for second in range(2):
@@ -608,7 +608,7 @@
             out_ref[rows_of] = flow_ref[rows_of] - high[place, 0:COLS]
 
 
-def remove(chunks, flow, rim, own_near, own_far, near, far, whole):
+def remove(chunks, flow, rim, own_near, own_far, far, near, whole):
     return pl.pallas_call(
         remove_kernel,
         out_shape=jax.ShapeDtypeStruct(whole.shape, F32),
@@ -623,7 +623,7 @@
         input_output_aliases={7: 0},
         compiler_params=pltpu.CompilerParams(vmem_limit_bytes=24 * 2**20),
         name="remove",
-    )(chunks, flow, rim, own_near, own_far, near, far, whole)
+    )(chunks, flow, rim, own_near, own_far, far, near, whole)
 
 
 def swap(value, axis, first):
@@ -639,11 +639,10 @@
     return lax.ppermute(value, axis, pairs)
 
 
-def exchange(chunks, lead):
+def exchange(chunks, order):
     pairs = chunks.reshape(-1, 2, chunks.shape[1])
-    order = [[(place + lead) % RING for place in range(RING)]]
     return lax.all_to_all(
-        pairs, "lon", split_axis=0, concat_axis=0, axis_index_groups=order, tiled=True
+        pairs, "lon", split_axis=0, concat_axis=0, axis_index_groups=[order], tiled=True
     ).reshape(chunks.shape)
 
 
@@ -657,7 +656,7 @@
     fields = jnp.transpose(adjoint, (0, 2, 1, 3)).reshape(-1, shape[3])
     kappas = jnp.transpose(diffusivity, (1, 0, 2))
 
-    circles = exchange(pack(fields, land, kappas), LEAD_OUT)
+    circles = exchange(pack(fields, land, kappas), ORDER_OUT)
     own_near, own_far, sides = edge(fields, land, kappas)
     far_side = swap(sides, "lat", 1)
     near_side = swap(sides, "lat", 0)
@@ -665,12 +664,12 @@
 
     filtered = filter_rows(circles, square)
     filtered, own_near, own_far = lax.optimization_barrier((filtered, own_near, own_far))
-    removed = exchange(filtered, LEAD_BACK)
+    removed = exchange(filtered, ORDER_BACK)
+    far = swap(own_far, "lon", 1)
     near = swap(own_near, "lon", 0)
-    far = swap(own_far, "lon", 1)
     whole, flow, rim = stencil(fields, land, kappas, near_side, far_side)
 
-    out = remove(removed, flow, rim, own_near, own_far, near, far, whole)
+    out = remove(removed, flow, rim, own_near, own_far, far, near, whole)
     return jnp.transpose(out.reshape(shape[0], shape[2], shape[1], shape[3]), (0, 2, 1, 3))
 
 

time: 38.6 us -> 38.1 us (0.987)
  waiting for transfers between devices: 5.09 us -> 4.57 us
    all_to_all x2, waiting for transfers between devices: 2.96 us -> 2.56 us  [exchange(): lax.all_to_all(pairs, 'lon', split_axis=0, concat_axis=0, axis_index_grou...]
where the time goes in v6:
time: 38.1 us; the launch traced here: 37.8 us
  starting transfers between devices  24.3 us (64%)
  Pallas kernels  8.69 us (23%)
  waiting for transfers between devices  4.57 us (12%)
    all_to_all x2, starting transfers between devices, exchange(): lax.all_to_all(pairs, 'lon', split_axis=0, concat_axis=0, axis_index_grou...  19.5 us
    ppermute x4, starting transfers between devices, swap(): return lax.ppermute(value, axis, pairs)  4.79 us
    pallas_call x1, Pallas kernels, pack(): pl.pallas_call(pack_kernel, out_shape=jax.ShapeDtypeStruct((RING * CHUNK,...  2.85 us
    all_to_all x2, waiting for transfers between devices, exchange(): lax.all_to_all(pairs, 'lon', split_axis=0, concat_axis=0, axis_index_grou...  2.56 us
    pallas_call x1, Pallas kernels, stencil(): pl.pallas_call(stencil_kernel, grid=(1,), out_shape=(jax.ShapeDtypeStruct...  2.16 us
    ppermute x4, waiting for transfers between devices, swap(): return lax.ppermute(value, axis, pairs)  2.01 us
    pallas_call x1, Pallas kernels, filter_rows(): pl.pallas_call(filter_kernel, out_shape=jax.ShapeDtypeStruct((RING * CHUN...  1.94 us
    pallas_call x1, Pallas kernels, remove(): pl.pallas_call(remove_kernel, out_shape=jax.ShapeDtypeStruct(whole.shape,...  1.25 us
  transfers between devices with their start and end apart: 6, of which 4 were waited for; matrix products, arithmetic and copies ran while one was open for 0% of the time, Pallas kernels for 7%

profile of v6, /device:TPU:1, one launch (start us, length us, event | category | flops | bytes accessed | tf_op | source)
XLA Modules:
  0.0 37.8 jit_solution(6614535116965183577)
XLA Ops:
  0.0 0.0 copy-start.2
  0.0 0.0 copy-start.1
  0.0 2.9 %pack.1 = bf16[576,128]{1,0:T(8,128)(2,1)} custom-call(f32[2160,128]{1,0:T(8,128)} %bitcast.11, s32[135,128]{1,0:T(8,128)} %land_ref.3, f32[135,2,128]{2,1,0:T(2,128)} %bitcast.14), custom_call_target="tpu_custom_call" | custom-call | tf_op jit(solution)/shard_map/pack/pallas_call | solution.py:214
  2.9 0.0 copy-start.6
  2.9 0.0 copy-start.3
  2.9 0.0 copy-start.4
  2.9 0.0 copy-start.5
  2.9 11.5 %all-to-all-start = ((bf16[288,2,128]{2,1,0:T(2,128)(2,1)}), bf16[288,2,128]{2,1,0:T(2,128)(2,1)S(1)}, u32[]{:S(2)}, u32[]{:S(2)}) async-start(bf16[288,2,128]{2,1,0:T(2,128)(2,1)} %bitcast.19), calls=%async_computation | async-start | bytes 294912 | tf_op jit(solution)/shard_map/all_to_all | solution.py:644
  14.4 0.0 copy-done.2
  14.4 0.0 copy-done.1
  14.4 0.0 copy-done
  14.4 0.5 %edge.1 = (f32[24,128]{1,0:T(8,128)S(1)}, f32[24,128]{1,0:T(8,128)S(1)}, f32[48,128]{1,0:T(8,128)S(1)}) custom-call(f32[2160,128]{1,0:T(8,128)S(1)} %bitcast.12, s32[135,128]{1,0:T(8,128)S(1)} %copy-done.2, f32[135,2,128]{2,1,0:T(2,128)S(1)} %bitcast.15), custom_call_target="tpu_custom_call" | custom-call | tf_op jit(solution)/shard_map/edge/pallas_call | solution.py:408
  14.9 0.7 %collective-permute-start.1 = (f32[48,128]{1,0:T(8,128)S(1)}, f32[48,128]{1,0:T(8,128)S(1)}, u32[]{:S(2)}, u32[]{:S(2)}) collective-permute-start(f32[48,128]{1,0:T(8,128)S(1)} %get-tuple-element.17), channel_id=1, source_target_pairs={{1,2},{2,1},{3,4},{4,3},{5,6},{6,5},{9,10},{10,9},{11,12},{12,11},... | collective-permute-start | bytes 73736 | tf_op jit(solution)/shard_map/ppermute | solution.py:639
  15.6 2.5 %collective-permute-start = (f32[48,128]{1,0:T(8,128)S(1)}, f32[48,128]{1,0:T(8,128)S(1)}, u32[]{:S(2)}, u32[]{:S(2)}) collective-permute-start(f32[48,128]{1,0:T(8,128)S(1)} %get-tuple-element.17), channel_id=1, source_target_pairs={{0,1},{1,0},{2,3},{3,2},{4,5},{5,4},{6,7},{7,6},{8,9},{9,8},{10,11... | collective-permute-start | bytes 73736 | tf_op jit(solution)/shard_map/ppermute | solution.py:639
  18.1 0.0 copy-done.6
  18.1 0.1 convert_multiply_fusion
  18.1 0.0 collective-permute-done.1.far_side_ref
  18.1 1.9 %collective-permute-done.near_side_ref = f32[48,128]{1,0:T(8,128)S(1)} collective-permute-done((f32[48,128]{1,0:T(8,128)S(1)}, f32[48,128]{1,0:T(8,128)S(1)}, u32[]{:S(2)}, u32[]{:S(2)}) %collective-permute-start) | collective-permute-done | bytes 24608 | tf_op jit(solution)/shard_map/ppermute | solution.py:639
  20.0 1.3 %all-to-all-done = bf16[288,2,128]{2,1,0:T(2,128)(2,1)S(1)} async-done(((bf16[288,2,128]{2,1,0:T(2,128)(2,1)}), bf16[288,2,128]{2,1,0:T(2,128)(2,1)S(1)}, u32[]{:S(2)}, u32[]{:S(2)}) %all-to-all-start) | async-done | bytes 147488 | tf_op jit(solution)/shard_map/all_to_all | solution.py:644
  21.4 0.1 broadcast_in_dim.2.refs_1_
  21.4 0.0 copy-done.3
  21.4 0.0 copy-done.4
  21.4 0.0 copy-done.5
  21.4 1.9 %filter.1 = bf16[576,128]{1,0:T(8,128)(2,1)} custom-call(bf16[576,128]{1,0:T(8,128)(2,1)S(1)} %bitcast.18, f32[16,128]{1,0:T(8,128)S(1)} %broadcast_in_dim.2.refs_1_, bf16[256,256]{1,0:T(8,128)(2,1)S(1)} %copy-done.4, bf16[256,256]{1,0:T(8,128)(2,1)S(1)} %copy-done.3, f32[32,128]{1,0:T(8,128)S(1)} %copy-done.5), custom_call_target="tpu_custom_call" | custom-call | tf_op jit(solution)/shard_map/filter/pallas_call | solution.py:362
  23.4 8.0 %all-to-all-start.1 = ((bf16[288,2,128]{2,1,0:T(2,128)(2,1)}), bf16[288,2,128]{2,1,0:T(2,128)(2,1)S(1)}, u32[]{:S(2)}, u32[]{:S(2)}) async-start(bf16[288,2,128]{2,1,0:T(2,128)(2,1)} %bitcast.6), calls=%async_computation.1 | async-start | bytes 294912 | tf_op jit(solution)/shard_map/all_to_all | solution.py:644
  31.4 0.5 %collective-permute-start.3 = (f32[24,128]{1,0:T(8,128)S(1)}, f32[24,128]{1,0:T(8,128)S(1)}, u32[]{:S(2)}, u32[]{:S(2)}) collective-permute-start(f32[24,128]{1,0:T(8,128)S(1)} %get-tuple-element.26.own_near_ref), channel_id=1, source_target_pairs={{0,8},{8,0},{16,24},{24,16},{32,40},{40,32},{48,56},{56,48},{64,72... | collective-permute-start | bytes 36872 | tf_op jit(solution)/shard_map/ppermute | solution.py:639
  31.9 1.2 %collective-permute-start.2 = (f32[24,128]{1,0:T(8,128)S(1)}, f32[24,128]{1,0:T(8,128)S(1)}, u32[]{:S(2)}, u32[]{:S(2)}) collective-permute-start(f32[24,128]{1,0:T(8,128)S(1)} %get-tuple-element.27.own_far_ref), channel_id=1, source_target_pairs={{8,16},{16,8},{24,32},{32,24},{40,48},{48,40},{56,64},{64,56},{72,... | collective-permute-start | bytes 36872 | tf_op jit(solution)/shard_map/ppermute | solution.py:639
  33.1 2.2 %stencil.1 = (f32[2160,128]{1,0:T(8,128)}, f32[1080,128]{1,0:T(8,128)S(1)}, f32[24,128]{1,0:T(8,128)S(1)}) custom-call(f32[2160,128]{1,0:T(8,128)S(1)} %bitcast.13, s32[135,128]{1,0:T(8,128)S(1)} %copy-done.2, f32[135,2,128]{2,1,0:T(2,128)S(1)} %bitcast.16, f32[48,128]{1,0:T(8,128)S(1)} %collective-permute-done.near_side_ref, ...), custom_call_target="tpu_custom_call" | custom-call | tf_op jit(solution)/shard_map/stencil/pallas_call | solution.py:487
  35.2 0.0 collective-permute-done.3.near_ref
  35.2 0.1 collective-permute-done.2.far_ref
  35.4 1.2 %all-to-all-done.1 = bf16[288,2,128]{2,1,0:T(2,128)(2,1)S(1)} async-done(((bf16[288,2,128]{2,1,0:T(2,128)(2,1)}), bf16[288,2,128]{2,1,0:T(2,128)(2,1)S(1)}, u32[]{:S(2)}, u32[]{:S(2)}) %all-to-all-start.1) | async-done | bytes 147488 | tf_op jit(solution)/shard_map/all_to_all | solution.py:644
  36.6 1.3 %remove.1 = f32[2160,128]{1,0:T(8,128)} custom-call(bf16[576,128]{1,0:T(8,128)(2,1)S(1)} %bitcast.17, f32[1080,128]{1,0:T(8,128)S(1)} %get-tuple-element.24.flow_ref, f32[24,128]{1,0:T(8,128)S(1)} %get-tuple-element.25.rim_ref, f32[24,128]{1,0:T(8,128)S(1)} %get-tuple-element.26.own_near_ref, ...), custom_call_target="tpu_custom_call", output_to_operand_aliasing={{}: (7, {})} | custom-call | tf_op jit(solution)/shard_map/remove/pallas_call | solution.py:612
  (1 shorter events, 0.0 us)
Async XLA Ops:
  0.0 14.4 %copy-start.2 = (s32[135,128]{1,0:T(8,128)S(1)}, s32[135,128]{1,0:T(8,128)}, u32[]{:S(2)}) copy-start(s32[135,128]{1,0:T(8,128)} %land_ref.3) | copy-start | bytes 207364
  0.0 14.4 %copy-start.1 = (f32[2,135,128]{2,0,1:T(2,128)S(1)}, f32[2,135,128]{2,0,1:T(2,128)}, u32[]{:S(2)}) copy-start(f32[2,135,128]{2,0,1:T(2,128)} %param.9) | copy-start | bytes 414724
  0.0 14.4 %copy-start = (f32[4,4,135,128]{3,1,2,0:T(4,128)S(1)}, f32[4,4,135,128]{3,1,2,0:T(4,128)}, u32[]{:S(2)}) copy-start(f32[4,4,135,128]{3,1,2,0:T(4,128)} %param.7) | copy-start | bytes 3317764
  2.9 15.2 %copy-start.6 = (s32[128]{0:T(128)S(1)}, s32[128]{0:T(128)}, u32[]{:S(2)}) copy-start(s32[128]{0:T(128)} %param.10) | copy-start | bytes 1540
  2.9 18.5 %copy-start.3 = (bf16[256,256]{1,0:T(8,128)(2,1)S(1)}, bf16[256,256]{1,0:T(8,128)(2,1)}, u32[]{:S(2)}) copy-start(bf16[256,256]{1,0:T(8,128)(2,1)} %constant.38.clone.refs_3_) | copy-start | bytes 393220
  2.9 18.5 %copy-start.4 = (bf16[256,256]{1,0:T(8,128)(2,1)S(1)}, bf16[256,256]{1,0:T(8,128)(2,1)}, u32[]{:S(2)}) copy-start(bf16[256,256]{1,0:T(8,128)(2,1)} %constant.37.clone.refs_2_) | copy-start | bytes 393220
  2.9 18.5 %copy-start.5 = (f32[32,128]{1,0:T(8,128)S(1)}, f32[32,128]{1,0:T(8,128)}, u32[]{:S(2)}) copy-start(f32[32,128]{1,0:T(8,128)} %constant.39.clone.refs_4_) | copy-start | bytes 49156
  2.9 18.4 %all-to-all-start = ((bf16[288,2,128]{2,1,0:T(2,128)(2,1)}), bf16[288,2,128]{2,1,0:T(2,128)(2,1)S(1)}, u32[]{:S(2)}, u32[]{:S(2)}) async-start(bf16[288,2,128]{2,1,0:T(2,128)(2,1)} %bitcast.19), calls=%async_computation | async-start | bytes 294912 | tf_op jit(solution)/shard_map/all_to_all | solution.py:644
  14.9 3.2 %collective-permute-start.1 = (f32[48,128]{1,0:T(8,128)S(1)}, f32[48,128]{1,0:T(8,128)S(1)}, u32[]{:S(2)}, u32[]{:S(2)}) collective-permute-start(f32[48,128]{1,0:T(8,128)S(1)} %get-tuple-element.17), channel_id=1, source_target_pairs={{1,2},{2,1},{3,4},{4,3},{5,6},{6,5},{9,10},{10,9},{11,12},{12,11},... | collective-permute-start | bytes 73736 | tf_op jit(solution)/shard_map/ppermute | solution.py:639
  15.6 4.4 %collective-permute-start = (f32[48,128]{1,0:T(8,128)S(1)}, f32[48,128]{1,0:T(8,128)S(1)}, u32[]{:S(2)}, u32[]{:S(2)}) collective-permute-start(f32[48,128]{1,0:T(8,128)S(1)} %get-tuple-element.17), channel_id=1, source_target_pairs={{0,1},{1,0},{2,3},{3,2},{4,5},{5,4},{6,7},{7,6},{8,9},{9,8},{10,11... | collective-permute-start | bytes 73736 | tf_op jit(solution)/shard_map/ppermute | solution.py:639
  23.4 13.2 %all-to-all-start.1 = ((bf16[288,2,128]{2,1,0:T(2,128)(2,1)}), bf16[288,2,128]{2,1,0:T(2,128)(2,1)S(1)}, u32[]{:S(2)}, u32[]{:S(2)}) async-start(bf16[288,2,128]{2,1,0:T(2,128)(2,1)} %bitcast.6), calls=%async_computation.1 | async-start | bytes 294912 | tf_op jit(solution)/shard_map/all_to_all | solution.py:644
  31.4 3.8 %collective-permute-start.3 = (f32[24,128]{1,0:T(8,128)S(1)}, f32[24,128]{1,0:T(8,128)S(1)}, u32[]{:S(2)}, u32[]{:S(2)}) collective-permute-start(f32[24,128]{1,0:T(8,128)S(1)} %get-tuple-element.26.own_near_ref), channel_id=1, source_target_pairs={{0,8},{8,0},{16,24},{24,16},{32,40},{40,32},{48,56},{56,48},{64,72... | collective-permute-start | bytes 36872 | tf_op jit(solution)/shard_map/ppermute | solution.py:639
  31.9 3.5 %collective-permute-start.2 = (f32[24,128]{1,0:T(8,128)S(1)}, f32[24,128]{1,0:T(8,128)S(1)}, u32[]{:S(2)}, u32[]{:S(2)}) collective-permute-start(f32[24,128]{1,0:T(8,128)S(1)} %get-tuple-element.27.own_far_ref), channel_id=1, source_target_pairs={{8,16},{16,8},{24,32},{32,24},{40,48},{48,40},{56,64},{64,56},{72,... | collective-permute-start | bytes 36872 | tf_op jit(solution)/shard_map/ppermute | solution.py:639

commit v7 on v6

--- a/solution.py
+++ b/solution.py
@@ -19,8 +19,8 @@
 INV = 23
 CRT_RING = 3105
 CRT_COLS = 1216
-ORDER_OUT = [(place + 24) % RING for place in range(RING)]
-ORDER_BACK = [16] + [tile for tile in reversed(range(RING)) if tile != 16]
+ORDER_OUT = [((place + 24) % RING) ^ 1 for place in range(RING)]
+ORDER_BACK = [17] + [tile for tile in reversed(range(RING)) if tile != 17]
 WAVES = 68
 ROWS = 16
 LEVELS = 4
@@ -202,7 +202,7 @@
                 chunks[place + ROWS : place + CHUNK] = jnp.concatenate(two, axis=0).astype(BF16)
             if level % 2:
                 number = 2 * name + level // 2
-                span = pl.ds(chunk_row(8 * number, ORDER_OUT), PART)
+                span = pl.ds(PART * (ORDER_OUT.index(8 * number) // 8), PART)
                 copy = pltpu.make_async_copy(chunks.at[span], out_hbm.at[span], left.at[number])
                 copy.start()
                 copies.append(copy)

time: 38.1 us -> 37.6 us (0.987)
  starting transfers between devices: 24.3 us -> 23.6 us
    all_to_all x2, starting transfers between devices: 19.5 us -> 18.8 us  [exchange(): lax.all_to_all(pairs, 'lon', split_axis=0, concat_axis=0, axis_index_grou...]
where the time goes in v7:
time: 37.6 us; the launch traced here: 37.3 us
  starting transfers between devices  23.6 us (63%)
  Pallas kernels  8.69 us (23%)
  waiting for transfers between devices  4.75 us (13%)
    all_to_all x2, starting transfers between devices, exchange(): lax.all_to_all(pairs, 'lon', split_axis=0, concat_axis=0, axis_index_grou...  18.8 us
    ppermute x4, starting transfers between devices, swap(): return lax.ppermute(value, axis, pairs)  4.8 us
    pallas_call x1, Pallas kernels, pack(): pl.pallas_call(pack_kernel, out_shape=jax.ShapeDtypeStruct((RING * CHUNK,...  2.85 us
    all_to_all x2, waiting for transfers between devices, exchange(): lax.all_to_all(pairs, 'lon', split_axis=0, concat_axis=0, axis_index_grou...  2.74 us
    pallas_call x1, Pallas kernels, stencil(): pl.pallas_call(stencil_kernel, grid=(1,), out_shape=(jax.ShapeDtypeStruct...  2.16 us
    ppermute x4, waiting for transfers between devices, swap(): return lax.ppermute(value, axis, pairs)  2.01 us
    pallas_call x1, Pallas kernels, filter_rows(): pl.pallas_call(filter_kernel, out_shape=jax.ShapeDtypeStruct((RING * CHUN...  1.95 us
    pallas_call x1, Pallas kernels, remove(): pl.pallas_call(remove_kernel, out_shape=jax.ShapeDtypeStruct(whole.shape,...  1.25 us
  transfers between devices with their start and end apart: 6, of which 4 were waited for; matrix products, arithmetic and copies ran while one was open for 0% of the time, Pallas kernels for 7%

profile of v7, /device:TPU:1, one launch (start us, length us, event | category | flops | bytes accessed | tf_op | source)
XLA Modules:
  0.0 37.3 jit_solution(5206236152678722148)
XLA Ops:
  0.0 0.0 copy-start.2
  0.0 0.0 copy-start.1
  0.0 2.9 %pack.1 = bf16[576,128]{1,0:T(8,128)(2,1)} custom-call(f32[2160,128]{1,0:T(8,128)} %bitcast.11, s32[135,128]{1,0:T(8,128)} %land_ref.3, f32[135,2,128]{2,1,0:T(2,128)} %bitcast.14), custom_call_target="tpu_custom_call" | custom-call | tf_op jit(solution)/shard_map/pack/pallas_call | solution.py:214
  2.9 0.0 copy-start.6
  2.9 0.0 copy-start.3
  2.9 0.0 copy-start.4
  2.9 0.0 copy-start.5
  2.9 11.2 %all-to-all-start = ((bf16[288,2,128]{2,1,0:T(2,128)(2,1)}), bf16[288,2,128]{2,1,0:T(2,128)(2,1)S(1)}, u32[]{:S(2)}, u32[]{:S(2)}) async-start(bf16[288,2,128]{2,1,0:T(2,128)(2,1)} %bitcast.19), calls=%async_computation | async-start | bytes 294912 | tf_op jit(solution)/shard_map/all_to_all | solution.py:644
  14.1 0.0 copy-done.2
  14.1 0.0 copy-done.1
  14.1 0.0 copy-done
  14.1 0.5 %edge.1 = (f32[24,128]{1,0:T(8,128)S(1)}, f32[24,128]{1,0:T(8,128)S(1)}, f32[48,128]{1,0:T(8,128)S(1)}) custom-call(f32[2160,128]{1,0:T(8,128)S(1)} %bitcast.12, s32[135,128]{1,0:T(8,128)S(1)} %copy-done.2, f32[135,2,128]{2,1,0:T(2,128)S(1)} %bitcast.15), custom_call_target="tpu_custom_call" | custom-call | tf_op jit(solution)/shard_map/edge/pallas_call | solution.py:408
  14.6 0.7 %collective-permute-start.1 = (f32[48,128]{1,0:T(8,128)S(1)}, f32[48,128]{1,0:T(8,128)S(1)}, u32[]{:S(2)}, u32[]{:S(2)}) collective-permute-start(f32[48,128]{1,0:T(8,128)S(1)} %get-tuple-element.17), channel_id=1, source_target_pairs={{1,2},{2,1},{3,4},{4,3},{5,6},{6,5},{9,10},{10,9},{11,12},{12,11},... | collective-permute-start | bytes 73736 | tf_op jit(solution)/shard_map/ppermute | solution.py:639
  15.3 2.5 %collective-permute-start = (f32[48,128]{1,0:T(8,128)S(1)}, f32[48,128]{1,0:T(8,128)S(1)}, u32[]{:S(2)}, u32[]{:S(2)}) collective-permute-start(f32[48,128]{1,0:T(8,128)S(1)} %get-tuple-element.17), channel_id=1, source_target_pairs={{0,1},{1,0},{2,3},{3,2},{4,5},{5,4},{6,7},{7,6},{8,9},{9,8},{10,11... | collective-permute-start | bytes 73736 | tf_op jit(solution)/shard_map/ppermute | solution.py:639
  17.8 0.0 copy-done.6
  17.8 0.1 convert_multiply_fusion
  17.8 0.0 collective-permute-done.1.far_side_ref
  17.8 1.9 %collective-permute-done.near_side_ref = f32[48,128]{1,0:T(8,128)S(1)} collective-permute-done((f32[48,128]{1,0:T(8,128)S(1)}, f32[48,128]{1,0:T(8,128)S(1)}, u32[]{:S(2)}, u32[]{:S(2)}) %collective-permute-start) | collective-permute-done | bytes 24608 | tf_op jit(solution)/shard_map/ppermute | solution.py:639
  19.7 1.5 %all-to-all-done = bf16[288,2,128]{2,1,0:T(2,128)(2,1)S(1)} async-done(((bf16[288,2,128]{2,1,0:T(2,128)(2,1)}), bf16[288,2,128]{2,1,0:T(2,128)(2,1)S(1)}, u32[]{:S(2)}, u32[]{:S(2)}) %all-to-all-start) | async-done | bytes 147488 | tf_op jit(solution)/shard_map/all_to_all | solution.py:644
  21.2 0.1 broadcast_in_dim.2.refs_1_
  21.3 0.0 copy-done.3
  21.3 0.0 copy-done.4
  21.3 0.0 copy-done.5
  21.3 1.9 %filter.1 = bf16[576,128]{1,0:T(8,128)(2,1)} custom-call(bf16[576,128]{1,0:T(8,128)(2,1)S(1)} %bitcast.18, f32[16,128]{1,0:T(8,128)S(1)} %broadcast_in_dim.2.refs_1_, bf16[256,256]{1,0:T(8,128)(2,1)S(1)} %copy-done.4, bf16[256,256]{1,0:T(8,128)(2,1)S(1)} %copy-done.3, f32[32,128]{1,0:T(8,128)S(1)} %copy-done.5), custom_call_target="tpu_custom_call" | custom-call | tf_op jit(solution)/shard_map/filter/pallas_call | solution.py:362
  23.3 7.6 %all-to-all-start.1 = ((bf16[288,2,128]{2,1,0:T(2,128)(2,1)}), bf16[288,2,128]{2,1,0:T(2,128)(2,1)S(1)}, u32[]{:S(2)}, u32[]{:S(2)}) async-start(bf16[288,2,128]{2,1,0:T(2,128)(2,1)} %bitcast.6), calls=%async_computation.1 | async-start | bytes 294912 | tf_op jit(solution)/shard_map/all_to_all | solution.py:644
  30.9 0.5 %collective-permute-start.3 = (f32[24,128]{1,0:T(8,128)S(1)}, f32[24,128]{1,0:T(8,128)S(1)}, u32[]{:S(2)}, u32[]{:S(2)}) collective-permute-start(f32[24,128]{1,0:T(8,128)S(1)} %get-tuple-element.26.own_near_ref), channel_id=1, source_target_pairs={{0,8},{8,0},{16,24},{24,16},{32,40},{40,32},{48,56},{56,48},{64,72... | collective-permute-start | bytes 36872 | tf_op jit(solution)/shard_map/ppermute | solution.py:639
  31.4 1.2 %collective-permute-start.2 = (f32[24,128]{1,0:T(8,128)S(1)}, f32[24,128]{1,0:T(8,128)S(1)}, u32[]{:S(2)}, u32[]{:S(2)}) collective-permute-start(f32[24,128]{1,0:T(8,128)S(1)} %get-tuple-element.27.own_far_ref), channel_id=1, source_target_pairs={{8,16},{16,8},{24,32},{32,24},{40,48},{48,40},{56,64},{64,56},{72,... | collective-permute-start | bytes 36872 | tf_op jit(solution)/shard_map/ppermute | solution.py:639
  32.5 2.2 %stencil.1 = (f32[2160,128]{1,0:T(8,128)}, f32[1080,128]{1,0:T(8,128)S(1)}, f32[24,128]{1,0:T(8,128)S(1)}) custom-call(f32[2160,128]{1,0:T(8,128)S(1)} %bitcast.13, s32[135,128]{1,0:T(8,128)S(1)} %copy-done.2, f32[135,2,128]{2,1,0:T(2,128)S(1)} %bitcast.16, f32[48,128]{1,0:T(8,128)S(1)} %collective-permute-done.near_side_ref, ...), custom_call_target="tpu_custom_call" | custom-call | tf_op jit(solution)/shard_map/stencil/pallas_call | solution.py:487
  34.7 0.0 collective-permute-done.3.near_ref
  34.7 0.1 collective-permute-done.2.far_ref
  34.8 1.2 %all-to-all-done.1 = bf16[288,2,128]{2,1,0:T(2,128)(2,1)S(1)} async-done(((bf16[288,2,128]{2,1,0:T(2,128)(2,1)}), bf16[288,2,128]{2,1,0:T(2,128)(2,1)S(1)}, u32[]{:S(2)}, u32[]{:S(2)}) %all-to-all-start.1) | async-done | bytes 147488 | tf_op jit(solution)/shard_map/all_to_all | solution.py:644
  36.1 1.3 %remove.1 = f32[2160,128]{1,0:T(8,128)} custom-call(bf16[576,128]{1,0:T(8,128)(2,1)S(1)} %bitcast.17, f32[1080,128]{1,0:T(8,128)S(1)} %get-tuple-element.24.flow_ref, f32[24,128]{1,0:T(8,128)S(1)} %get-tuple-element.25.rim_ref, f32[24,128]{1,0:T(8,128)S(1)} %get-tuple-element.26.own_near_ref, ...), custom_call_target="tpu_custom_call", output_to_operand_aliasing={{}: (7, {})} | custom-call | tf_op jit(solution)/shard_map/remove/pallas_call | solution.py:612
  (1 shorter events, 0.0 us)
Async XLA Ops:
  0.0 14.1 %copy-start.2 = (s32[135,128]{1,0:T(8,128)S(1)}, s32[135,128]{1,0:T(8,128)}, u32[]{:S(2)}) copy-start(s32[135,128]{1,0:T(8,128)} %land_ref.3) | copy-start | bytes 207364
  0.0 14.1 %copy-start.1 = (f32[2,135,128]{2,0,1:T(2,128)S(1)}, f32[2,135,128]{2,0,1:T(2,128)}, u32[]{:S(2)}) copy-start(f32[2,135,128]{2,0,1:T(2,128)} %param.9) | copy-start | bytes 414724
  0.0 14.1 %copy-start = (f32[4,4,135,128]{3,1,2,0:T(4,128)S(1)}, f32[4,4,135,128]{3,1,2,0:T(4,128)}, u32[]{:S(2)}) copy-start(f32[4,4,135,128]{3,1,2,0:T(4,128)} %param.7) | copy-start | bytes 3317764
  2.9 14.9 %copy-start.6 = (s32[128]{0:T(128)S(1)}, s32[128]{0:T(128)}, u32[]{:S(2)}) copy-start(s32[128]{0:T(128)} %param.10) | copy-start | bytes 1540
  2.9 18.4 %copy-start.3 = (bf16[256,256]{1,0:T(8,128)(2,1)S(1)}, bf16[256,256]{1,0:T(8,128)(2,1)}, u32[]{:S(2)}) copy-start(bf16[256,256]{1,0:T(8,128)(2,1)} %constant.38.clone.refs_3_) | copy-start | bytes 393220
  2.9 18.4 %copy-start.4 = (bf16[256,256]{1,0:T(8,128)(2,1)S(1)}, bf16[256,256]{1,0:T(8,128)(2,1)}, u32[]{:S(2)}) copy-start(bf16[256,256]{1,0:T(8,128)(2,1)} %constant.37.clone.refs_2_) | copy-start | bytes 393220
  2.9 18.4 %copy-start.5 = (f32[32,128]{1,0:T(8,128)S(1)}, f32[32,128]{1,0:T(8,128)}, u32[]{:S(2)}) copy-start(f32[32,128]{1,0:T(8,128)} %constant.39.clone.refs_4_) | copy-start | bytes 49156
  2.9 18.3 %all-to-all-start = ((bf16[288,2,128]{2,1,0:T(2,128)(2,1)}), bf16[288,2,128]{2,1,0:T(2,128)(2,1)S(1)}, u32[]{:S(2)}, u32[]{:S(2)}) async-start(bf16[288,2,128]{2,1,0:T(2,128)(2,1)} %bitcast.19), calls=%async_computation | async-start | bytes 294912 | tf_op jit(solution)/shard_map/all_to_all | solution.py:644
  14.6 3.2 %collective-permute-start.1 = (f32[48,128]{1,0:T(8,128)S(1)}, f32[48,128]{1,0:T(8,128)S(1)}, u32[]{:S(2)}, u32[]{:S(2)}) collective-permute-start(f32[48,128]{1,0:T(8,128)S(1)} %get-tuple-element.17), channel_id=1, source_target_pairs={{1,2},{2,1},{3,4},{4,3},{5,6},{6,5},{9,10},{10,9},{11,12},{12,11},... | collective-permute-start | bytes 73736 | tf_op jit(solution)/shard_map/ppermute | solution.py:639
  15.3 4.4 %collective-permute-start = (f32[48,128]{1,0:T(8,128)S(1)}, f32[48,128]{1,0:T(8,128)S(1)}, u32[]{:S(2)}, u32[]{:S(2)}) collective-permute-start(f32[48,128]{1,0:T(8,128)S(1)} %get-tuple-element.17), channel_id=1, source_target_pairs={{0,1},{1,0},{2,3},{3,2},{4,5},{5,4},{6,7},{7,6},{8,9},{9,8},{10,11... | collective-permute-start | bytes 73736 | tf_op jit(solution)/shard_map/ppermute | solution.py:639
  23.3 12.8 %all-to-all-start.1 = ((bf16[288,2,128]{2,1,0:T(2,128)(2,1)}), bf16[288,2,128]{2,1,0:T(2,128)(2,1)S(1)}, u32[]{:S(2)}, u32[]{:S(2)}) async-start(bf16[288,2,128]{2,1,0:T(2,128)(2,1)} %bitcast.6), calls=%async_computation.1 | async-start | bytes 294912 | tf_op jit(solution)/shard_map/all_to_all | solution.py:644
  30.9 3.8 %collective-permute-start.3 = (f32[24,128]{1,0:T(8,128)S(1)}, f32[24,128]{1,0:T(8,128)S(1)}, u32[]{:S(2)}, u32[]{:S(2)}) collective-permute-start(f32[24,128]{1,0:T(8,128)S(1)} %get-tuple-element.26.own_near_ref), channel_id=1, source_target_pairs={{0,8},{8,0},{16,24},{24,16},{32,40},{40,32},{48,56},{56,48},{64,72... | collective-permute-start | bytes 36872 | tf_op jit(solution)/shard_map/ppermute | solution.py:639
  31.4 3.5 %collective-permute-start.2 = (f32[24,128]{1,0:T(8,128)S(1)}, f32[24,128]{1,0:T(8,128)S(1)}, u32[]{:S(2)}, u32[]{:S(2)}) collective-permute-start(f32[24,128]{1,0:T(8,128)S(1)} %get-tuple-element.27.own_far_ref), channel_id=1, source_target_pairs={{8,16},{16,8},{24,32},{32,24},{40,48},{48,40},{56,64},{64,56},{72,... | collective-permute-start | bytes 36872 | tf_op jit(solution)/shard_map/ppermute | solution.py:639
